TPU v7x, 32 devices: a whole 2x2x4 slice. The times are simulated.
32 devices in a mesh: seq: 8 (over z, core), tok: 4 (over y, x).
Axes of the slice: x: 2, y: 2, z: 4, core: 2. Of those that a mesh axis runs over, the one named last changes fastest.
Arguments:
- x_in: bfloat16 [2, 16, 1024, 768], P(None, 'seq', 'tok'), may hold values from -6 to 6
- cotangent: bfloat16 [2, 16, 1024, 768], P(None, 'seq', 'tok'), may hold values from -6 to 6
- counts: int32 [2, 8], P(None, 'seq'), may hold values from 1 to 2, as said below
- ln1_gain: bfloat16 [2, 768], replicated, may hold values from 0.5 to 1.5
- ln1_bias: bfloat16 [2, 768], replicated, may hold values from -3 to 3
- w_in: bfloat16 [2, 768, 2304], replicated, may hold values from -0.21875 to 0.21875
- short_w: bfloat16 [2, 3, 2304], replicated, may hold values from -5 to 5
- filt_w1: bfloat16 [2, 33, 64], replicated, may hold values from -1 to 1
- filt_freq: bfloat16 [2, 2, 64], replicated, may hold values from 0.5 to 4
- filt_w2: bfloat16 [2, 64, 64], replicated, may hold values from -0.75 to 0.75
- filt_w3: bfloat16 [2, 64, 768], replicated, may hold values from -0.09375 to 0.09375
- long_bias: bfloat16 [2, 768], replicated, may hold values from -5 to 5
- w_out: bfloat16 [2, 768, 768], replicated, may hold values from -0.21875 to 0.21875
- ln2_gain: bfloat16 [2, 768], replicated, may hold values from 0.5 to 1.5
- ln2_bias: bfloat16 [2, 768], replicated, may hold values from -3 to 3
- w_up: bfloat16 [2, 768, 3072], replicated, may hold values from -0.21875 to 0.21875
- w_down: bfloat16 [2, 3072, 768], replicated, may hold values from -0.109375 to 0.109375
Outputs:
- out_act: float32 [2, 16, 1024, 768], P(None, 'seq', 'tok')
- grad_in: float32 [2, 16, 1024, 768], P(None, 'seq', 'tok')
- grad_ln1_gain: float32 [2, 768], replicated
- grad_ln1_bias: float32 [2, 768], replicated
- grad_w_in: float32 [2, 768, 2304], P(None, 'seq', 'tok')
- grad_short_w: float32 [2, 3, 2304], replicated
- grad_filt_w1: float32 [2, 33, 64], replicated
- grad_filt_freq: float32 [2, 2, 64], replicated
- grad_filt_w2: float32 [2, 64, 64], replicated
- grad_filt_w3: float32 [2, 64, 768], replicated
- grad_long_bias: float32 [2, 768], replicated
- grad_w_out: float32 [2, 768, 768], P(None, 'seq', 'tok')
- grad_ln2_gain: float32 [2, 768], replicated
- grad_ln2_bias: float32 [2, 768], replicated
- grad_w_up: float32 [2, 768, 3072], P(None, 'seq', 'tok')
- grad_w_down: float32 [2, 3072, 768], P(None, 'tok', 'seq')
Inputs may be any that keep to these rules, and one draw needn't show every extreme that they name: Live sequences of group g in micro-batch m are its slots 0 to counts[m, g] - 1 of 2; in every micro-batch one group has all 2 slots live and another group has one.
All inputs are finite; a program needn't handle non-finite values.
Results may differ from a plain program's by a relative error of at most 0.019.
Values may be sent and summed in bfloat16 or wider, within the bound.
A program may use at most 512 MiB of HBM per device.

v0:
```python
import math

import jax
import jax.numpy as jnp
from jax import lax
from jax.sharding import PartitionSpec as P

EMB = 33
INNER = 64


HIGHEST = lax.Precision.HIGHEST
NORM_EPS = 1e-05
MOD_SHIFT = 0.05


def passed_along(block, axis, distance):
    devices = range(lax.axis_size(axis))
    route = [(i - distance, i) for i in devices if i - distance in devices]
    return lax.ppermute(block, axis, route)


def for_sending(value):

    def short(part):
        return part.astype(jnp.bfloat16) if part.dtype == jnp.float32 else part

    return jax.tree.map(short, value)


def position_features(length):
    band_count = (EMB - 1) // 2
    step_index = jnp.arange(length, dtype=jnp.int32).astype(jnp.float32)
    time_grid = step_index / (length - 1)
    base_angle = step_index * (2.0 * math.pi / length)
    band_freq = jnp.linspace(0.0001, band_count - 1, band_count, dtype=jnp.float32)
    phases = base_angle[:, None] * band_freq[None, :]
    return jnp.concatenate([time_grid[:, None], jnp.cos(phases), -jnp.sin(phases)], axis=1)


def decay_table(time_grid, first_chan, channels, model_width):
    fast_rate = math.log(0.01) / 0.3
    slow_rate = math.log(0.01) / 1.5
    chan_index = first_chan + jnp.arange(channels, dtype=jnp.int32).astype(jnp.float32)
    deltas = jnp.abs(fast_rate + (slow_rate - fast_rate) * chan_index / (model_width - 1))
    return jnp.exp(-time_grid * deltas[None, :]) + MOD_SHIFT


def filter_taps(features, weight_one, sine_freq, weight_two, weight_three, envelope):
    first_sine = jnp.sin(sine_freq[0] * jnp.dot(features, weight_one, precision=HIGHEST))
    second_sine = jnp.sin(sine_freq[1] * jnp.dot(first_sine, weight_two, precision=HIGHEST))
    return jnp.dot(second_sine, weight_three, precision=HIGHEST) * envelope


def layer_norm(values_in, gain_vec, bias_vec):
    mean_row = jnp.mean(values_in, axis=-1, keepdims=True)
    centred = values_in - mean_row
    variance = jnp.mean(centred * centred, axis=-1, keepdims=True)
    return centred * lax.rsqrt(variance + NORM_EPS) * gain_vec + bias_vec


def gelu_tanh(values_in):
    return jax.nn.gelu(values_in, approximate=True)


def dft_tables(outer_size, inner_size):
    padded_len = outer_size * inner_size
    outer_index = jnp.arange(outer_size, dtype=jnp.int32)
    half_index = jnp.arange(outer_size // 2, dtype=jnp.int32)
    inner_index = jnp.arange(inner_size, dtype=jnp.int32)
    angle_outer = (outer_index[:, None] * half_index[None, :] % outer_size).astype(jnp.float32) * (
        2.0 * math.pi / outer_size
    )
    angle_twist = (outer_index[:, None] * inner_index[None, :] % padded_len).astype(jnp.float32) * (
        2.0 * math.pi / padded_len
    )
    angle_inner = (inner_index[:, None] * inner_index[None, :] % inner_size).astype(jnp.float32) * (
        2.0 * math.pi / inner_size
    )
    return (
        jnp.cos(angle_outer),
        jnp.sin(angle_outer),
        jnp.cos(angle_twist)[None, :, :, None],
        jnp.sin(angle_twist)[None, :, :, None],
        jnp.cos(angle_inner),
        jnp.sin(angle_inner),
    )


def forward_dft(series, tables):
    cos_outer, sin_outer, cos_twist, sin_twist, cos_inner, sin_inner = tables
    outer_size = cos_outer.shape[0]
    inner_size = cos_inner.shape[0]
    seq_count = series.shape[0]
    channels = series.shape[2]
    token_grid = series.reshape(seq_count, outer_size // 2, inner_size, channels)
    first_re = jnp.einsum("ka,sabc->skbc", cos_outer, token_grid, precision=HIGHEST)
    first_im = -jnp.einsum("ka,sabc->skbc", sin_outer, token_grid, precision=HIGHEST)
    twist_re = first_re * cos_twist + first_im * sin_twist
    twist_im = first_im * cos_twist - first_re * sin_twist
    out_re = jnp.einsum("skbc,bj->skjc", twist_re, cos_inner, precision=HIGHEST) + jnp.einsum(
        "skbc,bj->skjc", twist_im, sin_inner, precision=HIGHEST
    )
    out_im = jnp.einsum("skbc,bj->skjc", twist_im, cos_inner, precision=HIGHEST) - jnp.einsum(
        "skbc,bj->skjc", twist_re, sin_inner, precision=HIGHEST
    )
    return (out_re, out_im)


def inverse_dft(spec_re, spec_im, tables):
    cos_outer, sin_outer, cos_twist, sin_twist, cos_inner, sin_inner = tables
    outer_size = cos_outer.shape[0]
    inner_size = cos_inner.shape[0]
    seq_count = spec_re.shape[0]
    channels = spec_re.shape[3]
    back_re = jnp.einsum("skjc,bj->skbc", spec_re, cos_inner, precision=HIGHEST) - jnp.einsum(
        "skjc,bj->skbc", spec_im, sin_inner, precision=HIGHEST
    )
    back_im = jnp.einsum("skjc,bj->skbc", spec_im, cos_inner, precision=HIGHEST) + jnp.einsum(
        "skjc,bj->skbc", spec_re, sin_inner, precision=HIGHEST
    )
    turn_re = back_re * cos_twist - back_im * sin_twist
    turn_im = back_im * cos_twist + back_re * sin_twist
    token_grid = (
        jnp.einsum("skbc,ka->sabc", turn_re, cos_outer, precision=HIGHEST)
        - jnp.einsum("skbc,ka->sabc", turn_im, sin_outer, precision=HIGHEST)
    ) / (outer_size * inner_size)
    return token_grid.reshape(seq_count, outer_size // 2 * inner_size, channels)


def complex_product(left_re, left_im, right_re, right_im):
    return (left_re * right_re - left_im * right_im, left_re * right_im + left_im * right_re)


def add_tree(running, update):
    if running is None:
        return update
    return jax.tree.map(jnp.add, running, update)


def shards(
    x_in,
    cotangent,
    counts,
    ln1_gain,
    ln1_bias,
    w_in,
    short_w,
    filt_w1,
    filt_freq,
    filt_w2,
    filt_w3,
    long_bias,
    w_out,
    ln2_gain,
    ln2_bias,
    w_up,
    w_down,
):
    tok_count = lax.axis_size("tok")
    micro_count, cap_size, tok_rows, model_width = x_in.shape
    channels = model_width // tok_count
    first_chan = lax.axis_index("tok") * channels
    layer_count = w_in.shape[0]
    length = tok_rows * tok_count
    tables = dft_tables(2 * length // INNER, INNER)
    features = position_features(length)
    envelope = decay_table(features[:, :1], first_chan.astype(jnp.float32), channels, model_width)
    gain_one = ln1_gain.astype(jnp.float32)
    bias_one = ln1_bias.astype(jnp.float32)
    gain_two = ln2_gain.astype(jnp.float32)
    bias_two = ln2_bias.astype(jnp.float32)
    short_taps = short_w.astype(jnp.float32)
    skip_scale = long_bias.astype(jnp.float32)
    filt_one = filt_w1.astype(jnp.float32)
    filt_sine = filt_freq.astype(jnp.float32)
    filt_two = filt_w2.astype(jnp.float32)
    filt_three = filt_w3.astype(jnp.float32)

    def taps_of(layer_index):

        def taps_fn(weight_one, sine_freq, weight_two, three_slice):
            return filter_taps(features, weight_one, sine_freq, weight_two, three_slice, envelope)

        three_slice = lax.dynamic_slice_in_dim(filt_three[layer_index], first_chan, channels, 1)
        return jax.vjp(
            taps_fn,
            filt_one[layer_index],
            filt_sine[layer_index],
            filt_two[layer_index],
            three_slice,
        )

    taps_spectra = []
    for layer_index in range(layer_count):
        filter_rows, _ = taps_of(layer_index)
        taps_spectra.append(forward_dft(filter_rows[None], tables))

    def backward_layer(grad_rows, kept, layer_index):
        (
            residual,
            normed,
            padded,
            short_out,
            carried,
            long_out,
            gated_rows,
            hidden,
            normed_two,
            raised,
            active,
            kept_signal,
        ) = kept
        down_grad = grad_rows.astype(jnp.bfloat16)
        active_grad = jnp.einsum(
            "std,fd->stf", down_grad, w_down[layer_index], preferred_element_type=jnp.float32
        )
        _, gelu_pull = jax.vjp(gelu_tanh, raised)
        raised_grad = gelu_pull(active_grad)[0].astype(jnp.bfloat16)
        normed_two_grad = jnp.einsum(
            "stf,df->std", raised_grad, w_up[layer_index], preferred_element_type=jnp.float32
        )
        _, second_pull = jax.vjp(layer_norm, hidden, gain_two[layer_index], bias_two[layer_index])
        hidden_part, grad_gain_two, grad_bias_two = second_pull(normed_two_grad)
        hidden_grad = grad_rows + hidden_part
        out_grad = hidden_grad.astype(jnp.bfloat16)
        gated_grad = jnp.einsum(
            "ste,de->std", out_grad, w_out[layer_index], preferred_element_type=jnp.float32
        )
        gate_out = short_out[:, :, :model_width]
        gate_in = short_out[:, :, model_width : 2 * model_width]
        values = short_out[:, :, 2 * model_width :]
        long_grad = gated_grad * gate_out
        gate_out_grad = gated_grad * long_out
        grad_skip = jnp.sum(carried * long_grad, axis=(0, 1))
        spec_re, spec_im = taps_spectra[layer_index]
        upstream_re, upstream_im = forward_dft(
            lax.all_to_all(
                long_grad.astype(jnp.bfloat16), "tok", split_axis=2, concat_axis=1, tiled=True
            ).astype(long_grad.dtype),
            tables,
        )
        back_re, back_im = complex_product(upstream_re, upstream_im, spec_re, -spec_im)
        back_rows = lax.all_to_all(
            for_sending(inverse_dft(back_re, back_im, tables)),
            "tok",
            split_axis=1,
            concat_axis=2,
            tiled=True,
        )
        back_rows, upstream_re, upstream_im = (back_rows, upstream_re, upstream_im)
        signal_re, signal_im = kept_signal
        cross_re = jnp.sum(signal_re * upstream_re + signal_im * upstream_im, axis=0)
        cross_im = jnp.sum(signal_re * upstream_im - signal_im * upstream_re, axis=0)
        carried_grad = back_rows + skip_scale[layer_index] * long_grad
        short_grad = jnp.concatenate(
            [gate_out_grad, carried_grad * values, carried_grad * gate_in], axis=2
        )
        next_rows = passed_along(for_sending(short_grad[:, :2, :]), "tok", -1)
        extended = jnp.concatenate([short_grad, next_rows], axis=1)
        kernel = short_taps[layer_index]
        projected_grad = (
            kernel[2] * short_grad + kernel[1] * extended[:, 1:-1] + kernel[0] * extended[:, 2:]
        ).astype(jnp.bfloat16)
        grad_short = jnp.stack(
            [
                jnp.sum(short_grad * padded[:, tap_index : tap_index + tok_rows], axis=(0, 1))
                for tap_index in range(3)
            ]
        )
        normed_grad = jnp.einsum(
            "ste,de->std", projected_grad, w_in[layer_index], preferred_element_type=jnp.float32
        )
        _, first_pull = jax.vjp(layer_norm, residual, gain_one[layer_index], bias_one[layer_index])
        residual_part, grad_gain_one, grad_bias_one = first_pull(normed_grad)
        left_all = (
            lax.all_gather(down_grad, "tok", axis=1, tiled=True),
            lax.all_gather(gated_rows, "tok", axis=1, tiled=True),
            lax.all_gather(normed_two, "tok", axis=1, tiled=True),
            lax.all_gather(normed, "tok", axis=1, tiled=True),
        )
        right_cols = (
            lax.all_to_all(active, "tok", split_axis=2, concat_axis=1, tiled=True),
            lax.all_to_all(out_grad, "tok", split_axis=2, concat_axis=1, tiled=True),
            lax.all_to_all(raised_grad, "tok", split_axis=2, concat_axis=1, tiled=True),
            lax.all_to_all(projected_grad, "tok", split_axis=2, concat_axis=1, tiled=True),
        )
        grad_down = jnp.einsum(
            "stf,std->fd", right_cols[0], left_all[0], preferred_element_type=jnp.float32
        )
        grad_out = jnp.einsum(
            "std,ste->de", left_all[1], right_cols[1], preferred_element_type=jnp.float32
        )
        grad_up = jnp.einsum(
            "std,stf->df", left_all[2], right_cols[2], preferred_element_type=jnp.float32
        )
        grad_in_proj = jnp.einsum(
            "std,ste->de", left_all[3], right_cols[3], preferred_element_type=jnp.float32
        )
        bundle = (
            (grad_in_proj, grad_out, grad_up, grad_down),
            (grad_gain_one, grad_bias_one, grad_short, grad_skip, grad_gain_two, grad_bias_two),
            (cross_re, cross_im),
        )
        return (hidden_grad + residual_part, bundle)

    def filter_grads(cross_re, cross_im, layer_index):
        taps_grad = inverse_dft(cross_re[None], cross_im[None], tables)[0]
        _, taps_pull = taps_of(layer_index)
        grad_one, grad_sine, grad_two, grad_three = taps_pull(taps_grad)
        grad_three_full = lax.dynamic_update_slice_in_dim(
            jnp.zeros_like(filt_three[layer_index]), grad_three, first_chan, 1
        )
        return (grad_one, grad_sine, grad_two, grad_three_full)

    outputs = []
    input_grads = []
    running = None
    reduced = None
    for micro_index in range(micro_count):
        live_mask = (jnp.arange(cap_size, dtype=jnp.int32) < counts[micro_index, 0]).astype(
            jnp.float32
        )[:, None, None]
        residual = x_in[micro_index].astype(jnp.float32)
        saved = []
        for layer_index in range(layer_count):
            forward_normed = layer_norm(
                residual, gain_one[layer_index], bias_one[layer_index]
            ).astype(jnp.bfloat16)
            projected = jnp.einsum(
                "std,de->ste", forward_normed, w_in[layer_index], preferred_element_type=jnp.float32
            )
            prev_rows = passed_along(projected[:, -2:, :], "tok", 1)
            forward_padded = jnp.concatenate([prev_rows, projected], axis=1)
            forward_kernel = short_taps[layer_index]
            forward_short_out = (
                forward_kernel[0] * forward_padded[:, :-2]
                + forward_kernel[1] * forward_padded[:, 1:-1]
                + forward_kernel[2] * forward_padded[:, 2:]
            )
            forward_gate_out = forward_short_out[:, :, :model_width]
            forward_gate_in = forward_short_out[:, :, model_width : 2 * model_width]
            forward_values = forward_short_out[:, :, 2 * model_width :]
            forward_carried = forward_values * forward_gate_in
            forward_spec_re, forward_spec_im = taps_spectra[layer_index]
            convolve_signal_re, convolve_signal_im = forward_dft(
                lax.all_to_all(forward_carried, "tok", split_axis=2, concat_axis=1, tiled=True),
                tables,
            )
            prod_re, prod_im = complex_product(
                convolve_signal_re, convolve_signal_im, forward_spec_re, forward_spec_im
            )
            convolve_back_rows = lax.all_to_all(
                inverse_dft(prod_re, prod_im, tables),
                "tok",
                split_axis=1,
                concat_axis=2,
                tiled=True,
            )
            results = (convolve_back_rows, convolve_signal_re, convolve_signal_im)
            forward_long_out = results[0] + skip_scale[layer_index] * forward_carried
            forward_gated_rows = (forward_long_out * forward_gate_out).astype(jnp.bfloat16)
            forward_hidden = residual + jnp.einsum(
                "std,de->ste",
                forward_gated_rows,
                w_out[layer_index],
                preferred_element_type=jnp.float32,
            )
            forward_normed_two = layer_norm(
                forward_hidden, gain_two[layer_index], bias_two[layer_index]
            ).astype(jnp.bfloat16)
            forward_raised = jnp.einsum(
                "std,df->stf",
                forward_normed_two,
                w_up[layer_index],
                preferred_element_type=jnp.float32,
            )
            forward_active = gelu_tanh(forward_raised).astype(jnp.bfloat16)
            result = forward_hidden + jnp.einsum(
                "stf,fd->std",
                forward_active,
                w_down[layer_index],
                preferred_element_type=jnp.float32,
            )
            forward_kept = (
                residual,
                forward_normed,
                forward_padded,
                forward_short_out,
                forward_carried,
                forward_long_out,
                forward_gated_rows,
                forward_hidden,
                forward_normed_two,
                forward_raised,
                forward_active,
                results[1:],
            )
            residual = result
            kept = forward_kept
            saved.append(kept)
        outputs.append(residual * live_mask)
        grad_rows = cotangent[micro_index].astype(jnp.float32) * live_mask
        layer_bundles = [None] * layer_count
        for layer_index in reversed(range(layer_count)):
            grad_rows, bundle = backward_layer(grad_rows, saved[layer_index], layer_index)
            layer_bundles[layer_index] = bundle
        input_grads.append(grad_rows)
        running = add_tree(running, layer_bundles)
    mats = [
        jnp.stack([running[layer_index][0][member] for layer_index in range(layer_count)])
        for member in range(4)
    ]
    vecs = [
        jnp.stack([running[layer_index][1][member] for layer_index in range(layer_count)])
        for member in range(6)
    ]
    filter_parts = [
        filter_grads(running[layer_index][2][0], running[layer_index][2][1], layer_index)
        for layer_index in range(layer_count)
    ]
    filt_parts = [
        jnp.stack([filter_parts[layer_index][member] for layer_index in range(layer_count)])
        for member in range(4)
    ]
    mat_done = (
        lax.psum_scatter(
            mats[0].astype(jnp.bfloat16), "seq", scatter_dimension=1, tiled=True
        ).astype(jnp.float32),
        lax.psum_scatter(
            mats[1].astype(jnp.bfloat16), "seq", scatter_dimension=1, tiled=True
        ).astype(jnp.float32),
        lax.psum_scatter(
            mats[2].astype(jnp.bfloat16), "seq", scatter_dimension=1, tiled=True
        ).astype(jnp.float32),
        lax.psum_scatter(
            mats[3].astype(jnp.bfloat16), "seq", scatter_dimension=2, tiled=True
        ).astype(jnp.float32),
    )
    small_done = lax.psum(
        (
            vecs[0],
            vecs[1],
            vecs[2],
            vecs[3],
            vecs[4],
            vecs[5],
            filt_parts[0],
            filt_parts[1],
            filt_parts[2],
            filt_parts[3],
        ),
        ("seq", "tok"),
    )
    reduced = (tuple(mat_done), tuple(small_done))
    mat_done, small_done = reduced
    return (
        jnp.stack(outputs),
        jnp.stack(input_grads),
        small_done[0],
        small_done[1],
        mat_done[0],
        small_done[2],
        small_done[6],
        small_done[7],
        small_done[8],
        small_done[9],
        small_done[3],
        mat_done[1],
        small_done[4],
        small_done[5],
        mat_done[2],
        mat_done[3],
    )


def solution(mesh):
    return jax.shard_map(
        shards,
        mesh=mesh,
        in_specs=(
            P(None, "seq", "tok", None),
            P(None, "seq", "tok", None),
            P(None, "seq"),
            P(),
            P(),
            P(),
            P(),
            P(),
            P(),
            P(),
            P(),
            P(),
            P(),
            P(),
            P(),
            P(),
            P(),
        ),
        out_specs=(
            P(None, "seq", "tok", None),
            P(None, "seq", "tok", None),
            P(),
            P(),
            P(None, "seq", "tok"),
            P(),
            P(),
            P(),
            P(),
            P(),
            P(),
            P(None, "seq", "tok"),
            P(),
            P(),
            P(None, "seq", "tok"),
            P(None, "tok", "seq"),
        ),
        check_vma=False,
    )
```

profile of v0, /device:TPU:0, one launch (start us, length us, event | category | flops | bytes accessed | tf_op | source)
XLA Modules:
  0.0 2364.7 jit_solution(4952225727151383812)
XLA Ops:
  155.8 13.6 fusion.163
  169.4 13.9 multiply_bitcast_fusion.3
  193.4 23.1 all-to-all-done.1
  234.8 9.1 multiply_convert_fusion.3
  327.9 11.3 fusion.160
  383.6 13.8 fusion.143
  397.4 13.6 multiply_bitcast_fusion.1
  413.9 28.1 %all_to_all.516 = f32[2,1024,192]{2,0,1:T(2,128)S(1)} all-to-all(f32[2,1024,192]{2,0,1:T(2,128)S(1)} %copy.763), channel_id=1, replica_groups=mesh['seq'=8,'tok'=4] {'tok'}, dimensions={1} | all-to-all | bytes 3145728 | tf_op jit(solution)/shard_map/all_to_all | solution.py:353
  468.0 9.4 fusion.220
  518.2 9.0 multiply_convert_fusion.1
  561.9 20.9 fusion.153
  582.8 13.9 multiply_bitcast_fusion.2
  667.6 13.5 fusion.133
  681.2 13.7 multiply_bitcast_fusion
  713.9 12.0 all-to-all-done.7
  814.5 14.9 all-to-all-done.12
  857.0 16.4 fusion.99
  894.2 13.8 fusion.91
  908.0 11.7 fusion.516
  992.9 9.6 multiply_reduce_fusion.2
  1011.5 9.1 fusion.20
  1063.6 9.3 fusion.88
  1092.8 18.5 fusion.85
  1111.4 9.1 fusion.769
  1147.5 16.9 fusion.127
  1186.4 12.9 fusion.119
  1199.4 11.5 fusion.510
  1217.1 10.1 fusion.767
  1251.5 9.5 multiply_reduce_fusion.5
  1270.0 8.9 fusion.6
  1301.5 21.1 fusion.77
  1327.3 20.9 fusion.519
  1376.4 10.8 fusion.188
  1387.1 17.4 fusion.113
  1427.7 10.0 fusion.775
  1442.0 10.0 fusion.711
  1456.4 20.3 fusion.105
  1482.2 20.3 fusion.513
  1526.2 8.8 copy.925
  1590.3 10.1 multiply_reduce_fusion.8
  1608.2 23.8 %all-to-all-done.30 = bf16[2,256,3072]{1,0,2:T(2,128)(2,1)} async-done(((bf16[2,256,3072]{1,0,2:T(2,128)(2,1)}), bf16[2,256,3072]{1,0,2:T(2,128)(2,1)}, u32[]{:S(2)}, u32[]{:S(2)}) %all-to-all-start.30) | async-done | bytes 3145760 | tf_op jit(solution)/shard_map/all_to_all | solution.py:283
  1636.9 13.0 multiply_reduce_fusion.11
  1657.0 15.5 all-to-all-done.27
  1719.5 9.3 copy.919
  1748.8 9.4 fusion.336
  1884.3 16.3 all-to-all-done.25
  2125.7 91.5 %all-reduce.16.cloned.1.call-done = (bf16[2,768,576]{2,0,1:T(2,128)(2,1)}, bf16[2,768,768]{1,0,2:T(2,128)(2,1)}) async-done(((bf16[2,768,576]{2,0,1:T(2,128)(2,1)}, bf16[2,768,768]{1,0,2:T(2,128)(2,1)}), (bf16[2,768,576]{2,0,1:T(2,128)(2,1)}, bf16[2,768,768]{1,0,2:T(2,128)(2,1)})) %all-reduce.16.cloned.1.call-update) | async-done | bytes 4128784
  2221.2 129.2 %all-reduce.12.cloned.1.call-done = f32[2,64,768]{2,1,0:T(8,128)} async-done(((f32[2,64,768]{2,1,0:T(8,128)}), f32[2,64,768]{2,1,0:T(8,128)}) %all-reduce.12.cloned.1.call-update) | async-done | bytes 393232 | tf_op jit(solution)/shard_map/psum | solution.py:440
  (1368 shorter events, 1483.4 us)
Async XLA Ops:
  17.9 40.5 %collective-permute-start = (f32[2,2,2304]{2,1,0:T(2,128)S(1)}, f32[2,2,2304]{2,1,0:T(2,128)S(1)}, u32[]{:S(2)}, u32[]{:S(2)}) collective-permute-start(f32[2,2,2304]{2,1,0:T(2,128)S(1)} %slice.437), channel_id=1, source_target_pairs={{0,1},{1,2},{2,3},{4,5},{5,6},{6,7},{8,9},{9,10},{10,11},{12,13},{... | collective-permute-start | bytes 110600 | tf_op jit(solution)/shard_map/ppermute | solution.py:20
  27.3 31.2 %collective-permute-start.2 = (f32[2,2,2304]{2,1,0:T(2,128)S(1)}, f32[2,2,2304]{2,1,0:T(2,128)S(1)}, u32[]{:S(2)}, u32[]{:S(2)}) collective-permute-start(f32[2,2,2304]{2,1,0:T(2,128)S(1)} %slice.466), channel_id=1, source_target_pairs={{0,1},{1,2},{2,3},{4,5},{5,6},{6,7},{8,9},{9,10},{10,11},{12,13},{... | collective-permute-start | bytes 110600 | tf_op jit(solution)/shard_map/ppermute | solution.py:20
  70.4 23.4 all-to-all-start
  187.4 29.0 %all-to-all-start.1 = ((f32[2,1024,192]{2,0,1:T(2,128)}), f32[2,1024,192]{2,0,1:T(2,128)}, u32[]{:S(2)}, u32[]{:S(2)}) async-start(f32[2,1024,192]{2,0,1:T(2,128)} %copy.707), calls=%async_computation.1 | async-start | bytes 4194304 | tf_op jit(solution)/shard_map/all_to_all | solution.py:353
  290.2 24.1 %all-to-all-start.2 = ((f32[2,256,768]{1,0,2:T(2,128)}), f32[2,256,768]{1,0,2:T(2,128)}, u32[]{:S(2)}, u32[]{:S(2)}) async-start(f32[2,256,768]{1,0,2:T(2,128)} %copy.711), calls=%async_computation.2 | async-start | bytes 3145728 | tf_op jit(solution)/shard_map/all_to_all | solution.py:347
  294.6 1470.3 %all-gather.27.cloned.1.call-start = ((), (), s32[]{:S(2)}) async-start(), calls=%async_computation.40 | async-start | bytes 3932160 | tf_op jit(solution)/shard_map/all_gather | solution.py:278
  452.4 1463.4 %all-gather.25.cloned.1.call-start = ((), (), s32[]{:S(2)}) async-start(), calls=%async_computation.39 | async-start | bytes 3932160 | tf_op jit(solution)/shard_map/all_gather | solution.py:278
  453.1 1500.4 %all-gather.21.cloned.1.call-start = ((), (), s32[]{:S(2)}) async-start(), calls=%async_computation.36 | async-start | bytes 3932160 | tf_op jit(solution)/shard_map/all_gather | solution.py:280
  557.5 43.4 %all-to-all-start.6 = ((f32[2,256,768]{1,0,2:T(2,128)}), f32[2,256,768]{1,0,2:T(2,128)}, u32[]{:S(2)}, u32[]{:S(2)}) async-start(f32[2,256,768]{1,0,2:T(2,128)} %copy.767), calls=%async_computation.6 | async-start | bytes 3145728 | tf_op jit(solution)/shard_map/all_to_all | solution.py:347
  600.9 98.1 %all-to-all-start.3 = ((f32[2,1024,192]{2,0,1:T(2,128)}), f32[2,1024,192]{2,0,1:T(2,128)}, u32[]{:S(2)}, u32[]{:S(2)}) async-start(f32[2,1024,192]{2,0,1:T(2,128)} %copy.741), calls=%async_computation.3 | async-start | bytes 4194304 | tf_op jit(solution)/shard_map/all_to_all | solution.py:353
  699.0 26.9 %all-to-all-start.7 = ((f32[2,1024,192]{2,0,1:T(2,128)}), f32[2,1024,192]{2,0,1:T(2,128)}, u32[]{:S(2)}, u32[]{:S(2)}) async-start(f32[2,1024,192]{2,0,1:T(2,128)} %copy.785), calls=%async_computation.7 | async-start | bytes 4194304 | tf_op jit(solution)/shard_map/all_to_all | solution.py:353
  703.5 1255.9 %all-gather.31.cloned.1.call-start = ((), (), s32[]{:S(2)}) async-start(), calls=%async_computation.42 | async-start | bytes 3932160 | tf_op jit(solution)/shard_map/all_gather | solution.py:278
  742.6 1220.5 %all-gather.29.cloned.1.call-start = ((), (), s32[]{:S(2)}) async-start(), calls=%async_computation.41 | async-start | bytes 3932160 | tf_op jit(solution)/shard_map/all_gather | solution.py:278
  743.2 1230.0 %all-gather.37.cloned.1.call-start = ((), (), s32[]{:S(2)}) async-start(), calls=%async_computation.45 | async-start | bytes 3932160 | tf_op jit(solution)/shard_map/all_gather | solution.py:279
  750.4 1238.2 %all-gather.39.cloned.1.call-start = ((), (), s32[]{:S(2)}) async-start(), calls=%async_computation.46 | async-start | bytes 3932160 | tf_op jit(solution)/shard_map/all_gather | solution.py:279
  751.2 1250.3 %all-gather.33.cloned.1.call-start = ((), (), s32[]{:S(2)}) async-start(), calls=%async_computation.43 | async-start | bytes 3932160 | tf_op jit(solution)/shard_map/all_gather | solution.py:279
  751.9 1256.7 %all-gather.35.cloned.1.call-start = ((), (), s32[]{:S(2)}) async-start(), calls=%async_computation.44 | async-start | bytes 3932160 | tf_op jit(solution)/shard_map/all_gather | solution.py:279
  752.7 1267.7 %all-gather.23.cloned.1.call-start = ((), (), s32[]{:S(2)}) async-start(), calls=%async_computation.37 | async-start | bytes 3932160 | tf_op jit(solution)/shard_map/all_gather | solution.py:280
  811.3 1215.3 %all-gather.45.cloned.1.call-start = ((), (), s32[]{:S(2)}) async-start(), calls=%async_computation.50 | async-start | bytes 3932160 | tf_op jit(solution)/shard_map/all_gather | solution.py:277
  941.8 45.5 %all-to-all-start.8 = ((bf16[2,256,768]{1,0,2:T(2,128)(2,1)}), bf16[2,256,768]{1,0,2:T(2,128)(2,1)}, u32[]{:S(2)}, u32[]{:S(2)}) async-start(bf16[2,256,768]{1,0,2:T(2,128)(2,1)} %copy.789), calls=%async_computation.8 | async-start | bytes 1572864 | tf_op jit(solution)/shard_map/all_to_all | solution.py:238
  946.0 1087.4 %all-gather.47.cloned.1.call-start = ((), (), s32[]{:S(2)}) async-start(), calls=%async_computation.51 | async-start | bytes 3932160 | tf_op jit(solution)/shard_map/all_gather | solution.py:277
  963.2 25.9 %collective-permute-start.6 = (bf16[2,2,2304]{2,1,0:T(2,128)(2,1)S(1)}, bf16[2,2,2304]{2,1,0:T(2,128)(2,1)S(1)}, u32[]{:S(2)}, u32[]{:S(2)}) collective-permute-start(bf16[2,2,2304]{2,1,0:T(2,128)(2,1)S(1)} %slice.833), channel_id=1, source_target_pairs={{1,0},{2,1},{3,2},{5,4},{6,5},{7,6},{9,8},{10,9},{11,10},{13,12},{... | collective-permute-start | bytes 55304 | tf_op jit(solution)/shard_map/ppermute | solution.py:20
  1038.6 22.1 all-to-all-start.14
  1297.2 25.4 %all-to-all-start.10 = ((bf16[2,256,768]{1,0,2:T(2,128)(2,1)}), bf16[2,256,768]{1,0,2:T(2,128)(2,1)S(1)}, u32[]{:S(2)}, u32[]{:S(2)}) async-start(bf16[2,256,768]{1,0,2:T(2,128)(2,1)} %copy.811), calls=%async_computation.10 | async-start | bytes 1572864 | tf_op jit(solution)/shard_map/all_to_all | solution.py:238
  1322.6 48.9 %all-to-all-start.28 = ((bf16[2,256,3072]{1,0,2:T(2,128)(2,1)}), bf16[2,256,3072]{1,0,2:T(2,128)(2,1)}, u32[]{:S(2)}, u32[]{:S(2)}) async-start(bf16[2,256,3072]{1,0,2:T(2,128)(2,1)} %copy.928), calls=%async_computation.29 | async-start | bytes 6291456 | tf_op jit(solution)/shard_map/all_to_all | solution.py:283
  1327.3 721.5 %all-gather.41.cloned.1.call-start = ((), (), s32[]{:S(2)}) async-start(), calls=%async_computation.48 | async-start | bytes 3932160 | tf_op jit(solution)/shard_map/all_gather | solution.py:277
  1371.5 52.5 %all-to-all-start.29 = ((bf16[2,256,3072]{1,0,2:T(2,128)(2,1)}), bf16[2,256,3072]{1,0,2:T(2,128)(2,1)}, u32[]{:S(2)}, u32[]{:S(2)}) async-start(bf16[2,256,3072]{1,0,2:T(2,128)(2,1)} %copy.930), calls=%async_computation.30 | async-start | bytes 6291456 | tf_op jit(solution)/shard_map/all_to_all | solution.py:283
  1452.0 24.7 %all-to-all-start.21 = ((bf16[2,256,768]{1,0,2:T(2,128)(2,1)}), bf16[2,256,768]{1,0,2:T(2,128)(2,1)S(1)}, u32[]{:S(2)}, u32[]{:S(2)}) async-start(bf16[2,256,768]{1,0,2:T(2,128)(2,1)} %copy.907), calls=%async_computation.21 | async-start | bytes 1572864 | tf_op jit(solution)/shard_map/all_to_all | solution.py:284
  1477.6 27.3 %all-to-all-start.15 = ((bf16[2,1024,192]{2,0,1:T(2,128)(2,1)}), bf16[2,1024,192]{2,0,1:T(2,128)(2,1)S(1)}, u32[]{:S(2)}, u32[]{:S(2)}) async-start(bf16[2,1024,192]{2,0,1:T(2,128)(2,1)} %copy.873), calls=%async_computation.15 | async-start | bytes 2097152 | tf_op jit(solution)/shard_map/all_to_all | solution.py:244
  1520.2 61.6 %all-to-all-start.31 = ((bf16[2,256,3072]{1,0,2:T(2,128)(2,1)}), bf16[2,256,3072]{1,0,2:T(2,128)(2,1)}, u32[]{:S(2)}, u32[]{:S(2)}) async-start(bf16[2,256,3072]{1,0,2:T(2,128)(2,1)} %copy.934), calls=%async_computation.32 | async-start | bytes 6291456 | tf_op jit(solution)/shard_map/all_to_all | solution.py:283
  1524.9 530.9 %all-gather.43.cloned.1.call-start = ((), (), s32[]{:S(2)}) async-start(), calls=%async_computation.49 | async-start | bytes 3932160 | tf_op jit(solution)/shard_map/all_gather | solution.py:277
  1578.1 22.2 collective-permute-start.5
  1581.8 50.2 %all-to-all-start.30 = ((bf16[2,256,3072]{1,0,2:T(2,128)(2,1)}), bf16[2,256,3072]{1,0,2:T(2,128)(2,1)}, u32[]{:S(2)}, u32[]{:S(2)}) async-start(bf16[2,256,3072]{1,0,2:T(2,128)(2,1)} %copy.932), calls=%async_computation.31 | async-start | bytes 6291456 | tf_op jit(solution)/shard_map/all_to_all | solution.py:283
  1632.0 40.4 %all-to-all-start.27 = ((bf16[2,256,3072]{1,0,2:T(2,128)(2,1)}), bf16[2,256,3072]{1,0,2:T(2,128)(2,1)}, u32[]{:S(2)}, u32[]{:S(2)}) async-start(bf16[2,256,3072]{1,0,2:T(2,128)(2,1)} %copy.925), calls=%async_computation.27 | async-start | bytes 6291456 | tf_op jit(solution)/shard_map/all_to_all | solution.py:285
  1672.4 71.9 %all-to-all-start.26 = ((bf16[2,256,3072]{1,0,2:T(2,128)(2,1)}), bf16[2,256,3072]{1,0,2:T(2,128)(2,1)}, u32[]{:S(2)}, u32[]{:S(2)}) async-start(bf16[2,256,3072]{1,0,2:T(2,128)(2,1)} %copy.922), calls=%async_computation.26 | async-start | bytes 6291456 | tf_op jit(solution)/shard_map/all_to_all | solution.py:285
  1677.1 388.8 %all-gather.17.cloned.1.call-start = ((), (), s32[]{:S(2)}) async-start(), calls=%async_computation.34 | async-start | bytes 3932160 | tf_op jit(solution)/shard_map/all_gather | solution.py:280
  1744.3 87.5 %all-to-all-start.19 = ((bf16[2,256,2304]{1,0,2:T(2,128)(2,1)}), bf16[2,256,2304]{1,0,2:T(2,128)(2,1)}, u32[]{:S(2)}, u32[]{:S(2)}) async-start(bf16[2,256,2304]{1,0,2:T(2,128)(2,1)} %copy.886), calls=%async_computation.19 | async-start | bytes 4718592 | tf_op jit(solution)/shard_map/all_to_all | solution.py:286
  1836.0 235.9 %all-gather.19.cloned.1.call-start = ((), (), s32[]{:S(2)}) async-start(), calls=%async_computation.35 | async-start | bytes 3932160 | tf_op jit(solution)/shard_map/all_gather | solution.py:280
  1850.4 50.2 %all-to-all-start.25 = ((bf16[2,256,3072]{1,0,2:T(2,128)(2,1)}), bf16[2,256,3072]{1,0,2:T(2,128)(2,1)}, u32[]{:S(2)}, u32[]{:S(2)}) async-start(bf16[2,256,3072]{1,0,2:T(2,128)(2,1)} %copy.919), calls=%async_computation.25 | async-start | bytes 6291456 | tf_op jit(solution)/shard_map/all_to_all | solution.py:285
  1900.6 42.7 %all-to-all-start.18 = ((bf16[2,256,2304]{1,0,2:T(2,128)(2,1)}), bf16[2,256,2304]{1,0,2:T(2,128)(2,1)S(1)}, u32[]{:S(2)}, u32[]{:S(2)}) async-start(bf16[2,256,2304]{1,0,2:T(2,128)(2,1)} %copy.883), calls=%async_computation.18 | async-start | bytes 4718592 | tf_op jit(solution)/shard_map/all_to_all | solution.py:286
  1944.7 39.0 %all-to-all-start.24 = ((bf16[2,256,3072]{1,0,2:T(2,128)(2,1)}), bf16[2,256,3072]{1,0,2:T(2,128)(2,1)S(1)}, u32[]{:S(2)}, u32[]{:S(2)}) async-start(bf16[2,256,3072]{1,0,2:T(2,128)(2,1)} %copy.916), calls=%async_computation.24 | async-start | bytes 6291456 | tf_op jit(solution)/shard_map/all_to_all | solution.py:285
  1948.9 171.6 %all-reduce.14.cloned.1.call-start = ((), (), s32[]{:S(2)}) async-start(), calls=%async_computation.53 | async-start | bytes 389120 | tf_op jit(solution)/shard_map/psum | solution.py:440
  1949.6 172.4 %reduce-scatter.7.cloned.1.call-start = ((), (), s32[]{:S(2)}) async-start(), calls=%async_computation.52 | async-start | bytes 663552
  1983.7 32.0 %all-to-all-start.17 = ((bf16[2,256,2304]{1,0,2:T(2,128)(2,1)}), bf16[2,256,2304]{1,0,2:T(2,128)(2,1)}, u32[]{:S(2)}, u32[]{:S(2)}) async-start(bf16[2,256,2304]{1,0,2:T(2,128)(2,1)} %copy.880), calls=%async_computation.17 | async-start | bytes 4718592 | tf_op jit(solution)/shard_map/all_to_all | solution.py:286
  1988.3 135.6 %reduce-scatter.5.cloned.1.call-start = ((), (), s32[]{:S(2)}) async-start(), calls=%async_computation.47 | async-start | bytes 2654208 | tf_op jit(solution)/shard_map/reduce_scatter | solution.py:433
  2015.8 30.9 %all-to-all-start.16 = ((bf16[2,256,2304]{1,0,2:T(2,128)(2,1)}), bf16[2,256,2304]{1,0,2:T(2,128)(2,1)S(1)}, u32[]{:S(2)}, u32[]{:S(2)}) async-start(bf16[2,256,2304]{1,0,2:T(2,128)(2,1)} %copy.877), calls=%async_computation.16 | async-start | bytes 4718592 | tf_op jit(solution)/shard_map/all_to_all | solution.py:286
  2019.9 197.3 %all-reduce.16.cloned.1.call-start = ((), (), s32[]{:S(2)}) async-start(), calls=%async_computation.54 | async-start | bytes 8650752
  2084.6 265.7 %all-reduce.12.cloned.1.call-start = ((), (), s32[]{:S(2)}) async-start(), calls=%async_computation.38 | async-start | bytes 786432 | tf_op jit(solution)/shard_map/psum | solution.py:440
  (393 other events, 8687.7 us)
Sparse Core Ops, SparseCore 0:
  452.5 43.6 all-gather.26
  498.2 44.1 all-gather.24
  544.4 53.3 all-gather.20
  742.7 44.2 all-gather.30
  788.8 49.8 all-gather.28
  840.5 44.2 all-gather.36
  886.8 54.4 all-gather.38
  943.3 45.1 all-gather.32
  990.4 43.9 all-gather.34
  1036.3 50.0 all-gather.22
  1088.4 43.9 all-gather.44
  1134.3 43.9 all-gather.46
  1350.7 73.4 all-gather.40
  1552.4 71.9 all-gather.42
  1684.9 61.0 all-gather.16
  1850.5 89.1 all-gather.18
  1973.3 32.7 reduce-scatter.6
  2015.8 37.9 reduce-scatter.4
Sparse Core Ops, SparseCore 1:
  1956.9 157.1 all-reduce.13
  2116.5 100.6 all-reduce.15
  2223.0 127.3 all-reduce.11
where the time goes:
time: 2380 us; the launch traced here: 2360 us
  matrix products  1190 us (50%)
  local copies, waits for them, and re-layouts  445 us (19%)
  waiting for transfers between devices  364 us (15%)
  starting transfers between devices  160 us (7%)
  other arithmetic  159 us (7%)
  blocking collectives  28.1 us (1%)
    dot_general x10, matrix products, inverse_dft(): jnp.einsum('skbc,ka->sabc', turn_re, cos_outer, precision=HIGHEST)  143 us
    dot_general x10, matrix products, inverse_dft(): jnp.einsum('skbc,ka->sabc', turn_im, sin_outer, precision=HIGHEST)  135 us
    psum x2, waiting for transfers between devices, shards(): lax.psum((vecs[0], vecs[1], vecs[2], vecs[3], vecs[4], vecs[5], filt_part...  129 us
    dot_general x10, matrix products, forward_dft(): jnp.einsum('skbc,bj->skjc', twist_re, sin_inner, precision=HIGHEST)  104 us
    unnamed x23, waiting for transfers between devices  95 us
    dot_general x10, matrix products, forward_dft(): jnp.einsum('skbc,bj->skjc', twist_im, cos_inner, precision=HIGHEST)  69.7 us
    dot_general x10, matrix products, forward_dft(): jnp.einsum('skbc,bj->skjc', twist_re, cos_inner, precision=HIGHEST)  62.2 us
    unnamed x780, local copies, waits for them, and re-layouts  60.3 us
  transfers between devices with their start and end apart: 60, of which 18 were waited for; matrix products, arithmetic and copies ran while one was open for 62% of the time, Pallas kernels for 0%

commit v1 on v0

--- a/solution.py
+++ b/solution.py
@@ -2,6 +2,7 @@
 
 import jax
 import jax.numpy as jnp
+import numpy as np
 from jax import lax
 from jax.sharding import PartitionSpec as P
 
@@ -138,7 +139,7 @@
     return jax.tree.map(jnp.add, running, update)
 
 
-def shards(
+def split_positions(
     x_in,
     cotangent,
     counts,
@@ -474,6 +475,180 @@
     )
 
 
+def spectral_table(length):
+    k = np.arange(length, dtype=np.int64)[:, None]
+    t = np.arange(length, dtype=np.int64)[None, :]
+    angle = ((2 * k + 1) * t % (4 * length)).astype(np.float64) * (2.0 * math.pi / (4 * length))
+    return np.concatenate([np.cos(angle), -np.sin(angle)], axis=0).astype(jnp.bfloat16)
+
+
+def mm(left, right):
+    return jnp.dot(left, right, preferred_element_type=jnp.float32)
+
+
+def mm_nt(left, right):
+    return lax.dot_general(left, right, (((1,), (1,)), ((), ())), preferred_element_type=jnp.float32)
+
+
+def mm_tn(left, right):
+    return lax.dot_general(left, right, (((0,), (0,)), ((), ())), preferred_element_type=jnp.float32)
+
+
+def shifted(values, distance):
+    rows = values.shape[0]
+    zeros = jnp.zeros((abs(distance), values.shape[1]), values.dtype)
+    if distance > 0:
+        return jnp.concatenate([zeros, values[: rows - distance]], axis=0)
+    return jnp.concatenate([values[-distance:], zeros], axis=0)
+
+
+def whole_sequences(
+    x_in, cotangent, counts, ln1_gain, ln1_bias, w_in, short_w, filt_w1, filt_freq, filt_w2, filt_w3, long_bias,
+    w_out, ln2_gain, ln2_bias, w_up, w_down,
+):
+    micro_count, cap_size, tok_rows, width = x_in.shape
+    slots = micro_count * cap_size
+    layers = w_in.shape[0]
+    length = tok_rows * lax.axis_size("tok")
+    me = lax.axis_index("tok")
+
+    def gather_mine(block):
+        return lax.all_to_all(block.reshape(slots, tok_rows, width), "tok", split_axis=0, concat_axis=1, tiled=True)[0]
+
+    def scatter_back(rows):
+        blocks = rows.reshape(slots, tok_rows, width)
+        back = lax.all_to_all(blocks, "tok", split_axis=0, concat_axis=0, tiled=True)
+        return back.reshape(micro_count, cap_size, tok_rows, width)
+
+    live = (me % cap_size < counts[me // cap_size, 0]).astype(jnp.float32)
+    f32 = lambda v: v.astype(jnp.float32)
+    bf = lambda v: v.astype(jnp.bfloat16)
+    table = jnp.asarray(spectral_table(length))
+    table_back = jnp.asarray(spectral_table(length).T.copy())
+    features = position_features(length)
+    envelope = decay_table(features[:, :1], 0.0, width, width)
+
+    def spectrum(rows):
+        both = mm(table, rows)
+        return both[:length], both[length:]
+
+    def from_spectrum(re, im):
+        return mm(table_back, jnp.concatenate([bf(re), bf(im)], axis=0)) * (1.0 / length)
+
+    def taps_fn(layer):
+        def fn(one, sine, two, three):
+            return filter_taps(features, one, sine, two, three, envelope)
+
+        return jax.vjp(fn, f32(filt_w1[layer]), f32(filt_freq[layer]), f32(filt_w2[layer]), f32(filt_w3[layer]))
+
+    residual = f32(gather_mine(x_in))
+    filters = [taps_fn(layer) for layer in range(layers)]
+    spectra = [spectrum(bf(filters[layer][0])) for layer in range(layers)]
+    kept = []
+    for layer in range(layers):
+        g1, b1, g2, b2 = f32(ln1_gain[layer]), f32(ln1_bias[layer]), f32(ln2_gain[layer]), f32(ln2_bias[layer])
+        kernel, skip = f32(short_w[layer]), f32(long_bias[layer])
+        normed = bf(layer_norm(residual, g1, b1))
+        projected = mm(normed, w_in[layer])
+        mixed = kernel[0] * shifted(projected, 2) + kernel[1] * shifted(projected, 1) + kernel[2] * projected
+        gate_out, gate_in, vals = mixed[:, :width], mixed[:, width : 2 * width], mixed[:, 2 * width :]
+        carried = vals * gate_in
+        sig_re, sig_im = spectrum(bf(carried))
+        tap_re, tap_im = spectra[layer]
+        long_out = from_spectrum(*complex_product(sig_re, sig_im, tap_re, tap_im)) + skip * carried
+        gated = bf(long_out * gate_out)
+        hidden = residual + mm(gated, w_out[layer])
+        normed_two = bf(layer_norm(hidden, g2, b2))
+        raised = mm(normed_two, w_up[layer])
+        active = bf(gelu_tanh(raised))
+        result = hidden + mm(active, w_down[layer])
+        kept.append((residual, normed, projected, mixed, carried, long_out, gated, hidden, normed_two, raised, active,
+                     bf(sig_re), bf(sig_im)))
+        residual = result
+    out_act = scatter_back(bf(residual * live)).astype(jnp.float32)
+
+    grad = f32(gather_mine(cotangent)) * live
+    mats = [None] * layers
+    vecs = [None] * layers
+    for layer in reversed(range(layers)):
+        (residual, normed, projected, mixed, carried, long_out, gated, hidden, normed_two, raised, active, sig_re,
+         sig_im) = kept[layer]
+        g1, b1, g2, b2 = f32(ln1_gain[layer]), f32(ln1_bias[layer]), f32(ln2_gain[layer]), f32(ln2_bias[layer])
+        kernel, skip = f32(short_w[layer]), f32(long_bias[layer])
+        gate_out, gate_in, vals = mixed[:, :width], mixed[:, width : 2 * width], mixed[:, 2 * width :]
+        down_grad = bf(grad)
+        grad_down = mm_tn(active, down_grad)
+        _, gelu_pull = jax.vjp(gelu_tanh, raised)
+        raised_grad = bf(gelu_pull(mm_nt(down_grad, w_down[layer]))[0])
+        grad_up = mm_tn(normed_two, raised_grad)
+        _, second_pull = jax.vjp(layer_norm, hidden, g2, b2)
+        hidden_part, grad_g2, grad_b2 = second_pull(mm_nt(raised_grad, w_up[layer]))
+        hidden_grad = grad + hidden_part
+        out_grad = bf(hidden_grad)
+        grad_out = mm_tn(gated, out_grad)
+        gated_grad = mm_nt(out_grad, w_out[layer])
+        long_grad = gated_grad * gate_out
+        gate_out_grad = gated_grad * long_out
+        grad_skip = jnp.sum(carried * long_grad, axis=0)
+        up_re, up_im = spectrum(bf(long_grad))
+        tap_re, tap_im = spectra[layer]
+        carried_grad = from_spectrum(*complex_product(up_re, up_im, tap_re, -tap_im)) + skip * long_grad
+        cross = complex_product(up_re, up_im, f32(sig_re), -f32(sig_im))
+        taps_grad = from_spectrum(*cross)
+        mixed_grad = jnp.concatenate([gate_out_grad, carried_grad * vals, carried_grad * gate_in], axis=1)
+        projected_grad = bf(
+            kernel[2] * mixed_grad + kernel[1] * shifted(mixed_grad, -1) + kernel[0] * shifted(mixed_grad, -2)
+        )
+        grad_short = jnp.stack(
+            [jnp.sum(mixed_grad * (shifted(projected, 2 - k) if k < 2 else projected), axis=0) for k in range(3)]
+        )
+        grad_proj = mm_tn(normed, projected_grad)
+        _, first_pull = jax.vjp(layer_norm, residual, g1, b1)
+        first_part, grad_g1, grad_b1 = first_pull(mm_nt(projected_grad, w_in[layer]))
+        grad = hidden_grad + first_part
+        filter_grads = filters[layer][1](taps_grad)
+        mats[layer] = (grad_proj, grad_out, grad_up, grad_down)
+        vecs[layer] = (grad_g1, grad_b1, grad_short, grad_skip, grad_g2, grad_b2) + tuple(filter_grads)
+    grad_in = scatter_back(bf(grad)).astype(jnp.float32)
+
+    def pair_sum(block, dim):
+        count = lax.axis_size("seq")
+        core = lax.axis_index("seq") % 2
+        shape = block.shape
+        piece = shape[dim] // count
+        split = block.reshape(shape[:dim] + (count // 2, 2, piece) + shape[dim + 1 :])
+        mine = lax.dynamic_index_in_dim(split, core, dim + 1, keepdims=False)
+        other = lax.dynamic_index_in_dim(split, 1 - core, dim + 1, keepdims=False)
+        got = lax.ppermute(other, "seq", [(i, i ^ 1) for i in range(count)])
+        return mine + got
+
+    def reduced(block, seq_dim, tok_dim):
+        block = bf(block)
+        return lax.psum_scatter(
+            lax.psum_scatter(block, "tok", scatter_dimension=tok_dim, tiled=True),
+            "seq", scatter_dimension=seq_dim, tiled=True,
+        ).astype(jnp.float32)
+
+    dims = ((0, 1), (0, 1), (0, 1), (1, 0))
+    mat_done = [
+        jnp.stack([reduced(mats[layer][m], *dims[m]) for layer in range(layers)]) for m in range(4)
+    ]
+    small = lax.psum(
+        tuple(jnp.stack([vecs[layer][m] for layer in range(layers)]) for m in range(10)), ("seq", "tok")
+    )
+    return (
+        out_act, grad_in, small[0], small[1], mat_done[0], small[2], small[6], small[7], small[8], small[9], small[3],
+        mat_done[1], small[4], small[5], mat_done[2], mat_done[3],
+    )
+
+
+def shards(*args):
+    micro_count, cap_size = args[0].shape[:2]
+    if lax.axis_size("tok") == micro_count * cap_size:
+        return whole_sequences(*args)
+    return split_positions(*args)
+
+
 def solution(mesh):
     return jax.shard_map(
         shards,

time: 2380 us -> 991 us (0.42)
  matrix products: 1190 us -> 361 us
  local copies, waits for them, and re-layouts: 445 us -> 70.4 us
  starting transfers between devices: 160 us -> 15.4 us
  other arithmetic: 159 us -> 103 us
  waiting for transfers between devices: 364 us -> 389 us
    dot_general x168 -> x42, matrix products: 1160 us -> 334 us  [the longest x26 191 us: mm(): return jnp.dot(left, right, preferred_element_type=jnp.float32)]
    reduce_scatter x1 -> x10, waiting for transfers between devices: 0.01 us -> 255 us  [the longest x8 191 us: reduced(): lax.psum_scatter(block, 'tok', scatter_dimension=tok_dim, tiled=True)]
    all_to_all x60 -> x0, local copies, waits for them, and re-layouts: 176 us -> none  [the longest x8 48.7 us: backward_layer(): lax.all_to_all(active, 'tok', split_axis=2, concat_axis=1, tiled=True)]
    convert_element_type x40 -> x0, local copies, waits for them, and re-layouts: 152 us -> none  [the longest x4 35.4 us: backward_layer(): raised_grad = gelu_pull(active_grad)[0].astype(jnp.bfloat16)]
    all_to_all x31 -> x3, waiting for transfers between devices: 138 us -> 5.58 us  [the longest x1 5.58 us: scatter_back(): lax.all_to_all(blocks, 'tok', split_axis=0, concat_axis=0, tiled=True)]
    psum x2, waiting for transfers between devices: 129 us -> 0.03 us  [whole_sequences(): lax.psum(tuple((jnp.stack([vecs[layer][m] for layer in range(layers)]) fo...]
    all_to_all x31 -> x3, starting transfers between devices: 136 us -> 14 us  [the longest x2 9.65 us: gather_mine(): lax.all_to_all(block.reshape(slots, tok_rows, width), 'tok', split_axis=0...]
    unnamed x23 -> x24, waiting for transfers between devices: 95 us -> 129 us
  transfers between devices with their start and end apart: 60 -> 21, of which waited for: 18 -> 12; matrix products, arithmetic and copies ran while one was open for 62% -> 45% of each run, Pallas kernels for 0% -> 0%
where the time goes in v1:
time: 991 us; the launch traced here: 981 us
  waiting for transfers between devices  389 us (39%)
  matrix products  361 us (36%)
  other arithmetic  103 us (10%)
  local copies, waits for them, and re-layouts  70.4 us (7%)
  blocking collectives  23.5 us (2%)
  between operations  18.7 us (2%)
  starting transfers between devices  15.4 us (2%)
    dot_general x26, matrix products, mm(): return jnp.dot(left, right, preferred_element_type=jnp.float32)  191 us
    reduce_scatter x8, waiting for transfers between devices, reduced(): lax.psum_scatter(block, 'tok', scatter_dimension=tok_dim, tiled=True)  191 us
    unnamed x24, waiting for transfers between devices  129 us
    dot_general x8, matrix products, mm_nt(): lax.dot_general(left, right, (((1,), (1,)), ((), ())), preferred_element_...  80.6 us
    reduce_scatter x2, waiting for transfers between devices, reduced(): lax.psum_scatter(lax.psum_scatter(block, 'tok', scatter_dimension=tok_dim...  63.9 us
    dot_general x8, matrix products, mm_tn(): lax.dot_general(left, right, (((0,), (0,)), ((), ())), preferred_element_...  62.8 us
    reduce_sum x2, other arithmetic, whole_sequences(): jnp.sum(mixed_grad * (shifted(projected, 2 - k) if k < 2 else projected),...  47.3 us
    unnamed x337, local copies, waits for them, and re-layouts  43.2 us
  transfers between devices with their start and end apart: 21, of which 12 were waited for; matrix products, arithmetic and copies ran while one was open for 45% of the time, Pallas kernels for 0%

profile of v1, /device:TPU:0, one launch (start us, length us, event | category | flops | bytes accessed | tf_op | source)
XLA Modules:
  0.0 981.4 jit_solution(6853160418355402077)
XLA Ops:
  30.6 8.3 fusion.182
  46.5 6.0 fusion.48
  56.4 11.6 %fusion.94 = f32[2048,768]{1,0:T(8,128)} fusion(bf16[2048,1024]{1,0:T(8,128)(2,1)} %constant.101.clone, f32[1024,2304]{1,0:T(8,128)S(1)} %multiply_add_fusion.1), kind=kOutput, calls=%fused_computation.179 | convolution fusion | flops 3222798336 | bytes 16777216 | tf_op jit(solution)/shard_map/dot_general | solution.py:486
  68.0 6.5 fusion.96
  74.5 7.6 multiply_convert_fusion.5
  87.2 8.4 fusion.28
  95.7 10.6 %fusion.177 = (f32[1024]{0:T(1024)S(1)}, f32[1024,768]{1,0:T(8,128)S(1)}) fusion(f32[1024,768]{1,0:T(8,128)S(1)} %get-tuple-element.147, bf16[2,3072,768]{2,1,0:T(8,128)(2,1)S(1)} %bitcast.304, f32[1024,3072]{1,0:T(8,128)} %fusion.28), kind=kOutput, calls=%fused_computation.353 | convolution fusion | flops 4861721600 | bytes 23597056 | tf_op jit(solution)/shard_map/dot_general | solution.py:486
  106.9 6.7 fusion.44
  117.5 11.7 %fusion.92 = f32[2048,768]{1,0:T(8,128)} fusion(bf16[2048,1024]{1,0:T(8,128)(2,1)} %constant.101.clone, f32[1024,2304]{1,0:T(8,128)S(1)} %multiply_add_fusion), kind=kOutput, calls=%fused_computation.177 | convolution fusion | flops 3222798336 | bytes 16777216 | tf_op jit(solution)/shard_map/dot_general | solution.py:486
  129.2 6.4 fusion.97
  135.6 8.1 multiply_convert_fusion.3
  147.5 11.2 %fusion.20 = f32[1024,3072]{1,0:T(8,128)} fusion(bf16[2,768,3072]{2,1,0:T(8,128)(2,1)} %param.34, f32[1024,768]{1,0:T(8,128)S(1)} %get-tuple-element.153, f32[768]{0:T(1024)S(1)} %get-tuple-element.91, f32[768]{0:T(1024)S(1)} %get-tuple-element.175, f32[1024]{0:T(1024)S(1)} %fusion.160, f32[1024]{0:T(1024)S(1)} %broadcast_multiply_fusion), kind=kOutput, calls=%fused_computation.48 | convolution fusion | flops 4835770368 | bytes 20461568 | tf_op jit(solution)/shard_map/dot_general | solution.py:486
  160.7 17.6 %fusion.13 = bf16[1024,3072]{1,0:T(8,128)(2,1)} fusion(f32[1024,3072]{1,0:T(8,128)} %fusion.20, bf16[1024,768]{1,0:T(8,128)(2,1)S(1)} %bitcast.276, bf16[2,3072,768]{2,1,0:T(8,128)(2,1)} %param.35), kind=kOutput, calls=%fused_computation.17 | convolution fusion | flops 4894752768 | bytes 25165824 | tf_op jit(solution)/shard_map/dot_general | solution.py:490
  178.2 8.5 multiply_reduce_fusion.6
  208.0 11.2 %slice_multiply_fusion.3 = (f32[1024,768]{1,0:T(8,128)}, f32[1024,768]{1,0:T(8,128)}, f32[768]{0:T(1024)}) fusion(f32[1024,2304]{1,0:T(8,128)} %copy-done.21, f32[1024,768]{1,0:T(8,128)S(1)} %get-tuple-element.156, f32[768]{0:T(1024)S(1)} %get-tuple-element.93, f32[768,1024]{0,1:T(8,128)S(1)} %fusion.98, bf16[1024,1024]{1,0:T(8,128)(2,1)S(1)} %copy-done.9, ...), kind=kOutput, calls=%fused_computation.160 | convolution fusion | flops 1622408448 | bytes 36706304 | tf_op jit(solution)/shard_map/dot_general | solution.py:486
  219.3 8.0 pad_maximum_fusion
  227.3 8.7 slice.336
  240.2 24.1 %multiply_reduce_fusion.2 = (f32[2304]{0:T(1024)}, f32[2304]{0:T(1024)}, f32[2304]{0:T(1024)}, bf16[1024,2304]{1,0:T(8,128)(2,1)}) fusion(f32[1022,2304]{1,0:T(8,128)} %bitcast.258, f32[1024,768]{1,0:T(8,128)} %get-tuple-element.117, f32[1024,768]{1,0:T(8,128)} %get-tuple-element.116, f32[1024,768]{1,0:T(8,128)} %get-tuple-element.155, ...), kind=kLoop, calls=%fused_computation.24 | loop fusion | flops 33023232 | bytes 61341696 | tf_op jit(solution)/shard_map/reduce_sum | solution.py:603
  264.3 9.4 multiply_reduce_fusion.10
  276.2 16.9 %fusion.6 = bf16[1024,3072]{1,0:T(8,128)(2,1)} fusion(f32[1024,3072]{1,0:T(8,128)} %fusion.28, bf16[2,3072,768]{2,1,0:T(8,128)(2,1)} %param.35, f32[1024,768]{1,0:T(8,128)S(1)} %add_add_fusion.5), kind=kOutput, calls=%fused_computation.10 | convolution fusion | flops 4895539200 | bytes 26738688 | tf_op jit(solution)/shard_map/dot_general | solution.py:490
  293.1 9.2 multiply_reduce_fusion.7
  308.7 6.4 fusion.180
  316.8 7.4 fusion.88
  324.2 6.3 convolution_convert_fusion.4
  330.6 7.4 fusion.99
  338.1 12.0 %slice_multiply_fusion.7 = (f32[1024,768]{1,0:T(8,128)}, f32[1024,768]{1,0:T(8,128)}, f32[768]{0:T(1024)S(1)}) fusion(f32[1024,2304]{1,0:T(8,128)} %copy-done.20, f32[1024,768]{1,0:T(8,128)S(1)} %copy-done.30, f32[768]{0:T(1024)S(1)} %copy-done.79, f32[768,1024]{0,1:T(8,128)S(1)} %fusion.99, bf16[1024,1024]{1,0:T(8,128)(2,1)S(1)} %copy-done.9, ...), kind=kOutput, calls=%fused_computation.164 | convolution fusion | flops 1622408448 | bytes 36706304 | tf_op jit(solution)/shard_map/dot_general | solution.py:486
  350.1 8.0 pad_maximum_fusion.1
  358.1 9.2 slice.340
  372.2 23.2 %multiply_reduce_fusion.5 = (f32[2304]{0:T(1024)S(1)}, f32[2304]{0:T(1024)S(1)}, f32[2304]{0:T(1024)S(1)}, bf16[1024,2304]{1,0:T(8,128)(2,1)}) fusion(f32[1022,2304]{1,0:T(8,128)} %bitcast.254, f32[1024,768]{1,0:T(8,128)} %get-tuple-element.115, f32[1024,768]{1,0:T(8,128)} %get-tuple-element.114, f32[1024,768]{1,0:T(8,128)} %get-tuple-element.159, ...), kind=kLoop, calls=%fused_computation.27 | loop fusion | flops 33023232 | bytes 61341696 | tf_op jit(solution)/shard_map/reduce_sum | solution.py:603
  395.4 7.1 fusion.171
  414.6 12.0 %convolution_convert_fusion = bf16[3072,768]{1,0:T(8,128)(2,1)} fusion(bf16[1024,768]{1,0:T(8,128)(2,1)S(1)} %bitcast_convert_fusion, f32[1024,3072]{1,0:T(8,128)} %fusion.20), kind=kOutput, calls=%fused_computation.32 | convolution fusion | flops 4862509056 | bytes 18874368 | tf_op jit(solution)/shard_map/dot_general | solution.py:494
  426.6 12.9 %convolution_convert_fusion.1 = bf16[3072,768]{1,0:T(8,128)(2,1)} fusion(f32[1024,768]{1,0:T(8,128)} %copy-done.28, f32[1024,3072]{1,0:T(8,128)} %fusion.28), kind=kOutput, calls=%fused_computation.33 | convolution fusion | flops 4863295488 | bytes 20447232 | tf_op jit(solution)/shard_map/dot_general | solution.py:494
  440.2 10.5 %convolution_convert_fusion.2 = bf16[768,3072]{1,0:T(8,128)(2,1)} fusion(bf16[1024,3072]{1,0:T(8,128)(2,1)} %fusion.13, f32[1024,768]{1,0:T(8,128)} %copy-done.11, f32[768]{0:T(1024)S(1)} %copy-done.112, f32[768]{0:T(1024)S(1)} %copy-done.83, f32[1024]{0:T(1024)S(1)} %copy-done.87, f32[1024]{0:T(1024)S(1)} %copy-done.73), kind=kOutput, calls=%fused_computation.34 | convolution fusion | flops 4838129664 | bytes 14170112 | tf_op jit(solution)/shard_map/dot_general | solution.py:494
  451.4 10.5 %convolution_convert_fusion.3 = bf16[768,3072]{1,0:T(8,128)(2,1)} fusion(bf16[1024,3072]{1,0:T(8,128)(2,1)} %fusion.6, f32[1024,768]{1,0:T(8,128)} %copy-done.22, f32[768]{0:T(1024)S(1)} %copy-done.110, f32[768]{0:T(1024)S(1)} %copy-done.81, f32[1024]{0:T(1024)S(1)} %copy-done.85, f32[1024]{0:T(1024)S(1)} %copy-done.71), kind=kOutput, calls=%fused_computation.35 | convolution fusion | flops 4838129664 | bytes 14170112 | tf_op jit(solution)/shard_map/dot_general | solution.py:494
  462.9 7.2 fusion.83
  470.2 7.1 bitcast_multiply_fusion
  507.6 14.2 %reduce-scatter.47.cloned.1.call-done = bf16[768,768]{1,0:T(8,128)(2,1)} async-done(((bf16[3072,768]{1,0:T(8,128)(2,1)}), bf16[768,768]{1,0:T(8,128)(2,1)}) %reduce-scatter.47.cloned.1.call-update) | async-done | bytes 1179664 | tf_op jit(solution)/shard_map/reduce_scatter | solution.py:628
  524.2 58.1 %reduce-scatter.45.cloned.1.call-done = bf16[768,768]{1,0:T(8,128)(2,1)} async-done(((bf16[3072,768]{1,0:T(8,128)(2,1)}), bf16[768,768]{1,0:T(8,128)(2,1)}) %reduce-scatter.45.cloned.1.call-update) | async-done | bytes 1179664 | tf_op jit(solution)/shard_map/reduce_scatter | solution.py:628
  584.7 58.2 %reduce-scatter.41.cloned.1.call-done = bf16[768,768]{1,0:T(8,128)(2,1)} async-done(((bf16[768,3072]{1,0:T(8,128)(2,1)}), bf16[768,768]{1,0:T(8,128)(2,1)}) %reduce-scatter.41.cloned.1.call-update) | async-done | bytes 1179664 | tf_op jit(solution)/shard_map/reduce_scatter | solution.py:628
  643.0 60.2 %reduce-scatter.37.cloned.1.call-done = bf16[768,768]{1,0:T(8,128)(2,1)} async-done(((bf16[768,3072]{1,0:T(8,128)(2,1)}), bf16[768,768]{1,0:T(8,128)(2,1)}) %reduce-scatter.37.cloned.1.call-update) | async-done | bytes 1179664 | tf_op jit(solution)/shard_map/reduce_scatter | solution.py:628
  703.3 11.7 %multiply_convert_fusion.2 = bf16[1024,768]{1,0:T(8,128)(2,1)S(1)} fusion(f32[1024,768]{1,0:T(8,128)S(1)} %copy-done.12, bf16[2,3072,768]{2,1,0:T(8,128)(2,1)} %param.35, f32[]{:T(128)S(6)} %convert_element_type.327, f32[1024,3072]{1,0:T(8,128)} %fusion.20), kind=kOutput, calls=%fused_computation.137 | convolution fusion | flops 4862509056 | bytes 22020100 | tf_op jit(solution)/shard_map/dot_general | solution.py:486
  715.0 23.5 %all_to_all.28 = bf16[4,256,768]{2,1,0:T(8,128)(2,1)} all-to-all(bf16[4,256,768]{2,1,0:T(8,128)(2,1)S(1)} %bitcast.274), channel_id=1, replica_groups=mesh['seq'=8,'tok'=4] {'tok'}, dimensions={0} | all-to-all | bytes 3145728 | tf_op jit(solution)/shard_map/all_to_all | solution.py:520
  770.2 30.9 %reduce-scatter.51.cloned.1.call-done = bf16[96,576]{1,0:T(8,128)(2,1)} async-done(((bf16[768,576]{1,0:T(8,128)(2,1)}), bf16[96,576]{1,0:T(8,128)(2,1)}) %reduce-scatter.51.cloned.1.call-update) | async-done | bytes 110608
  802.2 31.5 %reduce-scatter.49.cloned.1.call-done = bf16[96,576]{1,0:T(8,128)(2,1)} async-done(((bf16[768,576]{1,0:T(8,128)(2,1)}), bf16[96,576]{1,0:T(8,128)(2,1)}) %reduce-scatter.49.cloned.1.call-update) | async-done | bytes 110608
  835.9 30.9 %reduce-scatter.59.cloned.1.call-done = bf16[96,768]{1,0:T(8,128)(2,1)} async-done(((bf16[768,768]{1,0:T(8,128)(2,1)}), bf16[96,768]{1,0:T(8,128)(2,1)}) %reduce-scatter.59.cloned.1.call-update) | async-done | bytes 147472
  867.9 32.3 %reduce-scatter.57.cloned.1.call-done = bf16[96,768]{1,0:T(8,128)(2,1)} async-done(((bf16[768,768]{1,0:T(8,128)(2,1)}), bf16[96,768]{1,0:T(8,128)(2,1)}) %reduce-scatter.57.cloned.1.call-update) | async-done | bytes 147472
  902.4 31.0 %reduce-scatter.43.cloned.1.call-done = bf16[96,768]{1,0:T(8,128)(2,1)} async-done(((bf16[768,768]{1,0:T(8,128)(2,1)}), bf16[96,768]{1,0:T(8,128)(2,1)}) %reduce-scatter.43.cloned.1.call-update) | async-done | bytes 147472 | tf_op jit(solution)/shard_map/reduce_scatter | solution.py:627
  933.4 32.9 %reduce-scatter.39.cloned.1.call-done = bf16[96,768]{1,0:T(8,128)(2,1)} async-done(((bf16[768,768]{1,0:T(8,128)(2,1)}), bf16[96,768]{1,0:T(8,128)(2,1)}) %reduce-scatter.39.cloned.1.call-update) | async-done | bytes 147472 | tf_op jit(solution)/shard_map/reduce_scatter | solution.py:627
  (513 shorter events, 183.4 us)
Async XLA Ops:
  8.1 30.8 %all-to-all-start = ((bf16[4,256,768]{2,1,0:T(8,128)(2,1)}), bf16[4,256,768]{2,1,0:T(8,128)(2,1)S(1)}, u32[]{:S(2)}, u32[]{:S(2)}) async-start(bf16[4,256,768]{2,1,0:T(8,128)(2,1)} %bitcast.273), calls=%async_computation | async-start | bytes 3145728 | tf_op jit(solution)/shard_map/all_to_all | solution.py:516
  14.9 30.9 %copy-start.62 = (f32[768]{0:T(1024)}, f32[768]{0:T(1024)S(1)}, u32[]{:S(2)}) copy-start(f32[768]{0:T(1024)S(1)} %get-tuple-element.170) | copy-start | bytes 9220
  14.9 30.9 %copy-start.68 = (f32[768]{0:T(1024)}, f32[768]{0:T(1024)S(1)}, u32[]{:S(2)}) copy-start(f32[768]{0:T(1024)S(1)} %get-tuple-element.98) | copy-start | bytes 9220
  15.0 92.0 %copy-start.113 = (f32[768]{0:T(1024)}, f32[768]{0:T(1024)S(1)}, u32[]{:S(2)}) copy-start(f32[768]{0:T(1024)S(1)} %get-tuple-element.97) | copy-start | bytes 9220
  15.0 71.1 %copy-start.80 = (f32[768]{0:T(1024)}, f32[768]{0:T(1024)S(1)}, u32[]{:S(2)}) copy-start(f32[768]{0:T(1024)S(1)} %get-tuple-element.174) | copy-start | bytes 9220
  15.0 71.1 %copy-start.109 = (f32[768]{0:T(1024)}, f32[768]{0:T(1024)S(1)}, u32[]{:S(2)}) copy-start(f32[768]{0:T(1024)S(1)} %get-tuple-element.92) | copy-start | bytes 9220
  15.0 132.5 %copy-start.111 = (f32[768]{0:T(1024)}, f32[768]{0:T(1024)S(1)}, u32[]{:S(2)}) copy-start(f32[768]{0:T(1024)S(1)} %get-tuple-element.91) | copy-start | bytes 9220
  15.0 171.7 %copy-start.82 = (f32[768]{0:T(1024)}, f32[768]{0:T(1024)S(1)}, u32[]{:S(2)}) copy-start(f32[768]{0:T(1024)S(1)} %get-tuple-element.175) | copy-start | bytes 9220
  26.3 48.3 %copy-start.78 = (f32[768]{0:T(1024)}, f32[768]{0:T(1024)S(1)}, u32[]{:S(2)}) copy-start(f32[768]{0:T(1024)S(1)} %get-tuple-element.94) | copy-start | bytes 9220
  27.6 24.9 %copy-start.52 = (f32[2304]{0:T(1024)}, f32[2304]{0:T(1024)S(1)}, u32[]{:S(2)}) copy-start(f32[2304]{0:T(1024)S(1)} %get-tuple-element.86) | copy-start | bytes 27652
  27.6 24.9 %copy-start.54 = (f32[2304]{0:T(1024)}, f32[2304]{0:T(1024)S(1)}, u32[]{:S(2)}) copy-start(f32[2304]{0:T(1024)S(1)} %get-tuple-element.87) | copy-start | bytes 27652
  38.9 43.2 %copy-start.6 = (bf16[4,256,768]{2,1,0:T(8,128)(2,1)}, bf16[4,256,768]{2,1,0:T(8,128)(2,1)S(1)}, u32[]{:S(2)}) copy-start(bf16[4,256,768]{2,1,0:T(8,128)(2,1)S(1)} %all-to-all-done) | copy-start | bytes 4718596
  38.9 119.8 %all-to-all-start.2 = ((bf16[4,256,768]{2,1,0:T(8,128)(2,1)}), bf16[4,256,768]{2,1,0:T(8,128)(2,1)}, u32[]{:S(2)}, u32[]{:S(2)}) async-start(bf16[4,256,768]{2,1,0:T(8,128)(2,1)} %bitcast.26), calls=%async_computation.2 | async-start | bytes 3145728 | tf_op jit(solution)/shard_map/all_to_all | solution.py:516
  43.2 455.6 %reduce-scatter.35.cloned.1.call-start = ((), (), s32[]{:S(2)}) async-start(), calls=%async_computation.24 | async-start | bytes 1474560 | tf_op jit(solution)/shard_map/reduce_scatter | solution.py:628
  106.4 37.3 %copy-start.13 = (f32[1024,768]{1,0:T(8,128)}, f32[1024,768]{1,0:T(8,128)S(1)}, u32[]{:S(2)}) copy-start(f32[1024,768]{1,0:T(8,128)S(1)} %get-tuple-element.149) | copy-start | bytes 9437188
  146.9 39.8 %copy-start.11 = (f32[1024,768]{1,0:T(8,128)}, f32[1024,768]{1,0:T(8,128)S(1)}, u32[]{:S(2)}) copy-start(f32[1024,768]{1,0:T(8,128)S(1)} %get-tuple-element.153) | copy-start | bytes 9437188
  147.0 39.8 %copy-start.72 = (f32[1024]{0:T(1024)}, f32[1024]{0:T(1024)S(1)}, u32[]{:S(2)}) copy-start(f32[1024]{0:T(1024)S(1)} %broadcast_multiply_fusion) | copy-start | bytes 12292
  147.5 39.3 %copy-start.86 = (f32[1024]{0:T(1024)}, f32[1024]{0:T(1024)S(1)}, u32[]{:S(2)}) copy-start(f32[1024]{0:T(1024)S(1)} %fusion.160) | copy-start | bytes 12292
  160.6 27.7 %copy-start.10 = (f32[4,256,768]{2,1,0:T(8,128)}, f32[4,256,768]{2,1,0:T(8,128)S(1)}, u32[]{:S(2)}) copy-start(f32[4,256,768]{2,1,0:T(8,128)S(1)} %get-tuple-element.125) | copy-start | bytes 9437188
  240.2 260.7 %reduce-scatter.33.cloned.1.call-start = ((), (), s32[]{:S(2)}) async-start(), calls=%async_computation.23 | async-start | bytes 1474560 | tf_op jit(solution)/shard_map/reduce_scatter | solution.py:628
  276.1 27.9 %copy-start.28 = (f32[1024,768]{1,0:T(8,128)}, f32[1024,768]{1,0:T(8,128)S(1)}, u32[]{:S(2)}) copy-start(f32[1024,768]{1,0:T(8,128)S(1)} %add_add_fusion.5) | copy-start | bytes 9437188
  308.6 194.2 %reduce-scatter.31.cloned.1.call-start = ((), (), s32[]{:S(2)}) async-start(), calls=%async_computation.21 | async-start | bytes 4423680 | tf_op jit(solution)/shard_map/reduce_scatter | solution.py:628
  330.6 174.6 %reduce-scatter.29.cloned.1.call-start = ((), (), s32[]{:S(2)}) async-start(), calls=%async_computation.20 | async-start | bytes 4423680 | tf_op jit(solution)/shard_map/reduce_scatter | solution.py:628
  412.5 109.3 %reduce-scatter.47.cloned.1.call-start = ((), (), s32[]{:S(2)}) async-start(), calls=%async_computation.30 | async-start | bytes 5898240 | tf_op jit(solution)/shard_map/reduce_scatter | solution.py:628
  426.6 155.7 %reduce-scatter.45.cloned.1.call-start = ((), (), s32[]{:S(2)}) async-start(), calls=%async_computation.29 | async-start | bytes 5898240 | tf_op jit(solution)/shard_map/reduce_scatter | solution.py:628
  439.6 203.3 %reduce-scatter.41.cloned.1.call-start = ((), (), s32[]{:S(2)}) async-start(), calls=%async_computation.27 | async-start | bytes 5898240 | tf_op jit(solution)/shard_map/reduce_scatter | solution.py:628
  450.7 252.5 %reduce-scatter.37.cloned.1.call-start = ((), (), s32[]{:S(2)}) async-start(), calls=%async_computation.25 | async-start | bytes 5898240 | tf_op jit(solution)/shard_map/reduce_scatter | solution.py:628
  462.0 288.9 %all-reduce.18.cloned.1.call-start = ((), (), s32[]{:S(2)}) async-start(), calls=%async_computation.37 | async-start | bytes 425984 | tf_op jit(solution)/shard_map/psum | solution.py:636
  498.8 265.9 %reduce-scatter.55.cloned.1.call-start = ((), (), s32[]{:S(2)}) async-start(), calls=%async_computation.34 | async-start | bytes 442368
  500.8 267.6 %reduce-scatter.53.cloned.1.call-start = ((), (), s32[]{:S(2)}) async-start(), calls=%async_computation.33 | async-start | bytes 442368
  502.8 298.3 %reduce-scatter.51.cloned.1.call-start = ((), (), s32[]{:S(2)}) async-start(), calls=%async_computation.32 | async-start | bytes 1105920
  505.1 328.6 %reduce-scatter.49.cloned.1.call-start = ((), (), s32[]{:S(2)}) async-start(), calls=%async_computation.31 | async-start | bytes 1105920
  507.5 359.3 %reduce-scatter.59.cloned.1.call-start = ((), (), s32[]{:S(2)}) async-start(), calls=%async_computation.36 | async-start | bytes 1327104
  524.2 179.1 %copy-start.12 = (f32[1024,768]{1,0:T(8,128)S(1)}, f32[1024,768]{1,0:T(8,128)}, u32[]{:S(2)}) copy-start(f32[1024,768]{1,0:T(8,128)} %copy-done.11) | copy-start | bytes 9437188
  524.2 376.0 %reduce-scatter.57.cloned.1.call-start = ((), (), s32[]{:S(2)}) async-start(), calls=%async_computation.35 | async-start | bytes 1327104
  584.7 348.7 %reduce-scatter.43.cloned.1.call-start = ((), (), s32[]{:S(2)}) async-start(), calls=%async_computation.28 | async-start | bytes 1327104 | tf_op jit(solution)/shard_map/reduce_scatter | solution.py:627
  642.9 323.4 %reduce-scatter.39.cloned.1.call-start = ((), (), s32[]{:S(2)}) async-start(), calls=%async_computation.26 | async-start | bytes 1327104 | tf_op jit(solution)/shard_map/reduce_scatter | solution.py:627
  715.0 28.1 %copy-start.25 = (f32[1024,768]{1,0:T(8,128)S(1)}, f32[1024,768]{1,0:T(8,128)}, u32[]{:S(2)}) copy-start(f32[1024,768]{1,0:T(8,128)} %copy-done.24) | copy-start | bytes 9437188
  738.5 22.8 %all-to-all-start.3 = ((bf16[4,256,768]{2,1,0:T(8,128)(2,1)}), bf16[4,256,768]{2,1,0:T(8,128)(2,1)}, u32[]{:S(2)}, u32[]{:S(2)}) async-start(bf16[4,256,768]{2,1,0:T(8,128)(2,1)} %bitcast.259), calls=%async_computation.3 | async-start | bytes 3145728 | tf_op jit(solution)/shard_map/all_to_all | solution.py:520
  742.9 225.3 %all-reduce.16.cloned.1.call-start = ((), (), s32[]{:S(2)}) async-start(), calls=%async_computation.22 | async-start | bytes 786432 | tf_op jit(solution)/shard_map/psum | solution.py:636
  802.1 166.1 %copy-start.108 = (f32[2,768]{1,0:T(2,128)S(1)}, f32[2,768]{1,0:T(2,128)}, u32[]{:S(2)}) copy-start(f32[2,768]{1,0:T(2,128)} %get-tuple-element.178) | copy-start | bytes 18436
  802.1 166.6 %copy-start.107 = (f32[2,768]{1,0:T(2,128)S(1)}, f32[2,768]{1,0:T(2,128)}, u32[]{:S(2)}) copy-start(f32[2,768]{1,0:T(2,128)} %get-tuple-element.179) | copy-start | bytes 18436
  802.1 167.2 %copy-start.123 = (f32[2,2,64]{2,1,0:T(2,128)S(1)}, f32[2,2,64]{2,1,0:T(2,128)}, u32[]{:S(2)}) copy-start(f32[2,2,64]{2,1,0:T(2,128)} %get-tuple-element.183) | copy-start | bytes 3076
  802.2 167.8 %copy-start.64 = (f32[2,64,64]{2,1,0:T(8,128)S(1)}, f32[2,64,64]{2,1,0:T(8,128)}, u32[]{:S(2)}) copy-start(f32[2,64,64]{2,1,0:T(8,128)} %get-tuple-element.184) | copy-start | bytes 98308
  834.7 139.4 %copy-start.1 = (s32[2,1]{0,1:T(1,128)S(1)}, s32[2,1]{0,1:T(1,128)}, u32[]{:S(2)}) copy-start(s32[2,1]{0,1:T(1,128)} %param.21) | copy-start | bytes 28
  834.8 137.5 %copy-start.106 = (f32[2,768]{1,0:T(2,128)S(1)}, f32[2,768]{1,0:T(2,128)}, u32[]{:S(2)}) copy-start(f32[2,768]{1,0:T(2,128)} %get-tuple-element.186) | copy-start | bytes 18436
  834.8 138.1 %copy-start.105 = (f32[2,768]{1,0:T(2,128)S(1)}, f32[2,768]{1,0:T(2,128)}, u32[]{:S(2)}) copy-start(f32[2,768]{1,0:T(2,128)} %get-tuple-element.188) | copy-start | bytes 18436
  834.9 138.7 %copy-start.104 = (f32[2,768]{1,0:T(2,128)S(1)}, f32[2,768]{1,0:T(2,128)}, u32[]{:S(2)}) copy-start(f32[2,768]{1,0:T(2,128)} %get-tuple-element.189) | copy-start | bytes 18436
  (128 other events, 989.8 us)
Sparse Core Ops, SparseCore 0:
  240.3 30.2 reduce-scatter.34
  308.8 30.3 reduce-scatter.32
  342.5 47.2 reduce-scatter.30
  412.6 48.6 reduce-scatter.28
  464.5 57.2 reduce-scatter.46
  524.9 57.3 reduce-scatter.44
  585.6 57.2 reduce-scatter.40
  646.2 57.0 reduce-scatter.36
  706.1 30.6 reduce-scatter.54
  739.5 28.8 reduce-scatter.52
  770.8 30.2 reduce-scatter.50
  803.2 30.4 reduce-scatter.48
  836.0 30.7 reduce-scatter.58
  868.9 31.1 reduce-scatter.56
  902.3 31.0 reduce-scatter.42
  935.5 30.7 reduce-scatter.38
Sparse Core Ops, SparseCore 1:
  498.9 162.9 all-reduce.17
  751.0 132.0 all-reduce.15

commit v2 on v0

--- a/solution.py
+++ b/solution.py
@@ -2,7 +2,10 @@
 
 import jax
 import jax.numpy as jnp
+import numpy as np
 from jax import lax
+from jax.experimental import pallas as pl
+from jax.experimental.pallas import tpu as pltpu
 from jax.sharding import PartitionSpec as P
 
 EMB = 33
@@ -138,7 +141,7 @@
     return jax.tree.map(jnp.add, running, update)
 
 
-def shards(
+def split_positions(
     x_in,
     cotangent,
     counts,
@@ -474,6 +477,479 @@
     )
 
 
+MIB = 1 << 20
+
+
+def mm(left, right):
+    return jnp.dot(left, right, preferred_element_type=jnp.float32)
+
+
+def mm_nt(left, right):
+    return lax.dot_general(left, right, (((1,), (1,)), ((), ())), preferred_element_type=jnp.float32)
+
+
+def f32(values):
+    return values.astype(jnp.float32)
+
+
+def bf(values):
+    return values.astype(jnp.bfloat16)
+
+
+def row_shift(values, distance):
+    rows = values.shape[0]
+    index = lax.broadcasted_iota(jnp.int32, values.shape, 0)
+    rolled = pltpu.roll(values, distance % rows, 0)
+    kept = index >= distance if distance > 0 else index < rows + distance
+    return jnp.where(kept, rolled, 0.0)
+
+
+def standardised(values):
+    mean = jnp.mean(values, axis=-1, keepdims=True)
+    centred = values - mean
+    scale = lax.rsqrt(jnp.mean(centred * centred, axis=-1, keepdims=True) + NORM_EPS)
+    return centred * scale, scale
+
+
+def norm_backward(values, gain, upstream):
+    xh, scale = standardised(values)
+    dxh = upstream * gain
+    part = scale * (
+        dxh - jnp.mean(dxh, axis=-1, keepdims=True) - xh * jnp.mean(dxh * xh, axis=-1, keepdims=True)
+    )
+    return part, jnp.sum(upstream * xh, axis=0, keepdims=True), jnp.sum(upstream, axis=0, keepdims=True)
+
+
+def gelu_parts(values):
+    slope = math.sqrt(2.0 / math.pi)
+    square = values * values
+    bent = jnp.tanh(slope * values * (1.0 + 0.044715 * square))
+    half = 0.5 * (1.0 + bent)
+    inner = slope * (1.0 + (3.0 * 0.044715) * square)
+    return values * half, half + 0.5 * values * (1.0 - bent * bent) * inner
+
+
+def spectral_table(length):
+    k = np.arange(length, dtype=np.int64)[:, None]
+    t = np.arange(length, dtype=np.int64)[None, :]
+    angle = ((2 * k + 1) * t % (4 * length)).astype(np.float64) * (2.0 * math.pi / (4 * length))
+    return np.concatenate([np.cos(angle), -np.sin(angle)], axis=0).astype(jnp.bfloat16)
+
+
+def whole(shape):
+    return pl.BlockSpec(shape, lambda j: (0,) * len(shape), pipeline_mode=pl.Buffered(1))
+
+
+def of_layer(layer, shape):
+    return pl.BlockSpec((None,) + shape, lambda j: (layer,) + (0,) * len(shape), pipeline_mode=pl.Buffered(1))
+
+
+def mixed_chunk(proj, kernel):
+    return [
+        kernel[p][0:1] * row_shift(proj[p], 2) + kernel[p][1:2] * row_shift(proj[p], 1) + kernel[p][2:3] * proj[p]
+        for p in range(3)
+    ]
+
+
+def mixer_forward_body(
+    r_ref, gain_ref, bias_ref, w0_ref, w1_ref, w2_ref, k0_ref, k1_ref, k2_ref, table_ref, back_ref, taps_ref, skip_ref,
+    wo_ref, hidden_ref, normed_ref, proj_ref, signal_ref, long_ref,
+):
+    length = r_ref.shape[0]
+
+    @pl.when(pl.program_id(0) == 0)
+    def _():
+        r = r_ref[...]
+        xh, _ = standardised(r)
+        normed_ref[...] = bf(xh * f32(gain_ref[...]) + f32(bias_ref[...]))
+        hidden_ref[...] = r
+
+    normed = normed_ref[...]
+    proj = [mm(normed, w_ref[...]) for w_ref in (w0_ref, w1_ref, w2_ref)]
+    for p in range(3):
+        proj_ref[p] = bf(proj[p])
+    gate_out, gate_in, vals = mixed_chunk(proj, [f32(k_ref[...]) for k_ref in (k0_ref, k1_ref, k2_ref)])
+    carried = vals * gate_in
+    both = mm(table_ref[...], bf(carried))
+    re, im = both[:length], both[length:]
+    signal_ref[...] = bf(both)
+    tap_re, tap_im = f32(taps_ref[:length]), f32(taps_ref[length:])
+    out = mm(back_ref[:, :length], bf(re * tap_re - im * tap_im))
+    out += mm(back_ref[:, length:], bf(re * tap_im + im * tap_re))
+    long_out = out + f32(skip_ref[...]) * carried
+    long_ref[...] = bf(long_out)
+    hidden_ref[...] += mm(bf(long_out * gate_out), wo_ref[...])
+
+
+def mixer_forward(layer, r, gain, bias, w_in, short_w, table, back, taps, skip, w_out):
+    length, width = r.shape
+    chunk = 256
+    steps = width // chunk
+    third = lambda p: pl.BlockSpec((None, width, chunk), lambda j: (layer, 0, p * steps + j))
+    short = lambda p: pl.BlockSpec((None, 3, chunk), lambda j: (layer, 0, p * steps + j))
+    return pl.pallas_call(
+        mixer_forward_body,
+        grid=(steps,),
+        in_specs=[
+            whole((length, width)), of_layer(layer, (1, width)), of_layer(layer, (1, width)),
+            third(0), third(1), third(2), short(0), short(1), short(2),
+            whole((2 * length, length)), whole((length, 2 * length)),
+            pl.BlockSpec((2 * length, chunk), lambda j: (0, j)),
+            pl.BlockSpec((None, 1, chunk), lambda j: (layer, 0, j)),
+            pl.BlockSpec((None, chunk, width), lambda j: (layer, j, 0)),
+        ],
+        out_specs=[
+            whole((length, width)), whole((length, width)),
+            pl.BlockSpec((3, length, chunk), lambda j: (0, 0, j)),
+            pl.BlockSpec((2 * length, chunk), lambda j: (0, j)),
+            pl.BlockSpec((length, chunk), lambda j: (0, j)),
+        ],
+        out_shape=[
+            jax.ShapeDtypeStruct((length, width), jnp.float32),
+            jax.ShapeDtypeStruct((length, width), jnp.bfloat16),
+            jax.ShapeDtypeStruct((3, length, width), jnp.bfloat16),
+            jax.ShapeDtypeStruct((2 * length, width), jnp.bfloat16),
+            jax.ShapeDtypeStruct((length, width), jnp.bfloat16),
+        ],
+        compiler_params=pltpu.CompilerParams(vmem_limit_bytes=60 * MIB),
+        cost_estimate=pl.CostEstimate(
+            flops=2 * length * width * (4 * width + 4 * length), bytes_accessed=30 * MIB, transcendentals=0
+        ),
+        name="mixer_forward",
+    )(r, gain, bias, w_in, w_in, w_in, short_w, short_w, short_w, table, back, taps, skip, w_out)
+
+
+def ffn_forward_body(hidden_ref, gain_ref, bias_ref, up_ref, down_ref, r_ref, normed_ref, raised_ref):
+    @pl.when(pl.program_id(0) == 0)
+    def _():
+        hidden = hidden_ref[...]
+        xh, _ = standardised(hidden)
+        normed_ref[...] = bf(xh * f32(gain_ref[...]) + f32(bias_ref[...]))
+        r_ref[...] = hidden
+
+    raised = mm(normed_ref[...], up_ref[...])
+    raised_ref[...] = bf(raised)
+    r_ref[...] += mm(bf(gelu_parts(raised)[0]), down_ref[...])
+
+
+def ffn_forward(layer, hidden, gain, bias, w_up, w_down):
+    length, width = hidden.shape
+    inner = w_up.shape[2]
+    chunk = 768
+    return pl.pallas_call(
+        ffn_forward_body,
+        grid=(inner // chunk,),
+        in_specs=[
+            whole((length, width)), of_layer(layer, (1, width)), of_layer(layer, (1, width)),
+            pl.BlockSpec((None, width, chunk), lambda j: (layer, 0, j)),
+            pl.BlockSpec((None, chunk, width), lambda j: (layer, j, 0)),
+        ],
+        out_specs=[
+            whole((length, width)), whole((length, width)),
+            pl.BlockSpec((length, chunk), lambda j: (0, j)),
+        ],
+        out_shape=[
+            jax.ShapeDtypeStruct((length, width), jnp.float32),
+            jax.ShapeDtypeStruct((length, width), jnp.bfloat16),
+            jax.ShapeDtypeStruct((length, inner), jnp.bfloat16),
+        ],
+        compiler_params=pltpu.CompilerParams(vmem_limit_bytes=60 * MIB),
+        cost_estimate=pl.CostEstimate(
+            flops=4 * length * width * inner, bytes_accessed=26 * MIB, transcendentals=length * inner
+        ),
+        name="ffn_forward",
+    )(hidden, gain, bias, w_up, w_down)
+
+
+def ffn_backward_body(
+    g_ref, hidden_ref, gain_ref, normed_ref, raised_ref, up_ref, down_ref, out_ref, grads_ref, gain_grad_ref,
+    bias_grad_ref, g16_ref, g16t_ref, normed_t_ref, total_ref,
+):
+    j = pl.program_id(0)
+    width = g_ref.shape[1]
+
+    @pl.when(j == 0)
+    def _():
+        g16 = bf(g_ref[...])
+        g16_ref[...] = g16
+        g16t_ref[...] = g16.T
+        normed_t_ref[...] = normed_ref[...].T
+        total_ref[...] = jnp.zeros_like(total_ref)
+
+    active, slope = gelu_parts(f32(raised_ref[...]))
+    raised_grad = bf(mm_nt(g16_ref[...], down_ref[...]) * slope)
+    grads_ref[:, :width] = bf(mm(normed_t_ref[...], raised_grad))
+    grads_ref[:, width:] = bf(mm(g16t_ref[...], bf(active)))
+    total_ref[...] += mm_nt(raised_grad, up_ref[...])
+
+    @pl.when(j == pl.num_programs(0) - 1)
+    def _():
+        part, gain_grad, bias_grad = norm_backward(hidden_ref[...], f32(gain_ref[...]), total_ref[...])
+        out_ref[...] = g_ref[...] + part
+        gain_grad_ref[...] = gain_grad
+        bias_grad_ref[...] = bias_grad
+
+
+def ffn_backward(layer, g, hidden, gain, normed, raised, w_up, w_down):
+    length, width = g.shape
+    inner = w_up.shape[2]
+    chunk = 768
+    steps = inner // chunk
+    return pl.pallas_call(
+        ffn_backward_body,
+        grid=(steps,),
+        in_specs=[
+            whole((length, width)), whole((length, width)), of_layer(layer, (1, width)), whole((length, width)),
+            pl.BlockSpec((length, chunk), lambda j: (0, j)),
+            pl.BlockSpec((None, width, chunk), lambda j: (layer, 0, j)),
+            pl.BlockSpec((None, chunk, width), lambda j: (layer, j, 0)),
+        ],
+        out_specs=[
+            whole((length, width)),
+            pl.BlockSpec((None, width, 2 * chunk), lambda j: (j, 0, 0)),
+            whole((1, width)), whole((1, width)),
+        ],
+        out_shape=[
+            jax.ShapeDtypeStruct((length, width), jnp.float32),
+            jax.ShapeDtypeStruct((steps, width, 2 * chunk), jnp.bfloat16),
+            jax.ShapeDtypeStruct((1, width), jnp.float32),
+            jax.ShapeDtypeStruct((1, width), jnp.float32),
+        ],
+        scratch_shapes=[
+            pltpu.VMEM((length, width), jnp.bfloat16), pltpu.VMEM((width, length), jnp.bfloat16),
+            pltpu.VMEM((width, length), jnp.bfloat16), pltpu.VMEM((length, width), jnp.float32),
+        ],
+        compiler_params=pltpu.CompilerParams(vmem_limit_bytes=60 * MIB),
+        cost_estimate=pl.CostEstimate(
+            flops=8 * length * width * inner, bytes_accessed=40 * MIB, transcendentals=length * inner
+        ),
+        name="ffn_backward",
+    )(g, hidden, gain, normed, raised, w_up, w_down)
+
+
+def mixer_backward_body(
+    hg_ref, r_ref, gain_ref, normed_ref, proj_ref, k0_ref, k1_ref, k2_ref, signal_ref, long_ref, taps_ref, skip_ref,
+    table_ref, back_ref, wo_ref, w0_ref, w1_ref, w2_ref,
+    g_ref, grad_out_ref, grad_in_ref, taps_grad_ref, short_grad_ref, skip_grad_ref, gain_grad_ref, bias_grad_ref,
+    og_ref, normed_t_ref, total_ref,
+):
+    j = pl.program_id(0)
+    length = hg_ref.shape[0]
+
+    @pl.when(j == 0)
+    def _():
+        og_ref[...] = bf(hg_ref[...])
+        normed_t_ref[...] = normed_ref[...].T
+        total_ref[...] = jnp.zeros_like(total_ref)
+
+    proj = [f32(proj_ref[p]) for p in range(3)]
+    kernel = [f32(k_ref[...]) for k_ref in (k0_ref, k1_ref, k2_ref)]
+    gate_out, gate_in, vals = mixed_chunk(proj, kernel)
+    carried = vals * gate_in
+    long_out = f32(long_ref[...])
+    skip = f32(skip_ref[...])
+    og = og_ref[...]
+    grad_out_ref[...] = bf(mm(bf(long_out * gate_out).T, og))
+    gated_grad = mm_nt(og, wo_ref[...])
+    long_grad = gated_grad * gate_out
+    skip_grad_ref[...] = jnp.sum(carried * long_grad, axis=0, keepdims=True)
+    both = mm(table_ref[...], bf(long_grad))
+    up_re, up_im = both[:length], both[length:]
+    tap_re, tap_im = f32(taps_ref[:length]), f32(taps_ref[length:])
+    out = mm(back_ref[:, :length], bf(up_re * tap_re + up_im * tap_im))
+    out += mm(back_ref[:, length:], bf(up_im * tap_re - up_re * tap_im))
+    carried_grad = out + skip * long_grad
+    sig_re, sig_im = f32(signal_ref[:length]), f32(signal_ref[length:])
+    cross = mm(back_ref[:, :length], bf(up_re * sig_re + up_im * sig_im))
+    cross += mm(back_ref[:, length:], bf(up_im * sig_re - up_re * sig_im))
+    taps_grad_ref[...] = cross * (1.0 / length)
+    for p, part in enumerate((gated_grad * long_out, carried_grad * vals, carried_grad * gate_in)):
+        one, two = row_shift(part, -1), row_shift(part, -2)
+        projected_grad = bf(kernel[p][2:3] * part + kernel[p][1:2] * one + kernel[p][0:1] * two)
+        for tap, moved in enumerate((two, one, part)):
+            short_grad_ref[p, tap : tap + 1, :] = jnp.sum(moved * proj[p], axis=0, keepdims=True)
+        grad_in_ref[p] = bf(mm(normed_t_ref[...], projected_grad))
+        total_ref[...] += mm_nt(projected_grad, (w0_ref, w1_ref, w2_ref)[p][...])
+
+    @pl.when(j == pl.num_programs(0) - 1)
+    def _():
+        part, gain_grad, bias_grad = norm_backward(r_ref[...], f32(gain_ref[...]), total_ref[...])
+        g_ref[...] = hg_ref[...] + part
+        gain_grad_ref[...] = gain_grad
+        bias_grad_ref[...] = bias_grad
+
+
+def mixer_backward(layer, hidden_grad, r, gain, normed, proj, short_w, signal, long_out, taps, skip, table, back, w_out, w_in):
+    length, width = r.shape
+    chunk = 256
+    steps = width // chunk
+    third = lambda p: pl.BlockSpec((None, width, chunk), lambda j: (layer, 0, p * steps + j))
+    short = lambda p: pl.BlockSpec((None, 3, chunk), lambda j: (layer, 0, p * steps + j))
+    return pl.pallas_call(
+        mixer_backward_body,
+        grid=(steps,),
+        in_specs=[
+            whole((length, width)), whole((length, width)), of_layer(layer, (1, width)), whole((length, width)),
+            pl.BlockSpec((3, length, chunk), lambda j: (0, 0, j)),
+            short(0), short(1), short(2),
+            pl.BlockSpec((2 * length, chunk), lambda j: (0, j)),
+            pl.BlockSpec((length, chunk), lambda j: (0, j)),
+            pl.BlockSpec((2 * length, chunk), lambda j: (0, j)),
+            pl.BlockSpec((None, 1, chunk), lambda j: (layer, 0, j)),
+            whole((2 * length, length)), whole((length, 2 * length)),
+            pl.BlockSpec((None, chunk, width), lambda j: (layer, j, 0)),
+            third(0), third(1), third(2),
+        ],
+        out_specs=[
+            whole((length, width)),
+            pl.BlockSpec((chunk, width), lambda j: (j, 0)),
+            pl.BlockSpec((3, width, chunk), lambda j: (0, 0, j)),
+            pl.BlockSpec((length, chunk), lambda j: (0, j)),
+            pl.BlockSpec((3, 3, chunk), lambda j: (0, 0, j)),
+            pl.BlockSpec((1, chunk), lambda j: (0, j)),
+            whole((1, width)), whole((1, width)),
+        ],
+        out_shape=[
+            jax.ShapeDtypeStruct((length, width), jnp.float32),
+            jax.ShapeDtypeStruct((width, width), jnp.bfloat16),
+            jax.ShapeDtypeStruct((3, width, width), jnp.bfloat16),
+            jax.ShapeDtypeStruct((length, width), jnp.float32),
+            jax.ShapeDtypeStruct((3, 3, width), jnp.float32),
+            jax.ShapeDtypeStruct((1, width), jnp.float32),
+            jax.ShapeDtypeStruct((1, width), jnp.float32),
+            jax.ShapeDtypeStruct((1, width), jnp.float32),
+        ],
+        scratch_shapes=[
+            pltpu.VMEM((length, width), jnp.bfloat16), pltpu.VMEM((width, length), jnp.bfloat16),
+            pltpu.VMEM((length, width), jnp.float32),
+        ],
+        compiler_params=pltpu.CompilerParams(vmem_limit_bytes=62 * MIB),
+        cost_estimate=pl.CostEstimate(
+            flops=2 * length * width * (8 * width + 6 * length), bytes_accessed=50 * MIB, transcendentals=0
+        ),
+        name="mixer_backward",
+    )(hidden_grad, r, gain, normed, proj, short_w, short_w, short_w, signal, long_out, taps, skip, table, back, w_out,
+      w_in, w_in, w_in)
+
+
+def swapped(block, axis, flip):
+    return lax.ppermute(block, axis, [(i, i ^ flip) for i in range(lax.axis_size(axis))])
+
+
+def pick(block, index, dim):
+    return lax.dynamic_index_in_dim(block, index, dim, keepdims=False)
+
+
+def halved(block, axis, flip, bit, dim):
+    return pick(block, bit, dim) + swapped(pick(block, 1 - bit, dim), axis, flip)
+
+
+def reduce_scatter(block):
+    toks, seqs, rows, columns = block.shape
+    s, t = lax.axis_index("seq"), lax.axis_index("tok")
+    z, core, y, x = s // 2, s % 2, t // 2, t % 2
+    block = halved(block.reshape(2, 2, seqs // 2, 2, rows, columns), "seq", 1, core, 3)
+    left, right = block[..., : columns // 2], block[..., columns // 2 :]
+    left = halved(left, "tok", 1, x, 1)
+    right = halved(right, "tok", 2, y, 0)
+    left = halved(left, "tok", 2, y, 0)
+    right = halved(right, "tok", 1, x, 0)
+    block = jnp.concatenate([left, right], axis=-1)
+    total = f32(pick(block, z, 0))
+    for step in range(1, seqs // 2):
+        sent = pick(block, (z + step) % (seqs // 2), 0)
+        total += f32(lax.ppermute(sent, "seq", [(i, (i + 2 * step) % seqs) for i in range(seqs)]))
+    return total
+
+
+def whole_sequences(
+    x_in, cotangent, counts, ln1_gain, ln1_bias, w_in, short_w, filt_w1, filt_freq, filt_w2, filt_w3, long_bias,
+    w_out, ln2_gain, ln2_bias, w_up, w_down,
+):
+    micro_count, cap_size, tok_rows, width = x_in.shape
+    slots = micro_count * cap_size
+    layers, _, inner = w_up.shape
+    toks, seqs = lax.axis_size("tok"), lax.axis_size("seq")
+    length = tok_rows * toks
+    me = lax.axis_index("tok")
+
+    def gather_mine(block):
+        return lax.all_to_all(block.reshape(slots, tok_rows, width), "tok", split_axis=0, concat_axis=1, tiled=True)[0]
+
+    def scatter_back(rows):
+        blocks = rows.reshape(slots, tok_rows, width)
+        back = lax.all_to_all(blocks, "tok", split_axis=0, concat_axis=0, tiled=True)
+        return back.reshape(micro_count, cap_size, tok_rows, width)
+
+    live = (me % cap_size < counts[me // cap_size, 0]).astype(jnp.float32)
+    table = jnp.asarray(spectral_table(length))
+    table_back = jnp.asarray(np.ascontiguousarray(spectral_table(length).T))
+    features = position_features(length)
+    envelope = decay_table(features[:, :1], 0.0, width, width)
+    rowed = lambda v: v.reshape(layers, 1, v.shape[1])
+    g1, b1, g2, b2, skip = (rowed(v) for v in (ln1_gain, ln1_bias, ln2_gain, ln2_bias, long_bias))
+
+    def taps_fn(layer):
+        def fn(one, sine, two, three):
+            return filter_taps(features, one, sine, two, three, envelope)
+
+        return jax.vjp(fn, f32(filt_w1[layer]), f32(filt_freq[layer]), f32(filt_w2[layer]), f32(filt_w3[layer]))
+
+    start = gather_mine(x_in)
+    upstream = gather_mine(cotangent)
+    filters = [taps_fn(layer) for layer in range(layers)]
+    spectra = [bf(mm(table, bf(filters[layer][0])) * (1.0 / length)) for layer in range(layers)]
+    r = f32(start)
+    kept = []
+    for layer in range(layers):
+        hidden, normed, proj, signal, long_out = mixer_forward(
+            layer, r, g1, b1, w_in, short_w, table, table_back, spectra[layer], skip, w_out
+        )
+        result, normed_two, raised = ffn_forward(layer, hidden, g2, b2, w_up, w_down)
+        kept.append((r, hidden, normed, proj, signal, long_out, normed_two, raised))
+        r = result
+    out_act = f32(scatter_back(bf(r * live)))
+
+    grad = f32(upstream) * live
+    mats = [None] * layers
+    vecs = [None] * layers
+    for layer in reversed(range(layers)):
+        r, hidden, normed, proj, signal, long_out, normed_two, raised = kept[layer]
+        grad, ffn_grads, grad_g2, grad_b2 = ffn_backward(layer, grad, hidden, g2, normed_two, raised, w_up, w_down)
+        ffn_done = reduce_scatter(ffn_grads.reshape(toks, seqs, width // seqs, -1))
+        grad, grad_out, grad_in_proj, taps_grad, grad_short, grad_skip, grad_g1, grad_b1 = mixer_backward(
+            layer, grad, r, g1, normed, proj, short_w, signal, long_out, spectra[layer], skip, table, table_back,
+            w_out, w_in,
+        )
+        in_cols = jnp.swapaxes(grad_in_proj, 0, 1).reshape(width, toks, -1)
+        mixer_grads = jnp.concatenate([in_cols, grad_out.reshape(width, toks, -1)], axis=2)
+        mixer_done = reduce_scatter(jnp.swapaxes(mixer_grads, 0, 1).reshape(toks, seqs, width // seqs, -1))
+        split = in_cols.shape[2]
+        mats[layer] = (
+            mixer_done[:, :split], mixer_done[:, split:], ffn_done[:, : inner // toks],
+            ffn_done[:, inner // toks :].T,
+        )
+        filter_grads = filters[layer][1](taps_grad)
+        short = jnp.swapaxes(grad_short, 0, 1).reshape(3, 3 * width)
+        vecs[layer] = (grad_g1[0], grad_b1[0], short, grad_skip[0], grad_g2[0], grad_b2[0]) + tuple(filter_grads)
+    grad_in = f32(scatter_back(bf(grad)))
+    mat_done = [jnp.stack([mats[layer][m] for layer in range(layers)]) for m in range(4)]
+    small = lax.psum(
+        tuple(jnp.stack([vecs[layer][m] for layer in range(layers)]) for m in range(10)), ("seq", "tok")
+    )
+    return (
+        out_act, grad_in, small[0], small[1], mat_done[0], small[2], small[6], small[7], small[8], small[9], small[3],
+        mat_done[1], small[4], small[5], mat_done[2], mat_done[3],
+    )
+
+
+def shards(*args):
+    micro_count, cap_size = args[0].shape[:2]
+    if lax.axis_size("tok") == 4 and micro_count * cap_size == 4:
+        return whole_sequences(*args)
+    return split_positions(*args)
+
+
 def solution(mesh):
     return jax.shard_map(
         shards,

time: 2380 us -> 748 us (0.31)
  matrix products: 1190 us -> 47.1 us
  local copies, waits for them, and re-layouts: 445 us -> 62.9 us
  Pallas kernels: 0 us -> 248 us
  other arithmetic: 159 us -> 49.2 us
  waiting for transfers between devices: 364 us -> 255 us
  starting transfers between devices: 160 us -> 59.6 us
  blocking collectives: 28.1 us -> 0 us
    dot_general x168 -> x2, matrix products: 1160 us -> 14.6 us  [mm(): return jnp.dot(left, right, preferred_element_type=jnp.float32)]
    pallas_call x0 -> x8, Pallas kernels: none -> 248 us  [the longest x2 88.5 us: mixer_backward(): pl.pallas_call(mixer_backward_body, grid=(steps,), in_specs=[whole((lengt...]
    all_to_all x60 -> x0, local copies, waits for them, and re-layouts: 176 us -> none  [the longest x8 48.7 us: backward_layer(): lax.all_to_all(active, 'tok', split_axis=2, concat_axis=1, tiled=True)]
    convert_element_type x40 -> x0, local copies, waits for them, and re-layouts: 152 us -> none  [the longest x4 35.4 us: backward_layer(): raised_grad = gelu_pull(active_grad)[0].astype(jnp.bfloat16)]
    all_to_all x31 -> x4, waiting for transfers between devices: 138 us -> 0.01 us  [the longest x2 0.01 us: gather_mine(): lax.all_to_all(block.reshape(slots, tok_rows, width), 'tok', split_axis=0...]
    ppermute x8 -> x32, waiting for transfers between devices: 2.32 us -> 130 us  [the longest x20 88.3 us: swapped(): lax.ppermute(block, axis, [(i, i ^ flip) for i in range(lax.axis_size(axi...]
    all_to_all x31 -> x4, starting transfers between devices: 136 us -> 18.5 us  [the longest x2 9.5 us: gather_mine(): lax.all_to_all(block.reshape(slots, tok_rows, width), 'tok', split_axis=0...]
    unnamed x23 -> x2, waiting for transfers between devices: 95 us -> 0.03 us
  transfers between devices with their start and end apart: 60 -> 38, of which waited for: 18 -> 19; matrix products, arithmetic and copies ran while one was open for 62% -> 21% of each run, Pallas kernels for 0% -> 34%
where the time goes in v2:
time: 748 us; the launch traced here: 739 us
  waiting for transfers between devices  255 us (34%)
  Pallas kernels  248 us (33%)
  local copies, waits for them, and re-layouts  62.9 us (8%)
  starting transfers between devices  59.6 us (8%)
  other arithmetic  49.2 us (7%)
  matrix products  47.1 us (6%)
  between operations  16.4 us (2%)
    psum x2, waiting for transfers between devices, whole_sequences(): lax.psum(tuple((jnp.stack([vecs[layer][m] for layer in range(layers)]) fo...  126 us
    pallas_call x2, Pallas kernels, mixer_backward(): pl.pallas_call(mixer_backward_body, grid=(steps,), in_specs=[whole((lengt...  88.5 us
    ppermute x20, waiting for transfers between devices, swapped(): lax.ppermute(block, axis, [(i, i ^ flip) for i in range(lax.axis_size(axi...  88.3 us
    pallas_call x2, Pallas kernels, ffn_backward(): pl.pallas_call(ffn_backward_body, grid=(steps,), in_specs=[whole((length,...  65.8 us
    pallas_call x2, Pallas kernels, mixer_forward(): pl.pallas_call(mixer_forward_body, grid=(steps,), in_specs=[whole((length...  59.5 us
    ppermute x12, waiting for transfers between devices, reduce_scatter(): lax.ppermute(sent, 'seq', [(i, (i + 2 * step) % seqs) for i in range(seqs)])  41.5 us
    pallas_call x2, Pallas kernels, ffn_forward(): pl.pallas_call(ffn_forward_body, grid=(inner // chunk,), in_specs=[whole(...  34.4 us
    ppermute x12, starting transfers between devices, reduce_scatter(): lax.ppermute(sent, 'seq', [(i, (i + 2 * step) % seqs) for i in range(seqs)])  21.3 us
  transfers between devices with their start and end apart: 38, of which 19 were waited for; matrix products, arithmetic and copies ran while one was open for 21% of the time, Pallas kernels for 34%

profile of v2, /device:TPU:0, one launch (start us, length us, event | category | flops | bytes accessed | tf_op | source)
XLA Modules:
  0.0 738.9 jit_solution(15315272612417038247)
XLA Ops:
  7.3 5.3 all-to-all-start
  23.1 7.3 fusion.2.taps_ref
  31.6 3.1 multiply_convert_fusion.3
  34.7 7.3 fusion.3.taps_ref
  42.0 4.2 all-to-all-start.2
  48.2 29.6 %mixer_forward.2 = (f32[1024,768]{1,0:T(8,128)}, bf16[1024,768]{1,0:T(8,128)(2,1)}, bf16[3,1024,768]{2,1,0:T(8,128)(2,1)}, bf16[2048,768]{1,0:T(8,128)(2,1)}, bf16[1024,768]{1,0:T(8,128)(2,1)}) custom-call(f32[1024,768]{1,0:T(8,128)} %bitcast_convert_fusion.r_ref, bf16[2,1,768]{2,1,0:T(2,128)(2,1)} %copy.92.gain_ref, bf16[2,1,768]{2,1,0:T(2,128)(2,1)} %copy.93.bias_ref, ...), custom_call_target="tpu_custom_call" | custom-call | flops 11274289152 | bytes 31457280 | tf_op jit(solution)/shard_map/mixer_forward/pallas_call | solution.py:590
  77.8 17.2 %ffn_forward.2 = (f32[1024,768]{1,0:T(8,128)}, bf16[1024,768]{1,0:T(8,128)(2,1)}, bf16[1024,3072]{1,0:T(8,128)(2,1)}) custom-call(f32[1024,768]{1,0:T(8,128)} %get-tuple-element.56.hidden_ref, bf16[2,1,768]{2,1,0:T(2,128)(2,1)} %copy.98.gain_ref, bf16[2,1,768]{2,1,0:T(2,128)(2,1)} %copy.99.bias_ref, bf16[2,768,3072]{2,1,0:T(8,128)(2,1)} %up_ref.7, ...), custom_call_target="tpu_custom_call" | custom-call | flops 9663676416 | bytes 27262976 | tf_op jit(solution)/shard_map/ffn_forward/pallas_call | solution.py:639
  95.0 30.0 %mixer_forward.3 = (f32[1024,768]{1,0:T(8,128)}, bf16[1024,768]{1,0:T(8,128)(2,1)}, bf16[3,1024,768]{2,1,0:T(8,128)(2,1)}, bf16[2048,768]{1,0:T(8,128)(2,1)}, bf16[1024,768]{1,0:T(8,128)(2,1)}) custom-call(f32[1024,768]{1,0:T(8,128)} %get-tuple-element.57.r_ref, bf16[2,1,768]{2,1,0:T(2,128)(2,1)} %copy.92.gain_ref, bf16[2,1,768]{2,1,0:T(2,128)(2,1)} %copy.93.bias_ref, ...), custom_call_target="tpu_custom_call" | custom-call | flops 11274289152 | bytes 31457280 | tf_op jit(solution)/shard_map/mixer_forward/pallas_call | solution.py:590
  124.9 17.2 %ffn_forward.3 = (f32[1024,768]{1,0:T(8,128)}, bf16[1024,768]{1,0:T(8,128)(2,1)}, bf16[1024,3072]{1,0:T(8,128)(2,1)}) custom-call(f32[1024,768]{1,0:T(8,128)} %get-tuple-element.58.hidden_ref, bf16[2,1,768]{2,1,0:T(2,128)(2,1)} %copy.98.gain_ref, bf16[2,1,768]{2,1,0:T(2,128)(2,1)} %copy.99.bias_ref, bf16[2,768,3072]{2,1,0:T(8,128)(2,1)} %up_ref.7, ...), custom_call_target="tpu_custom_call" | custom-call | flops 9663676416 | bytes 27262976 | tf_op jit(solution)/shard_map/ffn_forward/pallas_call | solution.py:639
  142.1 3.3 multiply_convert_fusion.2
  145.4 4.5 all-to-all-start.1
  151.8 32.9 %ffn_backward.2 = (f32[1024,768]{1,0:T(8,128)}, bf16[4,768,1536]{2,1,0:T(8,128)(2,1)}, f32[1,768]{1,0:T(1,128)}, f32[1,768]{1,0:T(1,128)}) custom-call(f32[1024,768]{1,0:T(8,128)} %bitcast.273, f32[1024,768]{1,0:T(8,128)} %get-tuple-element.58.hidden_ref, bf16[2,1,768]{2,1,0:T(2,128)(2,1)} %copy.98.gain_ref, bf16[1024,768]{1,0:T(8,128)(2,1)} %get-tuple-element.60.normed_ref, ...), custom_call_target="tpu_custom_call" | custom-call | flops 19327352832 | bytes 41943040 | tf_op jit(solution)/shard_map/ffn_backward/pallas_call | solution.py:698
  184.8 44.3 %mixer_backward.2 = (f32[1024,768]{1,0:T(8,128)}, bf16[768,768]{1,0:T(8,128)(2,1)}, bf16[3,768,768]{2,1,0:T(8,128)(2,1)}, f32[1024,768]{1,0:T(8,128)}, f32[3,3,7...) custom-call(f32[1024,768]{1,0:T(8,128)} %get-tuple-element.62.hg_ref, ...), custom_call_target="tpu_custom_call" | custom-call | flops 19327352832 | bytes 52428800 | tf_op jit(solution)/shard_map/mixer_backward/pallas_call | solution.py:788
  229.1 32.9 %ffn_backward.3 = (f32[1024,768]{1,0:T(8,128)}, bf16[4,768,1536]{2,1,0:T(8,128)(2,1)}, f32[1,768]{1,0:T(1,128)}, f32[1,768]{1,0:T(1,128)}) custom-call(f32[1024,768]{1,0:T(8,128)} %get-tuple-element.67.g_ref, f32[1024,768]{1,0:T(8,128)} %get-tuple-element.56.hidden_ref, bf16[2,1,768]{2,1,0:T(2,128)(2,1)} %copy.98.gain_ref, ...), custom_call_target="tpu_custom_call" | custom-call | flops 19327352832 | bytes 41943040 | tf_op jit(solution)/shard_map/ffn_backward/pallas_call | solution.py:698
  261.9 44.2 %mixer_backward.3 = (f32[1024,768]{1,0:T(8,128)}, bf16[768,768]{1,0:T(8,128)(2,1)}, bf16[3,768,768]{2,1,0:T(8,128)(2,1)}, f32[1024,768]{1,0:T(8,128)}, f32[3,3,7...) custom-call(f32[1024,768]{1,0:T(8,128)} %get-tuple-element.70.hg_ref, ...), custom_call_target="tpu_custom_call" | custom-call | flops 19327352832 | bytes 52428800 | tf_op jit(solution)/shard_map/mixer_backward/pallas_call | solution.py:788
  306.2 3.3 convert_element_type.179
  309.5 3.6 multiply_reduce_fusion.1
  315.6 3.6 multiply_reduce_fusion.3
  323.1 4.3 copy.125
  327.4 3.7 maximum_bitcast_fusion.1
  331.1 6.6 copy.127
  337.7 3.3 dynamic-slice_bitcast_fusion.2
  342.5 4.3 copy.122
  346.8 3.7 maximum_bitcast_fusion
  350.5 6.8 copy.124
  357.3 3.3 dynamic-slice_bitcast_fusion.3
  361.1 5.0 dynamic-slice_bitcast_fusion
  366.4 5.1 dynamic-slice_bitcast_fusion.1
  378.0 4.5 all-to-all-start.3
  385.3 4.5 fusion.30
  389.9 3.4 fusion.33
  394.1 125.6 %all-reduce.10.cloned.1.call-done = (f32[2,768]{1,0:T(2,128)}, f32[2,768]{1,0:T(2,128)}, f32[2,3,2304]{2,1,0:T(4,128)}, f32[2,33,64]{2,1,0:T(8,128)}, f32[2,2,64...) async-done(((f32[2,768]{1,0:T(2,128)}, f32[2,768]{1,0:T(2,128)}, f32[2,3,2304]{2,1,0:T(4,128)}, ...) | async-done | bytes 136720 | tf_op jit(solution)/shard_map/psum | solution.py:937
  522.7 3.3 convert.8
  526.0 3.5 convert.9
  538.7 10.7 %collective-permute-done.9 = bf16[2,4,96,384]{3,2,1,0:T(8,128)(2,1)S(1)} collective-permute-done((bf16[2,4,96,384]{3,2,1,0:T(8,128)(2,1)S(1)}, bf16[2,4,96,384]{3,2,1,0:T(8,128)(2,1)S(1)}, u32[]{:S(2)}, u32[]{:S(2)}) %collective-permute-start.9) | collective-permute-done | bytes 589856 | tf_op jit(solution)/shard_map/ppermute | solution.py:836
  551.7 9.4 %collective-permute-done.1 = bf16[2,4,96,384]{3,2,1,0:T(8,128)(2,1)S(1)} collective-permute-done((bf16[2,4,96,384]{3,2,1,0:T(8,128)(2,1)S(1)}, bf16[2,4,96,384]{3,2,1,0:T(8,128)(2,1)S(1)}, u32[]{:S(2)}, u32[]{:S(2)}) %collective-permute-start.1) | collective-permute-done | bytes 589856 | tf_op jit(solution)/shard_map/ppermute | solution.py:836
  562.6 3.4 collective-permute-done.3
  567.3 5.0 collective-permute-done.10
  584.3 8.3 %collective-permute-done.14 = bf16[96,768]{1,0:T(8,128)(2,1)S(1)} collective-permute-done((bf16[96,768]{1,0:T(8,128)(2,1)S(1)}, bf16[96,768]{1,0:T(8,128)(2,1)S(1)}, u32[]{:S(2)}, u32[]{:S(2)}) %collective-permute-start.14) | collective-permute-done | bytes 147488 | tf_op jit(solution)/shard_map/ppermute | solution.py:861
  594.1 6.1 collective-permute-done.6
  602.5 3.0 bitcast_add_fusion
  617.7 18.9 %collective-permute-done.25 = bf16[2,4,96,768]{3,2,1,0:T(8,128)(2,1)} collective-permute-done((bf16[2,4,96,768]{3,2,1,0:T(8,128)(2,1)}, bf16[2,4,96,768]{3,2,1,0:T(8,128)(2,1)}, u32[]{:S(2)}, u32[]{:S(2)}) %collective-permute-start.25) | collective-permute-done | bytes 1179680 | tf_op jit(solution)/shard_map/ppermute | solution.py:836
  642.4 20.3 %collective-permute-done.17 = bf16[2,4,96,768]{3,2,1,0:T(8,128)(2,1)S(1)} collective-permute-done((bf16[2,4,96,768]{3,2,1,0:T(8,128)(2,1)S(1)}, bf16[2,4,96,768]{3,2,1,0:T(8,128)(2,1)S(1)}, u32[]{:S(2)}, u32[]{:S(2)}) %collective-permute-start.17) | collective-permute-done | bytes 1179680 | tf_op jit(solution)/shard_map/ppermute | solution.py:836
  666.1 11.9 %collective-permute-done.26 = bf16[4,96,768]{2,1,0:T(8,128)(2,1)S(1)} collective-permute-done((bf16[4,96,768]{2,1,0:T(8,128)(2,1)S(1)}, bf16[4,96,768]{2,1,0:T(8,128)(2,1)S(1)}, u32[]{:S(2)}, u32[]{:S(2)}) %collective-permute-start.26) | collective-permute-done | bytes 589856 | tf_op jit(solution)/shard_map/ppermute | solution.py:836
  681.4 6.4 collective-permute-done.18
  690.0 10.7 %collective-permute-start.21 = (bf16[96,1536]{1,0:T(8,128)(2,1)S(1)}, bf16[96,1536]{1,0:T(8,128)(2,1)S(1)}, u32[]{:S(2)}, u32[]{:S(2)}) collective-permute-start(bf16[96,1536]{1,0:T(8,128)(2,1)S(1)} %get-tuple-element.161), channel_id=1, source_target_pairs={{0,8},{4,12},{8,16},{12,20},{16,24},{20,28},{24,0},{28,4},{1,9},{5... | collective-permute-start | bytes 884744 | tf_op jit(solution)/shard_map/ppermute | solution.py:861
  700.7 15.0 %collective-permute-done.30 = bf16[96,1536]{1,0:T(8,128)(2,1)S(1)} collective-permute-done((bf16[96,1536]{1,0:T(8,128)(2,1)S(1)}, bf16[96,1536]{1,0:T(8,128)(2,1)S(1)}, u32[]{:S(2)}, u32[]{:S(2)}) %collective-permute-start.30) | collective-permute-done | bytes 294944 | tf_op jit(solution)/shard_map/ppermute | solution.py:861
  716.0 8.0 %collective-permute-done.22 = bf16[96,1536]{1,0:T(8,128)(2,1)S(1)} collective-permute-done((bf16[96,1536]{1,0:T(8,128)(2,1)S(1)}, bf16[96,1536]{1,0:T(8,128)(2,1)S(1)}, u32[]{:S(2)}, u32[]{:S(2)}) %collective-permute-start.22) | collective-permute-done | bytes 294944 | tf_op jit(solution)/shard_map/ppermute | solution.py:861
  (334 shorter events, 100.9 us)
Async XLA Ops:
  7.3 34.7 %all-to-all-start = ((bf16[4,256,768]{2,1,0:T(8,128)(2,1)}), bf16[4,256,768]{2,1,0:T(8,128)(2,1)S(1)}, u32[]{:S(2)}, u32[]{:S(2)}) async-start(bf16[4,256,768]{2,1,0:T(8,128)(2,1)} %bitcast.274), calls=%async_computation | async-start | bytes 3145728 | tf_op jit(solution)/shard_map/all_to_all | solution.py:877
  14.7 304.5 %copy-start.43 = (f32[64]{0:T(128)}, f32[64]{0:T(128)S(1)}, u32[]{:S(2)}) copy-start(f32[64]{0:T(128)S(1)} %get-tuple-element.185) | copy-start | bytes 772
  17.2 302.0 %copy-start.6 = (f32[1024,64]{0,1:T(8,128)}, f32[1024,64]{0,1:T(8,128)S(1)}, u32[]{:S(2)}) copy-start(f32[1024,64]{0,1:T(8,128)S(1)} %fusion.108) | copy-start | bytes 786436
  17.6 295.6 %copy-start.41 = (f32[64]{0:T(128)}, f32[64]{0:T(128)S(1)}, u32[]{:S(2)}) copy-start(f32[64]{0:T(128)S(1)} %get-tuple-element.182) | copy-start | bytes 772
  17.6 295.6 %copy-start.45 = (f32[64]{0:T(128)}, f32[64]{0:T(128)S(1)}, u32[]{:S(2)}) copy-start(f32[64]{0:T(128)S(1)} %get-tuple-element.181) | copy-start | bytes 772
  42.0 103.4 %all-to-all-start.2 = ((bf16[4,256,768]{2,1,0:T(8,128)(2,1)}), bf16[4,256,768]{2,1,0:T(8,128)(2,1)S(1)}, u32[]{:S(2)}, u32[]{:S(2)}) async-start(bf16[4,256,768]{2,1,0:T(8,128)(2,1)} %bitcast.275), calls=%async_computation.2 | async-start | bytes 3145728 | tf_op jit(solution)/shard_map/all_to_all | solution.py:877
  145.4 232.6 %all-to-all-start.1 = ((bf16[4,256,768]{2,1,0:T(8,128)(2,1)}), bf16[4,256,768]{2,1,0:T(8,128)(2,1)}, u32[]{:S(2)}, u32[]{:S(2)}) async-start(bf16[4,256,768]{2,1,0:T(8,128)(2,1)} %bitcast.20), calls=%async_computation.1 | async-start | bytes 3145728 | tf_op jit(solution)/shard_map/all_to_all | solution.py:881
  341.0 188.4 %collective-permute-start.8 = (bf16[2,2,4,96,768]{4,3,2,1,0:T(8,128)(2,1)}, bf16[2,2,4,96,768]{4,3,2,1,0:T(8,128)(2,1)}, u32[]{:S(2)}, u32[]{:S(2)}) collective-permute-start(bf16[2,2,4,96,768]{4,3,2,1,0:T(8,128)(2,1)} %dynamic-slice_bitcast_fusion.2), channel_id=1, source_target_pairs={{0,4},{4,0},{8,12},{12,8},{16,20},{20,16},{24,28},{28,24},{1,5},{5... | collective-permute-start | bytes 7077896 | tf_op jit(solution)/shard_map/ppermute | solution.py:836
  360.6 174.4 %collective-permute-start = (bf16[2,2,4,96,768]{4,3,2,1,0:T(8,128)(2,1)}, bf16[2,2,4,96,768]{4,3,2,1,0:T(8,128)(2,1)}, u32[]{:S(2)}, u32[]{:S(2)}) collective-permute-start(bf16[2,2,4,96,768]{4,3,2,1,0:T(8,128)(2,1)} %dynamic-slice_bitcast_fusion.3), channel_id=1, source_target_pairs={{0,4},{4,0},{8,12},{12,8},{16,20},{20,16},{24,28},{28,24},{1,5},{5... | collective-permute-start | bytes 7077896 | tf_op jit(solution)/shard_map/ppermute | solution.py:836
  366.1 236.4 %collective-permute-start.24 = (bf16[2,2,4,96,1536]{4,3,2,1,0:T(8,128)(2,1)}, bf16[2,2,4,96,1536]{4,3,2,1,0:T(8,128)(2,1)}, u32[]{:S(2)}, u32[]{:S(2)}) collective-permute-start(bf16[2,2,4,96,1536]{4,3,2,1,0:T(8,128)(2,1)} %dynamic-slice_bitcast_fusion), channel_id=1, source_target_pairs={{0,4},{4,0},{8,12},{12,8},{16,20},{20,16},{24,28},{28,24},{1,5},{5... | collective-permute-start | bytes 14155784 | tf_op jit(solution)/shard_map/ppermute | solution.py:836
  371.4 239.4 %collective-permute-start.16 = (bf16[2,2,4,96,1536]{4,3,2,1,0:T(8,128)(2,1)}, bf16[2,2,4,96,1536]{4,3,2,1,0:T(8,128)(2,1)}, u32[]{:S(2)}, u32[]{:S(2)}) collective-permute-start(bf16[2,2,4,96,1536]{4,3,2,1,0:T(8,128)(2,1)} %dynamic-slice_bitcast_fusion.1), channel_id=1, source_target_pairs={{0,4},{4,0},{8,12},{12,8},{16,20},{20,16},{24,28},{28,24},{1,5},{5... | collective-permute-start | bytes 14155784 | tf_op jit(solution)/shard_map/ppermute | solution.py:836
  378.0 147.9 %all-to-all-start.3 = ((bf16[4,256,768]{2,1,0:T(8,128)(2,1)}), bf16[4,256,768]{2,1,0:T(8,128)(2,1)}, u32[]{:S(2)}, u32[]{:S(2)}) async-start(bf16[4,256,768]{2,1,0:T(8,128)(2,1)} %bitcast.268), calls=%async_computation.3 | async-start | bytes 3145728 | tf_op jit(solution)/shard_map/all_to_all | solution.py:881
  382.5 137.2 %all-reduce.10.cloned.1.call-start = ((), (), s32[]{:S(2)}) async-start(), calls=%async_computation.5 | async-start | bytes 425984 | tf_op jit(solution)/shard_map/psum | solution.py:937
  385.3 340.6 %all-reduce.8.cloned.1.call-start = ((), (), s32[]{:S(2)}) async-start(), calls=%async_computation.4 | async-start | bytes 786432 | tf_op jit(solution)/shard_map/psum | solution.py:937
  532.6 16.8 %collective-permute-start.9 = (bf16[2,4,96,384]{3,2,1,0:T(8,128)(2,1)S(1)}, bf16[2,4,96,384]{3,2,1,0:T(8,128)(2,1)S(1)}, u32[]{:S(2)}, u32[]{:S(2)}) collective-permute-start(bf16[2,4,96,384]{3,2,1,0:T(8,128)(2,1)S(1)} %dynamic-slice_bitcast_fusion.13), channel_id=1, source_target_pairs={{0,1},{1,0},{2,3},{3,2},{4,5},{5,4},{6,7},{7,6},{8,9},{9,8},{10,11... | collective-permute-start | bytes 1769480 | tf_op jit(solution)/shard_map/ppermute | solution.py:836
  534.1 16.7 %collective-permute-start.11 = (bf16[2,4,96,384]{3,2,1,0:T(8,128)(2,1)S(1)}, bf16[2,4,96,384]{3,2,1,0:T(8,128)(2,1)S(1)}, u32[]{:S(2)}, u32[]{:S(2)}) collective-permute-start(bf16[2,4,96,384]{3,2,1,0:T(8,128)(2,1)S(1)} %dynamic-slice_bitcast_fusion.12), channel_id=1, source_target_pairs={{0,2},{1,3},{2,0},{3,1},{4,6},{5,7},{6,4},{7,5},{8,10},{9,11},{10,... | collective-permute-start | bytes 1769480 | tf_op jit(solution)/shard_map/ppermute | solution.py:836
  537.0 65.5 %slice-start.2 = ((s8[9437184]{0:T(1024)(128)(4,1)}), s8[4194304]{0:T(1024)(128)(4,1)S(1)}, s32[]{:S(2)}) async-start(s8[9437184]{0:T(1024)(128)(4,1)} %bitcast.261), calls=%async_computation.8 | async-start | bytes 8388608
  537.4 23.7 %collective-permute-start.1 = (bf16[2,4,96,384]{3,2,1,0:T(8,128)(2,1)S(1)}, bf16[2,4,96,384]{3,2,1,0:T(8,128)(2,1)S(1)}, u32[]{:S(2)}, u32[]{:S(2)}) collective-permute-start(bf16[2,4,96,384]{3,2,1,0:T(8,128)(2,1)S(1)} %dynamic-slice_bitcast_fusion.15), channel_id=1, source_target_pairs={{0,1},{1,0},{2,3},{3,2},{4,5},{5,4},{6,7},{7,6},{8,9},{9,8},{10,11... | collective-permute-start | bytes 1769480 | tf_op jit(solution)/shard_map/ppermute | solution.py:836
  538.7 63.8 %slice-start.3 = ((s8[9437184]{0:T(1024)(128)(4,1)}), s8[4194304]{0:T(1024)(128)(4,1)S(1)}, s32[]{:S(2)}) async-start(s8[9437184]{0:T(1024)(128)(4,1)} %bitcast.261), calls=%async_computation.9 | async-start | bytes 8388608
  549.3 16.6 %collective-permute-start.3 = (bf16[2,4,96,384]{3,2,1,0:T(8,128)(2,1)S(1)}, bf16[2,4,96,384]{3,2,1,0:T(8,128)(2,1)S(1)}, u32[]{:S(2)}, u32[]{:S(2)}) collective-permute-start(bf16[2,4,96,384]{3,2,1,0:T(8,128)(2,1)S(1)} %dynamic-slice_bitcast_fusion.14), channel_id=1, source_target_pairs={{0,2},{1,3},{2,0},{3,1},{4,6},{5,7},{6,4},{7,5},{8,10},{9,11},{10,... | collective-permute-start | bytes 1769480 | tf_op jit(solution)/shard_map/ppermute | solution.py:836
  550.8 21.5 %collective-permute-start.10 = (bf16[4,96,384]{2,1,0:T(8,128)(2,1)S(1)}, bf16[4,96,384]{2,1,0:T(8,128)(2,1)S(1)}, u32[]{:S(2)}, u32[]{:S(2)}) collective-permute-start(bf16[4,96,384]{2,1,0:T(8,128)(2,1)S(1)} %dynamic-slice_bitcast_fusion.17), channel_id=1, source_target_pairs={{0,2},{1,3},{2,0},{3,1},{4,6},{5,7},{6,4},{7,5},{8,10},{9,11},{10,... | collective-permute-start | bytes 884744 | tf_op jit(solution)/shard_map/ppermute | solution.py:836
  561.1 12.7 %collective-permute-start.12 = (bf16[4,96,384]{2,1,0:T(8,128)(2,1)S(1)}, bf16[4,96,384]{2,1,0:T(8,128)(2,1)S(1)}, u32[]{:S(2)}, u32[]{:S(2)}) collective-permute-start(bf16[4,96,384]{2,1,0:T(8,128)(2,1)S(1)} %dynamic-slice_bitcast_fusion.16), channel_id=1, source_target_pairs={{0,1},{1,0},{2,3},{3,2},{4,5},{5,4},{6,7},{7,6},{8,9},{9,8},{10,11... | collective-permute-start | bytes 884744 | tf_op jit(solution)/shard_map/ppermute | solution.py:836
  566.0 9.9 %collective-permute-start.2 = (bf16[4,96,384]{2,1,0:T(8,128)(2,1)S(1)}, bf16[4,96,384]{2,1,0:T(8,128)(2,1)S(1)}, u32[]{:S(2)}, u32[]{:S(2)}) collective-permute-start(bf16[4,96,384]{2,1,0:T(8,128)(2,1)S(1)} %dynamic-slice_bitcast_fusion.19), channel_id=1, source_target_pairs={{0,2},{1,3},{2,0},{3,1},{4,6},{5,7},{6,4},{7,5},{8,10},{9,11},{10,... | collective-permute-start | bytes 884744 | tf_op jit(solution)/shard_map/ppermute | solution.py:836
  572.3 6.7 collective-permute-start.4
  573.8 28.7 %slice-start.4 = ((s8[9437184]{0:T(1024)(128)(4,1)}), s8[1048576]{0:T(1024)(128)(4,1)S(1)}, s32[]{:S(2)}) async-start(s8[9437184]{0:T(1024)(128)(4,1)} %bitcast.261), calls=%async_computation.10 | async-start | bytes 2097152
  573.9 9.9 %collective-permute-start.15 = (bf16[96,768]{1,0:T(8,128)(2,1)S(1)}, bf16[96,768]{1,0:T(8,128)(2,1)S(1)}, u32[]{:S(2)}, u32[]{:S(2)}) collective-permute-start(bf16[96,768]{1,0:T(8,128)(2,1)S(1)} %get-tuple-element.176), channel_id=1, source_target_pairs={{0,24},{4,28},{8,0},{12,4},{16,8},{20,12},{24,16},{28,20},{1,25},{... | collective-permute-start | bytes 442376 | tf_op jit(solution)/shard_map/ppermute | solution.py:861
  575.9 16.7 %collective-permute-start.14 = (bf16[96,768]{1,0:T(8,128)(2,1)S(1)}, bf16[96,768]{1,0:T(8,128)(2,1)S(1)}, u32[]{:S(2)}, u32[]{:S(2)}) collective-permute-start(bf16[96,768]{1,0:T(8,128)(2,1)S(1)} %get-tuple-element.175), channel_id=1, source_target_pairs={{0,16},{4,20},{8,24},{12,28},{16,0},{20,4},{24,8},{28,12},{1,17},{... | collective-permute-start | bytes 442376 | tf_op jit(solution)/shard_map/ppermute | solution.py:861
  579.0 13.6 %collective-permute-start.13 = (bf16[96,768]{1,0:T(8,128)(2,1)S(1)}, bf16[96,768]{1,0:T(8,128)(2,1)S(1)}, u32[]{:S(2)}, u32[]{:S(2)}) collective-permute-start(bf16[96,768]{1,0:T(8,128)(2,1)S(1)} %get-tuple-element.174), channel_id=1, source_target_pairs={{0,8},{4,12},{8,16},{12,20},{16,24},{20,28},{24,0},{28,4},{1,9},{5... | collective-permute-start | bytes 442376 | tf_op jit(solution)/shard_map/ppermute | solution.py:861
  583.8 10.3 %collective-permute-start.7 = (bf16[96,768]{1,0:T(8,128)(2,1)S(1)}, bf16[96,768]{1,0:T(8,128)(2,1)S(1)}, u32[]{:S(2)}, u32[]{:S(2)}) collective-permute-start(bf16[96,768]{1,0:T(8,128)(2,1)S(1)} %get-tuple-element.173), channel_id=1, source_target_pairs={{0,24},{4,28},{8,0},{12,4},{16,8},{20,12},{24,16},{28,20},{1,25},{... | collective-permute-start | bytes 442376 | tf_op jit(solution)/shard_map/ppermute | solution.py:861
  592.6 7.6 %collective-permute-start.6 = (bf16[96,768]{1,0:T(8,128)(2,1)S(1)}, bf16[96,768]{1,0:T(8,128)(2,1)S(1)}, u32[]{:S(2)}, u32[]{:S(2)}) collective-permute-start(bf16[96,768]{1,0:T(8,128)(2,1)S(1)} %get-tuple-element.172), channel_id=1, source_target_pairs={{0,16},{4,20},{8,24},{12,28},{16,0},{20,4},{24,8},{28,12},{1,17},{... | collective-permute-start | bytes 442376 | tf_op jit(solution)/shard_map/ppermute | solution.py:861
  592.6 7.6 %collective-permute-start.5 = (bf16[96,768]{1,0:T(8,128)(2,1)S(1)}, bf16[96,768]{1,0:T(8,128)(2,1)S(1)}, u32[]{:S(2)}, u32[]{:S(2)}) collective-permute-start(bf16[96,768]{1,0:T(8,128)(2,1)S(1)} %get-tuple-element.171), channel_id=1, source_target_pairs={{0,8},{4,12},{8,16},{12,20},{16,24},{20,28},{24,0},{28,4},{1,9},{5... | collective-permute-start | bytes 442376 | tf_op jit(solution)/shard_map/ppermute | solution.py:861
  607.2 29.4 %collective-permute-start.25 = (bf16[2,4,96,768]{3,2,1,0:T(8,128)(2,1)}, bf16[2,4,96,768]{3,2,1,0:T(8,128)(2,1)}, u32[]{:S(2)}, u32[]{:S(2)}) collective-permute-start(bf16[2,4,96,768]{3,2,1,0:T(8,128)(2,1)} %dynamic-slice_bitcast_fusion.5), channel_id=1, source_target_pairs={{0,1},{1,0},{2,3},{3,2},{4,5},{5,4},{6,7},{7,6},{8,9},{9,8},{10,11... | collective-permute-start | bytes 3538952 | tf_op jit(solution)/shard_map/ppermute | solution.py:836
  609.9 29.7 %collective-permute-start.27 = (bf16[2,4,96,768]{3,2,1,0:T(8,128)(2,1)}, bf16[2,4,96,768]{3,2,1,0:T(8,128)(2,1)}, u32[]{:S(2)}, u32[]{:S(2)}) collective-permute-start(bf16[2,4,96,768]{3,2,1,0:T(8,128)(2,1)} %dynamic-slice_bitcast_fusion.4), channel_id=1, source_target_pairs={{0,2},{1,3},{2,0},{3,1},{4,6},{5,7},{6,4},{7,5},{8,10},{9,11},{10,... | collective-permute-start | bytes 3538952 | tf_op jit(solution)/shard_map/ppermute | solution.py:836
  614.4 48.2 %collective-permute-start.17 = (bf16[2,4,96,768]{3,2,1,0:T(8,128)(2,1)S(1)}, bf16[2,4,96,768]{3,2,1,0:T(8,128)(2,1)S(1)}, u32[]{:S(2)}, u32[]{:S(2)}) collective-permute-start(bf16[2,4,96,768]{3,2,1,0:T(8,128)(2,1)S(1)} %dynamic-slice_bitcast_fusion.7), channel_id=1, source_target_pairs={{0,1},{1,0},{2,3},{3,2},{4,5},{5,4},{6,7},{7,6},{8,9},{9,8},{10,11... | collective-permute-start | bytes 3538952 | tf_op jit(solution)/shard_map/ppermute | solution.py:836
  617.0 48.3 %collective-permute-start.19 = (bf16[2,4,96,768]{3,2,1,0:T(8,128)(2,1)S(1)}, bf16[2,4,96,768]{3,2,1,0:T(8,128)(2,1)S(1)}, u32[]{:S(2)}, u32[]{:S(2)}) collective-permute-start(bf16[2,4,96,768]{3,2,1,0:T(8,128)(2,1)S(1)} %dynamic-slice_bitcast_fusion.6), channel_id=1, source_target_pairs={{0,2},{1,3},{2,0},{3,1},{4,6},{5,7},{6,4},{7,5},{8,10},{9,11},{10,... | collective-permute-start | bytes 3538952 | tf_op jit(solution)/shard_map/ppermute | solution.py:836
  638.1 39.9 %collective-permute-start.26 = (bf16[4,96,768]{2,1,0:T(8,128)(2,1)S(1)}, bf16[4,96,768]{2,1,0:T(8,128)(2,1)S(1)}, u32[]{:S(2)}, u32[]{:S(2)}) collective-permute-start(bf16[4,96,768]{2,1,0:T(8,128)(2,1)S(1)} %dynamic-slice_bitcast_fusion.9), channel_id=1, source_target_pairs={{0,2},{1,3},{2,0},{3,1},{4,6},{5,7},{6,4},{7,5},{8,10},{9,11},{10,... | collective-permute-start | bytes 1769480 | tf_op jit(solution)/shard_map/ppermute | solution.py:836
  641.1 37.0 %collective-permute-start.28 = (bf16[4,96,768]{2,1,0:T(8,128)(2,1)S(1)}, bf16[4,96,768]{2,1,0:T(8,128)(2,1)S(1)}, u32[]{:S(2)}, u32[]{:S(2)}) collective-permute-start(bf16[4,96,768]{2,1,0:T(8,128)(2,1)S(1)} %dynamic-slice_bitcast_fusion.8), channel_id=1, source_target_pairs={{0,1},{1,0},{2,3},{3,2},{4,5},{5,4},{6,7},{7,6},{8,9},{9,8},{10,11... | collective-permute-start | bytes 1769480 | tf_op jit(solution)/shard_map/ppermute | solution.py:836
  662.9 25.0 %collective-permute-start.18 = (bf16[4,96,768]{2,1,0:T(8,128)(2,1)S(1)}, bf16[4,96,768]{2,1,0:T(8,128)(2,1)S(1)}, u32[]{:S(2)}, u32[]{:S(2)}) collective-permute-start(bf16[4,96,768]{2,1,0:T(8,128)(2,1)S(1)} %dynamic-slice_bitcast_fusion.11), channel_id=1, source_target_pairs={{0,2},{1,3},{2,0},{3,1},{4,6},{5,7},{6,4},{7,5},{8,10},{9,11},{10,... | collective-permute-start | bytes 1769480 | tf_op jit(solution)/shard_map/ppermute | solution.py:836
  665.6 22.3 %collective-permute-start.20 = (bf16[4,96,768]{2,1,0:T(8,128)(2,1)S(1)}, bf16[4,96,768]{2,1,0:T(8,128)(2,1)S(1)}, u32[]{:S(2)}, u32[]{:S(2)}) collective-permute-start(bf16[4,96,768]{2,1,0:T(8,128)(2,1)S(1)} %dynamic-slice_bitcast_fusion.10), channel_id=1, source_target_pairs={{0,1},{1,0},{2,3},{3,2},{4,5},{5,4},{6,7},{7,6},{8,9},{9,8},{10,11... | collective-permute-start | bytes 1769480 | tf_op jit(solution)/shard_map/ppermute | solution.py:836
  678.2 11.8 %collective-permute-start.31 = (bf16[96,1536]{1,0:T(8,128)(2,1)S(1)}, bf16[96,1536]{1,0:T(8,128)(2,1)S(1)}, u32[]{:S(2)}, u32[]{:S(2)}) collective-permute-start(bf16[96,1536]{1,0:T(8,128)(2,1)S(1)} %get-tuple-element.166), channel_id=1, source_target_pairs={{0,24},{4,28},{8,0},{12,4},{16,8},{20,12},{24,16},{28,20},{1,25},{... | collective-permute-start | bytes 884744 | tf_op jit(solution)/shard_map/ppermute | solution.py:861
  679.2 36.5 %collective-permute-start.30 = (bf16[96,1536]{1,0:T(8,128)(2,1)S(1)}, bf16[96,1536]{1,0:T(8,128)(2,1)S(1)}, u32[]{:S(2)}, u32[]{:S(2)}) collective-permute-start(bf16[96,1536]{1,0:T(8,128)(2,1)S(1)} %get-tuple-element.165), channel_id=1, source_target_pairs={{0,16},{4,20},{8,24},{12,28},{16,0},{20,4},{24,8},{28,12},{1,17},{... | collective-permute-start | bytes 884744 | tf_op jit(solution)/shard_map/ppermute | solution.py:861
  679.4 36.3 %collective-permute-start.29 = (bf16[96,1536]{1,0:T(8,128)(2,1)S(1)}, bf16[96,1536]{1,0:T(8,128)(2,1)S(1)}, u32[]{:S(2)}, u32[]{:S(2)}) collective-permute-start(bf16[96,1536]{1,0:T(8,128)(2,1)S(1)} %get-tuple-element.164), channel_id=1, source_target_pairs={{0,8},{4,12},{8,16},{12,20},{16,24},{20,28},{24,0},{28,4},{1,9},{5... | collective-permute-start | bytes 884744 | tf_op jit(solution)/shard_map/ppermute | solution.py:861
  688.0 27.9 %collective-permute-start.23 = (bf16[96,1536]{1,0:T(8,128)(2,1)S(1)}, bf16[96,1536]{1,0:T(8,128)(2,1)S(1)}, u32[]{:S(2)}, u32[]{:S(2)}) collective-permute-start(bf16[96,1536]{1,0:T(8,128)(2,1)S(1)} %get-tuple-element.163), channel_id=1, source_target_pairs={{0,24},{4,28},{8,0},{12,4},{16,8},{20,12},{24,16},{28,20},{1,25},{... | collective-permute-start | bytes 884744 | tf_op jit(solution)/shard_map/ppermute | solution.py:861
  688.1 35.9 %collective-permute-start.22 = (bf16[96,1536]{1,0:T(8,128)(2,1)S(1)}, bf16[96,1536]{1,0:T(8,128)(2,1)S(1)}, u32[]{:S(2)}, u32[]{:S(2)}) collective-permute-start(bf16[96,1536]{1,0:T(8,128)(2,1)S(1)} %get-tuple-element.162), channel_id=1, source_target_pairs={{0,16},{4,20},{8,24},{12,28},{16,0},{20,4},{24,8},{28,12},{1,17},{... | collective-permute-start | bytes 884744 | tf_op jit(solution)/shard_map/ppermute | solution.py:861
  690.0 33.9 %collective-permute-start.21 = (bf16[96,1536]{1,0:T(8,128)(2,1)S(1)}, bf16[96,1536]{1,0:T(8,128)(2,1)S(1)}, u32[]{:S(2)}, u32[]{:S(2)}) collective-permute-start(bf16[96,1536]{1,0:T(8,128)(2,1)S(1)} %get-tuple-element.161), channel_id=1, source_target_pairs={{0,8},{4,12},{8,16},{12,20},{16,24},{20,28},{24,0},{28,4},{1,9},{5... | collective-permute-start | bytes 884744 | tf_op jit(solution)/shard_map/ppermute | solution.py:861
  715.9 16.0 %copy-start.1 = (s32[2,1]{0,1:T(1,128)S(1)}, s32[2,1]{0,1:T(1,128)}, u32[]{:S(2)}) copy-start(s32[2,1]{0,1:T(1,128)} %param.21) | copy-start | bytes 28
  716.0 14.7 %copy-start.48 = (f32[2,768]{1,0:T(2,128)S(1)}, f32[2,768]{1,0:T(2,128)}, u32[]{:S(2)}) copy-start(f32[2,768]{1,0:T(2,128)} %get-tuple-element.213) | copy-start | bytes 18436
  716.0 15.3 %copy-start.47 = (f32[2,768]{1,0:T(2,128)S(1)}, f32[2,768]{1,0:T(2,128)}, u32[]{:S(2)}) copy-start(f32[2,768]{1,0:T(2,128)} %get-tuple-element.214) | copy-start | bytes 18436
  (71 other events, 524.3 us)
Sparse Core Ops, SparseCore 0:
  390.9 128.7 all-reduce.9
  526.4 131.8 all-reduce.7

commit v3 on v2

--- a/solution.py
+++ b/solution.py
@@ -478,6 +478,7 @@
 
 
 MIB = 1 << 20
+MESH = pl.DeviceIdType.MESH
 
 
 def mm(left, right):
@@ -486,6 +487,10 @@
 
 def mm_nt(left, right):
     return lax.dot_general(left, right, (((1,), (1,)), ((), ())), preferred_element_type=jnp.float32)
+
+
+def mm_tn(left, right):
+    return lax.dot_general(left, right, (((0,), (0,)), ((), ())), preferred_element_type=jnp.float32)
 
 
 def f32(values):
@@ -544,6 +549,51 @@
     return pl.BlockSpec((None,) + shape, lambda j: (layer,) + (0,) * len(shape), pipeline_mode=pl.Buffered(1))
 
 
+ANY = pl.BlockSpec(memory_space=pl.ANY)
+
+
+def sds(shape, kind):
+    return jax.ShapeDtypeStruct(shape, kind)
+
+
+class Place:
+    def __init__(self):
+        s, t = lax.axis_index("seq"), lax.axis_index("tok")
+        self.depth = lax.axis_size("seq") // 2
+        self.z, self.core, self.y, self.x = s // 2, s % 2, t // 2, t % 2
+        self.s, self.t = s, t
+        self.over_core = (2 * self.z + 1 - self.core, t)
+        self.over_x = (s, 2 * self.y + 1 - self.x)
+        self.over_y = (s, 2 * (1 - self.y) + self.x)
+        self.over_z = [(2 * ((self.z + d) % self.depth) + self.core, t) for d in range(1, self.depth)]
+        self.from_z = [(2 * ((self.z + self.depth - d) % self.depth) + self.core, t) for d in range(1, self.depth)]
+
+
+def greet(partners):
+    barrier = pltpu.get_barrier_semaphore()
+    for partner in partners:
+        pl.semaphore_signal(barrier, inc=1, device_id=partner, device_id_type=MESH)
+    pl.semaphore_wait(barrier, len(partners))
+
+
+def remote(source, target, sent, landed, device):
+    return pltpu.make_async_remote_copy(
+        src_ref=source, dst_ref=target, send_sem=sent, recv_sem=landed, device_id=device, device_id_type=MESH
+    )
+
+
+def other_first(place, s, piece):
+    half = place.depth * piece
+    mine = (s % 2 + place.core + 1) % 2
+    return pl.multiple_of(mine * half + (s // 2) * piece, 16)
+
+
+def store_rows(place, target, values):
+    piece = values.shape[0] // (2 * place.depth)
+    for s in range(2 * place.depth):
+        target[pl.ds(other_first(place, s, piece), piece), :] = values[s * piece : (s + 1) * piece]
+
+
 def mixed_chunk(proj, kernel):
     return [
         kernel[p][0:1] * row_shift(proj[p], 2) + kernel[p][1:2] * row_shift(proj[p], 1) + kernel[p][2:3] * proj[p]
@@ -552,7 +602,7 @@
 
 
 def mixer_forward_body(
-    r_ref, gain_ref, bias_ref, w0_ref, w1_ref, w2_ref, k0_ref, k1_ref, k2_ref, table_ref, back_ref, taps_ref, skip_ref,
+    r_ref, gain_ref, bias_ref, w0_ref, w1_ref, w2_ref, k0_ref, k1_ref, k2_ref, table_ref, taps_ref, skip_ref,
     wo_ref, hidden_ref, normed_ref, proj_ref, signal_ref, long_ref,
 ):
     length = r_ref.shape[0]
@@ -574,14 +624,14 @@
     re, im = both[:length], both[length:]
     signal_ref[...] = bf(both)
     tap_re, tap_im = f32(taps_ref[:length]), f32(taps_ref[length:])
-    out = mm(back_ref[:, :length], bf(re * tap_re - im * tap_im))
-    out += mm(back_ref[:, length:], bf(re * tap_im + im * tap_re))
+    out = mm_tn(table_ref[:length], bf(re * tap_re - im * tap_im))
+    out += mm_tn(table_ref[length:], bf(re * tap_im + im * tap_re))
     long_out = out + f32(skip_ref[...]) * carried
     long_ref[...] = bf(long_out)
     hidden_ref[...] += mm(bf(long_out * gate_out), wo_ref[...])
 
 
-def mixer_forward(layer, r, gain, bias, w_in, short_w, table, back, taps, skip, w_out):
+def mixer_forward(layer, r, gain, bias, w_in, short_w, table, taps, skip, w_out):
     length, width = r.shape
     chunk = 256
     steps = width // chunk
@@ -593,7 +643,7 @@
         in_specs=[
             whole((length, width)), of_layer(layer, (1, width)), of_layer(layer, (1, width)),
             third(0), third(1), third(2), short(0), short(1), short(2),
-            whole((2 * length, length)), whole((length, 2 * length)),
+            whole((2 * length, length)),
             pl.BlockSpec((2 * length, chunk), lambda j: (0, j)),
             pl.BlockSpec((None, 1, chunk), lambda j: (layer, 0, j)),
             pl.BlockSpec((None, chunk, width), lambda j: (layer, j, 0)),
@@ -605,18 +655,16 @@
             pl.BlockSpec((length, chunk), lambda j: (0, j)),
         ],
         out_shape=[
-            jax.ShapeDtypeStruct((length, width), jnp.float32),
-            jax.ShapeDtypeStruct((length, width), jnp.bfloat16),
-            jax.ShapeDtypeStruct((3, length, width), jnp.bfloat16),
-            jax.ShapeDtypeStruct((2 * length, width), jnp.bfloat16),
-            jax.ShapeDtypeStruct((length, width), jnp.bfloat16),
+            sds((length, width), jnp.float32), sds((length, width), jnp.bfloat16),
+            sds((3, length, width), jnp.bfloat16), sds((2 * length, width), jnp.bfloat16),
+            sds((length, width), jnp.bfloat16),
         ],
         compiler_params=pltpu.CompilerParams(vmem_limit_bytes=60 * MIB),
         cost_estimate=pl.CostEstimate(
             flops=2 * length * width * (4 * width + 4 * length), bytes_accessed=30 * MIB, transcendentals=0
         ),
         name="mixer_forward",
-    )(r, gain, bias, w_in, w_in, w_in, short_w, short_w, short_w, table, back, taps, skip, w_out)
+    )(r, gain, bias, w_in, w_in, w_in, short_w, short_w, short_w, table, taps, skip, w_out)
 
 
 def ffn_forward_body(hidden_ref, gain_ref, bias_ref, up_ref, down_ref, r_ref, normed_ref, raised_ref):
@@ -635,7 +683,7 @@
 def ffn_forward(layer, hidden, gain, bias, w_up, w_down):
     length, width = hidden.shape
     inner = w_up.shape[2]
-    chunk = 768
+    chunk = inner // 4
     return pl.pallas_call(
         ffn_forward_body,
         grid=(inner // chunk,),
@@ -645,13 +693,11 @@
             pl.BlockSpec((None, chunk, width), lambda j: (layer, j, 0)),
         ],
         out_specs=[
-            whole((length, width)), whole((length, width)),
-            pl.BlockSpec((length, chunk), lambda j: (0, j)),
+            whole((length, width)), whole((length, width)), pl.BlockSpec((length, chunk), lambda j: (0, j)),
         ],
         out_shape=[
-            jax.ShapeDtypeStruct((length, width), jnp.float32),
-            jax.ShapeDtypeStruct((length, width), jnp.bfloat16),
-            jax.ShapeDtypeStruct((length, inner), jnp.bfloat16),
+            sds((length, width), jnp.float32), sds((length, width), jnp.bfloat16),
+            sds((length, inner), jnp.bfloat16),
         ],
         compiler_params=pltpu.CompilerParams(vmem_limit_bytes=60 * MIB),
         cost_estimate=pl.CostEstimate(
@@ -661,205 +707,508 @@
     )(hidden, gain, bias, w_up, w_down)
 
 
-def ffn_backward_body(
-    g_ref, hidden_ref, gain_ref, normed_ref, raised_ref, up_ref, down_ref, out_ref, grads_ref, gain_grad_ref,
-    bias_grad_ref, g16_ref, g16t_ref, normed_t_ref, total_ref,
-):
+def ffn_backward_body(carry, *refs):
+    refs = list(refs)
+    take = lambda n: [refs.pop(0) for _ in range(n)]
+    g_ref, hidden_ref, gain_ref, normed_ref, raised_ref, up_ref, down_ref = take(7)
+    zin_ref, min_ref = take(2) if carry else (None, None)
+    out_ref, gain_grad_ref, bias_grad_ref, c_out, w_out = take(5)
+    zfin_ref, wmix_ref = take(2) if carry else (None, None)
+    g16_ref, g16t_ref, normed_t_ref, give, got, c_ref, s1, core_s, core_r, s1_s, s1_r, out_sem = take(12)
+    if carry:
+        zgot, zown, mgot, mown, z_s, z_r, m_s, m_r, own_sem = take(9)
     j = pl.program_id(0)
+    steps = pl.num_programs(0)
     width = g_ref.shape[1]
+    place = Place()
+    half = c_ref.shape[1]
+    mcols = width // 2
+
+    def z_sends():
+        piece = [remote(zin_ref.at[:, (place.z + d) % place.depth], zgot.at[d - 1], z_s.at[d - 1], z_r.at[d - 1],
+                        place.over_z[d - 1]) for d in range(1, place.depth)]
+        return piece
+
+    def m_sends():
+        sends = []
+        for k in range(2):
+            sends.append(remote(min_ref.at[2 * k + 1 - place.x, :, pl.ds(0, mcols)], mgot.at[0, k], m_s.at[0, k],
+                                m_r.at[0, k], place.over_x))
+            sends.append(remote(min_ref.at[2 * (1 - place.y) + k, :, pl.ds(mcols, mcols)], mgot.at[1, k], m_s.at[1, k],
+                                m_r.at[1, k], place.over_y))
+        return sends
+
+    def own_copies():
+        copies = [pltpu.make_async_copy(zin_ref.at[:, place.z], zown, own_sem.at[4])]
+        for k in range(2):
+            copies.append(pltpu.make_async_copy(min_ref.at[2 * k + place.x, :, pl.ds(0, mcols)], mown.at[0, k],
+                                                own_sem.at[k]))
+            copies.append(pltpu.make_async_copy(min_ref.at[2 * place.y + k, :, pl.ds(mcols, mcols)], mown.at[1, k],
+                                                own_sem.at[2 + k]))
+        return copies
+
+    def core_send(slot):
+        return remote(give.at[slot], got.at[slot], core_s.at[slot], core_r.at[slot], place.over_core)
+
+    def s1_send(side, t):
+        device = place.over_x if side == 0 else place.over_y
+        return remote(c_ref.at[t, :, pl.ds(side * width, width)], s1.at[side], s1_s.at[side], s1_r.at[side], device)
+
+    def c_copy(t):
+        return pltpu.make_async_copy(c_ref.at[t], c_out.at[t], out_sem.at[t])
+
+    def finish(t, slot):
+        core_send(slot).wait_recv()
+        c_ref[t] = bf(f32(c_ref[t]) + f32(got[slot]))
+        c_copy(t).start()
 
     @pl.when(j == 0)
     def _():
+        greet([place.over_core, place.over_x, place.over_y] + (place.over_z if carry else []))
+        if carry:
+            for copy in z_sends() + m_sends() + own_copies():
+                copy.start()
         g16 = bf(g_ref[...])
         g16_ref[...] = g16
-        g16t_ref[...] = g16.T
-        normed_t_ref[...] = normed_ref[...].T
-        total_ref[...] = jnp.zeros_like(total_ref)
+        store_rows(place, g16t_ref, g16.T)
+        store_rows(place, normed_t_ref, normed_ref[...].T)
+        out_ref[...] = jnp.zeros_like(out_ref)
+
+    @pl.when(j == 1)
+    def _():
+        finish(0, 0)
+
+        @pl.when(place.x == 1)
+        def _():
+            s1_send(0, 0).start()
+
+        @pl.when(place.y == 1)
+        def _():
+            s1_send(1, 0).start()
+
+    @pl.when(j == 2)
+    def _():
+        finish(3, 1)
+
+        @pl.when(place.x == 0)
+        def _():
+            s1_send(0, 3).start()
+
+        @pl.when(place.y == 0)
+        def _():
+            s1_send(1, 3).start()
+
+    @pl.when(j == 3)
+    def _():
+        finish(2, 0)
 
     active, slope = gelu_parts(f32(raised_ref[...]))
+    active = bf(active)
     raised_grad = bf(mm_nt(g16_ref[...], down_ref[...]) * slope)
-    grads_ref[:, :width] = bf(mm(normed_t_ref[...], raised_grad))
-    grads_ref[:, width:] = bf(mm(g16t_ref[...], bf(active)))
-    total_ref[...] += mm_nt(raised_grad, up_ref[...])
-
-    @pl.when(j == pl.num_programs(0) - 1)
+    slot = j % 2
+
+    @pl.when(j >= 2)
     def _():
-        part, gain_grad, bias_grad = norm_backward(hidden_ref[...], f32(gain_ref[...]), total_ref[...])
+        core_send(slot).wait_send()
+
+    give[slot, :, :width] = bf(mm(normed_t_ref[:half], raised_grad))
+    give[slot, :, width:] = bf(mm(g16t_ref[:half], active))
+    core_send(slot).start()
+    t = (steps - j) % steps
+    c_ref[t, :, :width] = bf(mm(normed_t_ref[half:], raised_grad))
+    c_ref[t, :, width:] = bf(mm(g16t_ref[half:], active))
+    out_ref[...] += mm_nt(raised_grad, up_ref[...])
+
+    @pl.when(j == steps - 1)
+    def _():
+        part, gain_grad, bias_grad = norm_backward(hidden_ref[...], f32(gain_ref[...]), out_ref[...])
         out_ref[...] = g_ref[...] + part
         gain_grad_ref[...] = gain_grad
         bias_grad_ref[...] = bias_grad
-
-
-def ffn_backward(layer, g, hidden, gain, normed, raised, w_up, w_down):
+        finish(1, 1)
+        for k in range(2):
+            s1_send(k, 0).wait_recv()
+        w_out[0] = bf(f32(c_ref[3 * place.x, :, :width]) + f32(s1[0]))
+        w_out[1] = bf(f32(c_ref[3 * place.y, :, width:]) + f32(s1[1]))
+        if carry:
+            for copy in own_copies():
+                copy.wait()
+            for copy in z_sends() + m_sends():
+                copy.wait()
+            total = f32(zown[...])
+            for d in range(place.depth - 1):
+                total += f32(zgot[d])
+            zfin_ref[...] = total
+            for side in range(2):
+                for k in range(2):
+                    wmix_ref[side, k] = bf(f32(mown[side, k]) + f32(mgot[side, k]))
+        for k in range(2):
+            s1_send(k, 0).wait_send()
+            core_send(k).wait_send()
+        for k in range(steps):
+            c_copy(k).wait()
+
+
+def ffn_backward(layer, carry, collective, g, hidden, gain, normed, raised, w_up, w_down, *carried):
     length, width = g.shape
     inner = w_up.shape[2]
-    chunk = 768
-    steps = inner // chunk
+    chunk = inner // 4
+    depth = lax.axis_size("seq") // 2
+    piece = width // (2 * depth)
+    half = depth * piece
+    b16, b32, dma = jnp.bfloat16, jnp.float32, pltpu.SemaphoreType.DMA
+    order = lambda j: (4 - j) % 4
     return pl.pallas_call(
-        ffn_backward_body,
-        grid=(steps,),
+        lambda *refs: ffn_backward_body(carry, *refs),
+        grid=(4,),
         in_specs=[
             whole((length, width)), whole((length, width)), of_layer(layer, (1, width)), whole((length, width)),
-            pl.BlockSpec((length, chunk), lambda j: (0, j)),
-            pl.BlockSpec((None, width, chunk), lambda j: (layer, 0, j)),
-            pl.BlockSpec((None, chunk, width), lambda j: (layer, j, 0)),
-        ],
-        out_specs=[
-            whole((length, width)),
-            pl.BlockSpec((None, width, 2 * chunk), lambda j: (j, 0, 0)),
-            whole((1, width)), whole((1, width)),
-        ],
+            pl.BlockSpec((length, chunk), lambda j: (0, order(j))),
+            pl.BlockSpec((None, width, chunk), lambda j: (layer, 0, order(j))),
+            pl.BlockSpec((None, chunk, width), lambda j: (layer, order(j), 0)),
+        ] + [ANY] * len(carried),
+        out_specs=[whole((length, width)), whole((1, width)), whole((1, width)), ANY, whole((2, half, width))]
+        + ([whole((2, piece, width)), whole((2, 2, half, width // 2))] if carry else []),
         out_shape=[
-            jax.ShapeDtypeStruct((length, width), jnp.float32),
-            jax.ShapeDtypeStruct((steps, width, 2 * chunk), jnp.bfloat16),
-            jax.ShapeDtypeStruct((1, width), jnp.float32),
-            jax.ShapeDtypeStruct((1, width), jnp.float32),
-        ],
+            sds((length, width), b32), sds((1, width), b32), sds((1, width), b32), sds((4, half, 2 * chunk), b16),
+            sds((2, half, chunk), b16),
+        ] + ([sds((2, piece, chunk), b32), sds((2, 2, half, width // 2), b16)] if carry else []),
         scratch_shapes=[
-            pltpu.VMEM((length, width), jnp.bfloat16), pltpu.VMEM((width, length), jnp.bfloat16),
-            pltpu.VMEM((width, length), jnp.bfloat16), pltpu.VMEM((length, width), jnp.float32),
-        ],
-        compiler_params=pltpu.CompilerParams(vmem_limit_bytes=60 * MIB),
+            pltpu.VMEM((length, width), b16), pltpu.VMEM((width, length), b16), pltpu.VMEM((width, length), b16),
+            pltpu.VMEM((2, half, 2 * chunk), b16), pltpu.VMEM((2, half, 2 * chunk), b16),
+            pltpu.VMEM((4, half, 2 * chunk), b16), pltpu.VMEM((2, half, chunk), b16),
+            dma((2,)), dma((2,)), dma((2,)), dma((2,)), dma((4,)),
+        ] + ([
+            pltpu.VMEM((depth - 1, 2, piece, chunk), b16), pltpu.VMEM((2, piece, chunk), b16),
+            pltpu.VMEM((2, 2, half, width // 2), b16), pltpu.VMEM((2, 2, half, width // 2), b16),
+            dma((depth - 1,)), dma((depth - 1,)), dma((2, 2)), dma((2, 2)), dma((5,)),
+        ] if carry else []),
+        compiler_params=pltpu.CompilerParams(
+            vmem_limit_bytes=62 * MIB, collective_id=collective, has_side_effects=True
+        ),
         cost_estimate=pl.CostEstimate(
             flops=8 * length * width * inner, bytes_accessed=40 * MIB, transcendentals=length * inner
         ),
         name="ffn_backward",
-    )(g, hidden, gain, normed, raised, w_up, w_down)
-
-
-def mixer_backward_body(
-    hg_ref, r_ref, gain_ref, normed_ref, proj_ref, k0_ref, k1_ref, k2_ref, signal_ref, long_ref, taps_ref, skip_ref,
-    table_ref, back_ref, wo_ref, w0_ref, w1_ref, w2_ref,
-    g_ref, grad_out_ref, grad_in_ref, taps_grad_ref, short_grad_ref, skip_grad_ref, gain_grad_ref, bias_grad_ref,
-    og_ref, normed_t_ref, total_ref,
-):
+    )(g, hidden, gain, normed, raised, w_up, w_down, *carried)
+
+
+def mixer_backward_body(carry, *refs):
+    refs = list(refs)
+    take = lambda n: [refs.pop(0) for _ in range(n)]
+    (hg_ref, r_ref, gain_ref, normed_ref, proj_ref, k0_ref, k1_ref, k2_ref, signal_ref, long_ref, taps_ref, skip_ref,
+     table_ref, wo_ref, w0_ref, w1_ref, w2_ref, c_in, w1_in) = take(19)
+    wmix_ref = take(1)[0] if carry else None
+    (g_ref, c_out, zout_ref, taps_grad_ref, short_grad_ref, skip_grad_ref, gain_grad_ref, bias_grad_ref) = take(8)
+    mfin_ref = take(1)[0] if carry else None
+    (og_ref, left_t, gated_ref, pg_ref, give, got, s1, wkeep, s2, core_s, core_r, s1_s, s1_r, s2_s, s2_r, own_sem,
+     out_sem) = take(17)
+    if carry:
+        mkeep, m2, mz, mzgot, m2_s, m2_r, mz_s, mz_r, m_sem = take(9)
     j = pl.program_id(0)
-    length = hg_ref.shape[0]
+    steps = pl.num_programs(0)
+    length, width = hg_ref.shape
+    place = Place()
+    half = give.shape[1]
+    piece = half // place.depth
+    x, y = place.x, place.y
+
+    def s1_sends():
+        return [
+            remote(c_in.at[1 + x, :, pl.ds(0, width)], s1.at[0], s1_s.at[0], s1_r.at[0], place.over_x),
+            remote(c_in.at[2 - y, :, pl.ds(width, width)], s1.at[1], s1_s.at[1], s1_r.at[1], place.over_y),
+        ]
+
+    def own_copies():
+        return [
+            pltpu.make_async_copy(w1_in.at[0], wkeep.at[0, x], own_sem.at[0]),
+            pltpu.make_async_copy(w1_in.at[1], wkeep.at[1, y], own_sem.at[1]),
+            pltpu.make_async_copy(c_in.at[2 - x, :, pl.ds(0, width)], wkeep.at[0, 1 - x], own_sem.at[2]),
+            pltpu.make_async_copy(c_in.at[1 + y, :, pl.ds(width, width)], wkeep.at[1, 1 - y], own_sem.at[3]),
+        ]
+
+    def s2_sends():
+        return [
+            remote(wkeep.at[0, 1 - y], s2.at[0], s2_s.at[0], s2_r.at[0], place.over_y),
+            remote(wkeep.at[1, 1 - x], s2.at[1], s2_s.at[1], s2_r.at[1], place.over_x),
+        ]
+
+    def m2_sends():
+        return [
+            remote(wmix_ref.at[0, 1 - y], m2.at[0], m2_s.at[0], m2_r.at[0], place.over_y),
+            remote(wmix_ref.at[1, 1 - x], m2.at[1], m2_s.at[1], m2_r.at[1], place.over_x),
+        ]
+
+    def m_copies():
+        return [
+            pltpu.make_async_copy(wmix_ref.at[0, y], mkeep.at[0], m_sem.at[0]),
+            pltpu.make_async_copy(wmix_ref.at[1, x], mkeep.at[1], m_sem.at[1]),
+        ]
+
+    def mz_sends():
+        return [
+            remote(mz.at[:, (place.z + d) % place.depth], mzgot.at[d - 1], mz_s.at[d - 1], mz_r.at[d - 1],
+                   place.over_z[d - 1])
+            for d in range(1, place.depth)
+        ]
+
+    def core_send(t):
+        return remote(give.at[t], got.at[t], core_s.at[t], core_r.at[t], place.over_core)
+
+    def c_copy(t):
+        return pltpu.make_async_copy(got.at[t], c_out.at[t], out_sem.at[t])
 
     @pl.when(j == 0)
     def _():
+        greet([place.over_core, place.over_x, place.over_y] + (place.over_z if carry else []))
+        for copy in s1_sends() + own_copies():
+            copy.start()
+        if carry:
+            for copy in m2_sends() + m_copies():
+                copy.start()
         og_ref[...] = bf(hg_ref[...])
-        normed_t_ref[...] = normed_ref[...].T
-        total_ref[...] = jnp.zeros_like(total_ref)
-
-    proj = [f32(proj_ref[p]) for p in range(3)]
-    kernel = [f32(k_ref[...]) for k_ref in (k0_ref, k1_ref, k2_ref)]
-    gate_out, gate_in, vals = mixed_chunk(proj, kernel)
-    carried = vals * gate_in
-    long_out = f32(long_ref[...])
-    skip = f32(skip_ref[...])
-    og = og_ref[...]
-    grad_out_ref[...] = bf(mm(bf(long_out * gate_out).T, og))
-    gated_grad = mm_nt(og, wo_ref[...])
-    long_grad = gated_grad * gate_out
-    skip_grad_ref[...] = jnp.sum(carried * long_grad, axis=0, keepdims=True)
-    both = mm(table_ref[...], bf(long_grad))
-    up_re, up_im = both[:length], both[length:]
-    tap_re, tap_im = f32(taps_ref[:length]), f32(taps_ref[length:])
-    out = mm(back_ref[:, :length], bf(up_re * tap_re + up_im * tap_im))
-    out += mm(back_ref[:, length:], bf(up_im * tap_re - up_re * tap_im))
-    carried_grad = out + skip * long_grad
-    sig_re, sig_im = f32(signal_ref[:length]), f32(signal_ref[length:])
-    cross = mm(back_ref[:, :length], bf(up_re * sig_re + up_im * sig_im))
-    cross += mm(back_ref[:, length:], bf(up_im * sig_re - up_re * sig_im))
-    taps_grad_ref[...] = cross * (1.0 / length)
-    for p, part in enumerate((gated_grad * long_out, carried_grad * vals, carried_grad * gate_in)):
-        one, two = row_shift(part, -1), row_shift(part, -2)
-        projected_grad = bf(kernel[p][2:3] * part + kernel[p][1:2] * one + kernel[p][0:1] * two)
-        for tap, moved in enumerate((two, one, part)):
-            short_grad_ref[p, tap : tap + 1, :] = jnp.sum(moved * proj[p], axis=0, keepdims=True)
-        grad_in_ref[p] = bf(mm(normed_t_ref[...], projected_grad))
-        total_ref[...] += mm_nt(projected_grad, (w0_ref, w1_ref, w2_ref)[p][...])
-
-    @pl.when(j == pl.num_programs(0) - 1)
+        g_ref[...] = jnp.zeros_like(g_ref)
+
+    if carry:
+        @pl.when(j == 1)
+        def _():
+            for copy in m2_sends() + m_copies():
+                copy.wait()
+            for side in range(2):
+                total = bf(f32(mkeep[side]) + f32(m2[side]))
+                for k in range(place.depth):
+                    mz[side, k] = total[k * piece : (k + 1) * piece]
+            for copy in mz_sends():
+                copy.start()
+
+    @pl.when(j == 2)
     def _():
-        part, gain_grad, bias_grad = norm_backward(r_ref[...], f32(gain_ref[...]), total_ref[...])
+        for copy in s1_sends() + own_copies():
+            copy.wait()
+        wkeep[0, 1 - x] = bf(f32(wkeep[0, 1 - x]) + f32(s1[0]))
+        wkeep[1, 1 - y] = bf(f32(wkeep[1, 1 - y]) + f32(s1[1]))
+        for copy in s2_sends():
+            copy.start()
+
+    @pl.when(j < steps - 1)
+    def _():
+        chunk = long_ref.shape[1]
+        proj = [f32(proj_ref[p]) for p in range(3)]
+        kernel = [f32(k_ref[...]) for k_ref in (k0_ref, k1_ref, k2_ref)]
+        gate_out, gate_in, vals = mixed_chunk(proj, kernel)
+        carried = vals * gate_in
+        long_out = f32(long_ref[...])
+        skip = f32(skip_ref[...])
+        gated_ref[:, pl.ds(pl.multiple_of(j * chunk, chunk), chunk)] = bf(long_out * gate_out)
+        gated_grad = mm_nt(og_ref[...], wo_ref[...])
+        long_grad = gated_grad * gate_out
+        skip_grad_ref[...] = jnp.sum(carried * long_grad, axis=0, keepdims=True)
+        both = mm(table_ref[...], bf(long_grad))
+        up_re, up_im = both[:length], both[length:]
+        tap_re, tap_im = f32(taps_ref[:length]), f32(taps_ref[length:])
+        out = mm_tn(table_ref[:length], bf(up_re * tap_re + up_im * tap_im))
+        out += mm_tn(table_ref[length:], bf(up_im * tap_re - up_re * tap_im))
+        carried_grad = out + skip * long_grad
+        sig_re, sig_im = f32(signal_ref[:length]), f32(signal_ref[length:])
+        cross = mm_tn(table_ref[:length], bf(up_re * sig_re + up_im * sig_im))
+        cross += mm_tn(table_ref[length:], bf(up_im * sig_re - up_re * sig_im))
+        taps_grad_ref[...] = cross * (1.0 / length)
+        upstream = None
+        for p, part in enumerate((gated_grad * long_out, carried_grad * vals, carried_grad * gate_in)):
+            one, two = row_shift(part, -1), row_shift(part, -2)
+            projected_grad = bf(kernel[p][2:3] * part + kernel[p][1:2] * one + kernel[p][0:1] * two)
+            for tap, moved in enumerate((two, one, part)):
+                short_grad_ref[p, tap : tap + 1, :] = jnp.sum(moved * proj[p], axis=0, keepdims=True)
+            pg_ref[:, pl.ds(pl.multiple_of(p * width + j * chunk, chunk), chunk)] = projected_grad
+            term = mm_nt(projected_grad, (w0_ref, w1_ref, w2_ref)[p][...])
+            upstream = term if upstream is None else upstream + term
+        g_ref[...] += upstream
+
+    @pl.when(j == steps - 1)
+    def _():
+        in_cols, out_cols = 3 * width // 4, width // 4
+        store_rows(place, left_t.at[0], normed_ref[...].T)
+        store_rows(place, left_t.at[1], gated_ref[...].T)
+        for t in range(4):
+            rights = pg_ref[:, in_cols * t : in_cols * (t + 1)], og_ref[:, out_cols * t : out_cols * (t + 1)]
+            give[t, :, :in_cols] = bf(mm(left_t[0, :half], rights[0]))
+            give[t, :, in_cols:] = bf(mm(left_t[1, :half], rights[1]))
+            core_send(t).start()
+        part, gain_grad, bias_grad = norm_backward(r_ref[...], f32(gain_ref[...]), g_ref[...])
         g_ref[...] = hg_ref[...] + part
         gain_grad_ref[...] = gain_grad
         bias_grad_ref[...] = bias_grad
-
-
-def mixer_backward(layer, hidden_grad, r, gain, normed, proj, short_w, signal, long_out, taps, skip, table, back, w_out, w_in):
+        for t in range(4):
+            rights = pg_ref[:, in_cols * t : in_cols * (t + 1)], og_ref[:, out_cols * t : out_cols * (t + 1)]
+            core_send(t).wait()
+            got[t, :, :in_cols] = bf(mm(left_t[0, half:], rights[0]) + f32(got[t, :, :in_cols]))
+            got[t, :, in_cols:] = bf(mm(left_t[1, half:], rights[1]) + f32(got[t, :, in_cols:]))
+            c_copy(t).start()
+        if carry:
+            for copy in mz_sends():
+                copy.wait()
+            for side in range(2):
+                total = f32(mz[side, place.z])
+                for d in range(place.depth - 1):
+                    total += f32(mzgot[d, side])
+                mfin_ref[side] = total
+        for copy in s2_sends():
+            copy.wait()
+        for side, keep in enumerate((y, x)):
+            total = bf(f32(wkeep[side, keep]) + f32(s2[side]))
+            for k in range(place.depth):
+                zout_ref[side, k] = total[k * piece : (k + 1) * piece]
+        for t in range(4):
+            c_copy(t).wait()
+
+
+def mixer_backward(
+    layer, carry, collective, hidden_grad, r, gain, normed, proj, short_w, signal, long_out, taps, skip, table, w_out,
+    w_in, ffn_c, ffn_w, *carried
+):
     length, width = r.shape
     chunk = 256
     steps = width // chunk
-    third = lambda p: pl.BlockSpec((None, width, chunk), lambda j: (layer, 0, p * steps + j))
-    short = lambda p: pl.BlockSpec((None, 3, chunk), lambda j: (layer, 0, p * steps + j))
+    depth = lax.axis_size("seq") // 2
+    piece = width // (2 * depth)
+    half = depth * piece
+    at = lambda j: jnp.minimum(j, steps - 1)
+    third = lambda p: pl.BlockSpec((None, width, chunk), lambda j: (layer, 0, p * steps + at(j)))
+    short = lambda p: pl.BlockSpec((None, 3, chunk), lambda j: (layer, 0, p * steps + at(j)))
+    b16, b32, dma = jnp.bfloat16, jnp.float32, pltpu.SemaphoreType.DMA
     return pl.pallas_call(
-        mixer_backward_body,
-        grid=(steps,),
+        lambda *refs: mixer_backward_body(carry, *refs),
+        grid=(steps + 1,),
         in_specs=[
             whole((length, width)), whole((length, width)), of_layer(layer, (1, width)), whole((length, width)),
-            pl.BlockSpec((3, length, chunk), lambda j: (0, 0, j)),
+            pl.BlockSpec((3, length, chunk), lambda j: (0, 0, at(j))),
             short(0), short(1), short(2),
-            pl.BlockSpec((2 * length, chunk), lambda j: (0, j)),
-            pl.BlockSpec((length, chunk), lambda j: (0, j)),
-            pl.BlockSpec((2 * length, chunk), lambda j: (0, j)),
-            pl.BlockSpec((None, 1, chunk), lambda j: (layer, 0, j)),
-            whole((2 * length, length)), whole((length, 2 * length)),
-            pl.BlockSpec((None, chunk, width), lambda j: (layer, j, 0)),
+            pl.BlockSpec((2 * length, chunk), lambda j: (0, at(j))),
+            pl.BlockSpec((length, chunk), lambda j: (0, at(j))),
+            pl.BlockSpec((2 * length, chunk), lambda j: (0, at(j))),
+            pl.BlockSpec((None, 1, chunk), lambda j: (layer, 0, at(j))),
+            whole((2 * length, length)),
+            pl.BlockSpec((None, chunk, width), lambda j: (layer, at(j), 0)),
             third(0), third(1), third(2),
-        ],
+        ] + [ANY] * (2 + len(carried)),
         out_specs=[
-            whole((length, width)),
-            pl.BlockSpec((chunk, width), lambda j: (j, 0)),
-            pl.BlockSpec((3, width, chunk), lambda j: (0, 0, j)),
-            pl.BlockSpec((length, chunk), lambda j: (0, j)),
-            pl.BlockSpec((3, 3, chunk), lambda j: (0, 0, j)),
-            pl.BlockSpec((1, chunk), lambda j: (0, j)),
+            whole((length, width)), ANY, whole((2, depth, piece, width)),
+            pl.BlockSpec((length, chunk), lambda j: (0, at(j))),
+            pl.BlockSpec((3, 3, chunk), lambda j: (0, 0, at(j))),
+            pl.BlockSpec((1, chunk), lambda j: (0, at(j))),
             whole((1, width)), whole((1, width)),
-        ],
+        ] + ([whole((2, piece, width // 2))] if carry else []),
         out_shape=[
-            jax.ShapeDtypeStruct((length, width), jnp.float32),
-            jax.ShapeDtypeStruct((width, width), jnp.bfloat16),
-            jax.ShapeDtypeStruct((3, width, width), jnp.bfloat16),
-            jax.ShapeDtypeStruct((length, width), jnp.float32),
-            jax.ShapeDtypeStruct((3, 3, width), jnp.float32),
-            jax.ShapeDtypeStruct((1, width), jnp.float32),
-            jax.ShapeDtypeStruct((1, width), jnp.float32),
-            jax.ShapeDtypeStruct((1, width), jnp.float32),
-        ],
+            sds((length, width), b32), sds((4, half, width), b16), sds((2, depth, piece, width), b16),
+            sds((length, width), b32), sds((3, 3, width), b32), sds((1, width), b32), sds((1, width), b32),
+            sds((1, width), b32),
+        ] + ([sds((2, piece, width // 2), b32)] if carry else []),
         scratch_shapes=[
-            pltpu.VMEM((length, width), jnp.bfloat16), pltpu.VMEM((width, length), jnp.bfloat16),
-            pltpu.VMEM((length, width), jnp.float32),
-        ],
-        compiler_params=pltpu.CompilerParams(vmem_limit_bytes=62 * MIB),
+            pltpu.VMEM((length, width), b16), pltpu.VMEM((2, width, length), b16), pltpu.VMEM((length, width), b16),
+            pltpu.VMEM((length, 3 * width), b16), pltpu.VMEM((4, half, width), b16), pltpu.VMEM((4, half, width), b16),
+            pltpu.VMEM((2, half, width), b16), pltpu.VMEM((2, 2, half, width), b16), pltpu.VMEM((2, half, width), b16),
+            dma((4,)), dma((4,)), dma((2,)), dma((2,)), dma((2,)), dma((2,)), dma((4,)), dma((4,)),
+        ] + ([
+            pltpu.VMEM((2, half, width // 2), b16), pltpu.VMEM((2, half, width // 2), b16),
+            pltpu.VMEM((2, depth, piece, width // 2), b16), pltpu.VMEM((depth - 1, 2, piece, width // 2), b16),
+            dma((2,)), dma((2,)), dma((depth - 1,)), dma((depth - 1,)), dma((2,)),
+        ] if carry else []),
+        compiler_params=pltpu.CompilerParams(
+            vmem_limit_bytes=63 * MIB, collective_id=collective, has_side_effects=True
+        ),
         cost_estimate=pl.CostEstimate(
             flops=2 * length * width * (8 * width + 6 * length), bytes_accessed=50 * MIB, transcendentals=0
         ),
         name="mixer_backward",
-    )(hidden_grad, r, gain, normed, proj, short_w, short_w, short_w, signal, long_out, taps, skip, table, back, w_out,
-      w_in, w_in, w_in)
-
-
-def swapped(block, axis, flip):
-    return lax.ppermute(block, axis, [(i, i ^ flip) for i in range(lax.axis_size(axis))])
-
-
-def pick(block, index, dim):
-    return lax.dynamic_index_in_dim(block, index, dim, keepdims=False)
-
-
-def halved(block, axis, flip, bit, dim):
-    return pick(block, bit, dim) + swapped(pick(block, 1 - bit, dim), axis, flip)
-
-
-def reduce_scatter(block):
-    toks, seqs, rows, columns = block.shape
-    s, t = lax.axis_index("seq"), lax.axis_index("tok")
-    z, core, y, x = s // 2, s % 2, t // 2, t % 2
-    block = halved(block.reshape(2, 2, seqs // 2, 2, rows, columns), "seq", 1, core, 3)
-    left, right = block[..., : columns // 2], block[..., columns // 2 :]
-    left = halved(left, "tok", 1, x, 1)
-    right = halved(right, "tok", 2, y, 0)
-    left = halved(left, "tok", 2, y, 0)
-    right = halved(right, "tok", 1, x, 0)
-    block = jnp.concatenate([left, right], axis=-1)
-    total = f32(pick(block, z, 0))
-    for step in range(1, seqs // 2):
-        sent = pick(block, (z + step) % (seqs // 2), 0)
-        total += f32(lax.ppermute(sent, "seq", [(i, (i + 2 * step) % seqs) for i in range(seqs)]))
-    return total
+    )(hidden_grad, r, gain, normed, proj, short_w, short_w, short_w, signal, long_out, taps, skip, table, w_out,
+      w_in, w_in, w_in, ffn_c, ffn_w, *carried)
+
+
+def last_sums_body(z_in, c_in, zfin_ref, mfin_ref, zgot, zown, mgot, w, m2, mz, mzgot, z_s, z_r, m_s, m_r, m2_s, m2_r,
+                   mz_s, mz_r, own_sem):
+    place = Place()
+    x, y = place.x, place.y
+    cols = w.shape[3]
+    piece = zown.shape[1]
+    greet([place.over_x, place.over_y] + place.over_z)
+    m_sends = []
+    for k in range(2):
+        m_sends.append(remote(c_in.at[2 * k + 1 - x, :, pl.ds(0, cols)], mgot.at[0, k], m_s.at[0, k], m_r.at[0, k],
+                              place.over_x))
+        m_sends.append(remote(c_in.at[2 * (1 - y) + k, :, pl.ds(cols, cols)], mgot.at[1, k], m_s.at[1, k],
+                              m_r.at[1, k], place.over_y))
+    z_sends = [
+        remote(z_in.at[:, (place.z + d) % place.depth], zgot.at[d - 1], z_s.at[d - 1], z_r.at[d - 1],
+               place.over_z[d - 1])
+        for d in range(1, place.depth)
+    ]
+    own = [pltpu.make_async_copy(z_in.at[:, place.z], zown, own_sem.at[4])]
+    for k in range(2):
+        own.append(pltpu.make_async_copy(c_in.at[2 * k + x, :, pl.ds(0, cols)], w.at[0, k], own_sem.at[k]))
+        own.append(pltpu.make_async_copy(c_in.at[2 * y + k, :, pl.ds(cols, cols)], w.at[1, k], own_sem.at[2 + k]))
+    for copy in m_sends + z_sends + own:
+        copy.start()
+    for copy in own + m_sends:
+        copy.wait()
+    for side in range(2):
+        for k in range(2):
+            w[side, k] = bf(f32(w[side, k]) + f32(mgot[side, k]))
+    m2_sends = [
+        remote(w.at[0, 1 - y], m2.at[0], m2_s.at[0], m2_r.at[0], place.over_y),
+        remote(w.at[1, 1 - x], m2.at[1], m2_s.at[1], m2_r.at[1], place.over_x),
+    ]
+    for copy in m2_sends:
+        copy.start()
+    for copy in m2_sends:
+        copy.wait()
+    for side, keep in enumerate((y, x)):
+        total = bf(f32(w[side, keep]) + f32(m2[side]))
+        for k in range(place.depth):
+            mz[side, k] = total[k * piece : (k + 1) * piece]
+    mz_sends = [
+        remote(mz.at[:, (place.z + d) % place.depth], mzgot.at[d - 1], mz_s.at[d - 1], mz_r.at[d - 1],
+               place.over_z[d - 1])
+        for d in range(1, place.depth)
+    ]
+    for copy in mz_sends:
+        copy.start()
+    for copy in z_sends:
+        copy.wait()
+    total = f32(zown[...])
+    for d in range(place.depth - 1):
+        total += f32(zgot[d])
+    zfin_ref[...] = total
+    for copy in mz_sends:
+        copy.wait()
+    for side in range(2):
+        total = f32(mz[side, place.z])
+        for d in range(place.depth - 1):
+            total += f32(mzgot[d, side])
+        mfin_ref[side] = total
+
+
+def last_sums(collective, ffn_z, mixer_c):
+    _, depth, piece, width = ffn_z.shape
+    half = depth * piece
+    b16, dma = jnp.bfloat16, pltpu.SemaphoreType.DMA
+    cols = width // 2
+    return pl.pallas_call(
+        last_sums_body,
+        in_specs=[ANY, ANY],
+        out_specs=[pl.BlockSpec(memory_space=pltpu.VMEM)] * 2,
+        out_shape=[sds((2, piece, width), jnp.float32), sds((2, piece, cols), jnp.float32)],
+        scratch_shapes=[
+            pltpu.VMEM((depth - 1, 2, piece, width), b16), pltpu.VMEM((2, piece, width), b16),
+            pltpu.VMEM((2, 2, half, cols), b16), pltpu.VMEM((2, 2, half, cols), b16), pltpu.VMEM((2, half, cols), b16),
+            pltpu.VMEM((2, depth, piece, cols), b16), pltpu.VMEM((depth - 1, 2, piece, cols), b16),
+            dma((depth - 1,)), dma((depth - 1,)), dma((2, 2)), dma((2, 2)), dma((2,)), dma((2,)), dma((depth - 1,)),
+            dma((depth - 1,)), dma((5,)),
+        ],
+        compiler_params=pltpu.CompilerParams(
+            vmem_limit_bytes=40 * MIB, collective_id=collective, has_side_effects=True
+        ),
+        name="last_sums",
+    )(ffn_z, mixer_c)
 
 
 def whole_sequences(
@@ -869,7 +1218,7 @@
     micro_count, cap_size, tok_rows, width = x_in.shape
     slots = micro_count * cap_size
     layers, _, inner = w_up.shape
-    toks, seqs = lax.axis_size("tok"), lax.axis_size("seq")
+    toks = lax.axis_size("tok")
     length = tok_rows * toks
     me = lax.axis_index("tok")
 
@@ -883,7 +1232,6 @@
 
     live = (me % cap_size < counts[me // cap_size, 0]).astype(jnp.float32)
     table = jnp.asarray(spectral_table(length))
-    table_back = jnp.asarray(np.ascontiguousarray(spectral_table(length).T))
     features = position_features(length)
     envelope = decay_table(features[:, :1], 0.0, width, width)
     rowed = lambda v: v.reshape(layers, 1, v.shape[1])
@@ -903,7 +1251,7 @@
     kept = []
     for layer in range(layers):
         hidden, normed, proj, signal, long_out = mixer_forward(
-            layer, r, g1, b1, w_in, short_w, table, table_back, spectra[layer], skip, w_out
+            layer, r, g1, b1, w_in, short_w, table, spectra[layer], skip, w_out
         )
         result, normed_two, raised = ffn_forward(layer, hidden, g2, b2, w_up, w_down)
         kept.append((r, hidden, normed, proj, signal, long_out, normed_two, raised))
@@ -911,29 +1259,38 @@
     out_act = f32(scatter_back(bf(r * live)))
 
     grad = f32(upstream) * live
-    mats = [None] * layers
     vecs = [None] * layers
+    carried_ffn, carried_mixer = (), ()
+    done = {}
     for layer in reversed(range(layers)):
         r, hidden, normed, proj, signal, long_out, normed_two, raised = kept[layer]
-        grad, ffn_grads, grad_g2, grad_b2 = ffn_backward(layer, grad, hidden, g2, normed_two, raised, w_up, w_down)
-        ffn_done = reduce_scatter(ffn_grads.reshape(toks, seqs, width // seqs, -1))
-        grad, grad_out, grad_in_proj, taps_grad, grad_short, grad_skip, grad_g1, grad_b1 = mixer_backward(
-            layer, grad, r, g1, normed, proj, short_w, signal, long_out, spectra[layer], skip, table, table_back,
-            w_out, w_in,
-        )
-        in_cols = jnp.swapaxes(grad_in_proj, 0, 1).reshape(width, toks, -1)
-        mixer_grads = jnp.concatenate([in_cols, grad_out.reshape(width, toks, -1)], axis=2)
-        mixer_done = reduce_scatter(jnp.swapaxes(mixer_grads, 0, 1).reshape(toks, seqs, width // seqs, -1))
-        split = in_cols.shape[2]
-        mats[layer] = (
-            mixer_done[:, :split], mixer_done[:, split:], ffn_done[:, : inner // toks],
-            ffn_done[:, inner // toks :].T,
-        )
+        carry = layer < layers - 1
+        grad, grad_g2, grad_b2, ffn_c, ffn_w, *rest = ffn_backward(
+            layer, carry, 2 * layer, grad, hidden, g2, normed_two, raised, w_up, w_down, *carried_ffn
+        )
+        if carry:
+            done["ffn", layer + 1] = rest[0]
+            carried_mixer = (rest[1],)
+        grad, mixer_c, ffn_z, taps_grad, grad_short, grad_skip, grad_g1, grad_b1, *rest = mixer_backward(
+            layer, carry, 2 * layer + 1, grad, r, g1, normed, proj, short_w, signal, long_out, spectra[layer], skip,
+            table, w_out, w_in, ffn_c, ffn_w, *carried_mixer,
+        )
+        if carry:
+            done["mixer", layer + 1] = rest[0]
+        carried_ffn = (ffn_z, mixer_c)
         filter_grads = filters[layer][1](taps_grad)
         short = jnp.swapaxes(grad_short, 0, 1).reshape(3, 3 * width)
         vecs[layer] = (grad_g1[0], grad_b1[0], short, grad_skip[0], grad_g2[0], grad_b2[0]) + tuple(filter_grads)
     grad_in = f32(scatter_back(bf(grad)))
-    mat_done = [jnp.stack([mats[layer][m] for layer in range(layers)]) for m in range(4)]
+    done["ffn", 0], done["mixer", 0] = last_sums(2 * layers, *carried_ffn)
+    split = 3 * width // toks
+    both = [jnp.concatenate([done["mixer", layer][0], done["mixer", layer][1]], axis=1) for layer in range(layers)]
+    mat_done = (
+        jnp.stack([b[:, :split] for b in both]),
+        jnp.stack([b[:, split:] for b in both]),
+        jnp.stack([done["ffn", layer][0] for layer in range(layers)]),
+        jnp.stack([done["ffn", layer][1].T for layer in range(layers)]),
+    )
     small = lax.psum(
         tuple(jnp.stack([vecs[layer][m] for layer in range(layers)]) for m in range(10)), ("seq", "tok")
     )

time: 748 us -> 681 us (0.910)
  Pallas kernels: 248 us -> 340 us
  local copies, waits for them, and re-layouts: 62.9 us -> 15.9 us
  starting transfers between devices: 59.6 us -> 18.3 us
  waiting for transfers between devices: 255 us -> 215 us
  other arithmetic: 49.2 us -> 22.7 us
    ppermute x32 -> x0, waiting for transfers between devices: 130 us -> none  [the longest x20 88.3 us: swapped(): lax.ppermute(block, axis, [(i, i ^ flip) for i in range(lax.axis_size(axi...]
    pallas_call x4 -> x5, Pallas kernels: 154 us -> 248 us  [the longest x2 116 us: mixer_backward(): pl.pallas_call(lambda *refs: mixer_backward_body(carry, *refs), grid=(ste...]
    psum x2, waiting for transfers between devices: 126 us -> 215 us  [whole_sequences(): lax.psum(tuple((jnp.stack([vecs[layer][m] for layer in range(layers)]) fo...]
    ppermute x32 -> x0, starting transfers between devices: 41 us -> none  [the longest x12 21.3 us: reduce_scatter(): lax.ppermute(sent, 'seq', [(i, (i + 2 * step) % seqs) for i in range(seqs)])]
    transpose x4 -> x0, local copies, waits for them, and re-layouts: 22 us -> none  [the longest x2 13.4 us: whole_sequences(): jnp.swapaxes(mixer_grads, 0, 1).reshape(toks, seqs, width // seqs, -1)]
    squeeze x20 -> x2, local copies, waits for them, and re-layouts: 19.7 us -> 0.04 us  [whole_sequences(): done['mixer', layer][0]]
    add x24 -> x0, other arithmetic: 14.7 us -> none  [the longest x20 14.2 us: halved(): pick(block, bit, dim) + swapped(pick(block, 1 - bit, dim), axis, flip)]
  transfers between devices with their start and end apart: 38 -> 6, of which waited for: 19 -> 2; matrix products, arithmetic and copies ran while one was open for 21% -> 8% of each run, Pallas kernels for 34% -> 19%
where the time goes in v3:
time: 681 us; the launch traced here: 674 us
  Pallas kernels  340 us (50%)
  waiting for transfers between devices  215 us (32%)
  matrix products  46.5 us (7%)
  other arithmetic  22.7 us (3%)
  starting transfers between devices  18.3 us (3%)
  local copies, waits for them, and re-layouts  15.9 us (2%)
  between operations  15.8 us (2%)
    psum x2, waiting for transfers between devices, whole_sequences(): lax.psum(tuple((jnp.stack([vecs[layer][m] for layer in range(layers)]) fo...  215 us
    pallas_call x2, Pallas kernels, mixer_backward(): pl.pallas_call(lambda *refs: mixer_backward_body(carry, *refs), grid=(ste...  116 us
    pallas_call x2, Pallas kernels, ffn_backward(): pl.pallas_call(lambda *refs: ffn_backward_body(carry, *refs), grid=(4,),...  92.9 us
    pallas_call x2, Pallas kernels, mixer_forward(): pl.pallas_call(mixer_forward_body, grid=(steps,), in_specs=[whole((length...  56.9 us
    pallas_call x1, Pallas kernels, last_sums(): pl.pallas_call(last_sums_body, in_specs=[ANY, ANY], out_specs=[pl.BlockSp...  39.5 us
    pallas_call x2, Pallas kernels, ffn_forward(): pl.pallas_call(ffn_forward_body, grid=(inner // chunk,), in_specs=[whole(...  34.5 us
    dot_general x6, matrix products, filter_taps(): return jnp.dot(second_sine, weight_three, precision=HIGHEST) * envelope  24.4 us
  transfers between devices with their start and end apart: 6, of which 2 were waited for; matrix products, arithmetic and copies ran while one was open for 8% of the time, Pallas kernels for 19%

profile of v3, /device:TPU:0, one launch (start us, length us, event | category | flops | bytes accessed | tf_op | source)
XLA Modules:
  0.0 674.2 jit_solution(11617310266466349871)
XLA Ops:
  7.3 5.3 all-to-all-start
  18.8 1.2 fusion.45
  20.0 0.7 copy-done.11
  20.7 2.9 multiply_convert_fusion.3
  23.6 4.8 fusion.3.taps_ref.refs_10_
  28.4 1.2 fusion.44
  29.6 0.7 copy-done.13
  30.3 2.9 multiply_convert_fusion.4
  33.2 4.8 fusion.2.taps_ref.refs_10_
  38.0 4.6 all-to-all-start.2
  42.6 2.0 bitcast_convert_fusion.r_ref.refs_1_
  44.6 28.3 %mixer_forward.2 = (f32[1024,768]{1,0:T(8,128)}, bf16[1024,768]{1,0:T(8,128)(2,1)}, bf16[3,1024,768]{2,1,0:T(8,128)(2,1)}, bf16[2048,768]{1,0:T(8,128)(2,1)}, bf16[1024,768]{1,0:T(8,128)(2,1)}) custom-call(f32[1024,768]{1,0:T(8,128)} %bitcast_convert_fusion.r_ref.refs_1_, bf16[2,1,768]{2,1,0:T(2,128)(2,1)} %copy.85.gain_ref.refs_2_, ...), custom_call_target="tpu_custom_call" | custom-call | flops 11274289152 | bytes 31457280 | tf_op jit(solution)/shard_map/mixer_forward/pallas_call | solution.py:640
  72.9 17.3 %ffn_forward.2 = (f32[1024,768]{1,0:T(8,128)}, bf16[1024,768]{1,0:T(8,128)(2,1)}, bf16[1024,3072]{1,0:T(8,128)(2,1)}) custom-call(f32[1024,768]{1,0:T(8,128)} %get-tuple-element.63.hidden_ref.refs_1_, bf16[2,1,768]{2,1,0:T(2,128)(2,1)} %copy.91.gain_ref.refs_2_, bf16[2,1,768]{2,1,0:T(2,128)(2,1)} %copy.92.bias_ref, bf16[2,768,3072]{2,1,0:T(8,128)(2,1)} %refs_5_.5, ...), custom_call_target="tpu_custom_call" | custom-call | flops 9663676416 | bytes 27262976 | tf_op jit(solution)/shard_map/ffn_forward/pallas_call | solution.py:687
  90.2 28.6 %mixer_forward.3 = (f32[1024,768]{1,0:T(8,128)}, bf16[1024,768]{1,0:T(8,128)(2,1)}, bf16[3,1024,768]{2,1,0:T(8,128)(2,1)}, bf16[2048,768]{1,0:T(8,128)(2,1)}, bf16[1024,768]{1,0:T(8,128)(2,1)}) custom-call(f32[1024,768]{1,0:T(8,128)} %get-tuple-element.64.r_ref.refs_1_, bf16[2,1,768]{2,1,0:T(2,128)(2,1)} %copy.85.gain_ref.refs_2_, ...), custom_call_target="tpu_custom_call" | custom-call | flops 11274289152 | bytes 31457280 | tf_op jit(solution)/shard_map/mixer_forward/pallas_call | solution.py:640
  118.8 17.3 %ffn_forward.3 = (f32[1024,768]{1,0:T(8,128)}, bf16[1024,768]{1,0:T(8,128)(2,1)}, bf16[1024,3072]{1,0:T(8,128)(2,1)}) custom-call(f32[1024,768]{1,0:T(8,128)} %get-tuple-element.65.hidden_ref.refs_1_, bf16[2,1,768]{2,1,0:T(2,128)(2,1)} %copy.91.gain_ref.refs_2_, bf16[2,1,768]{2,1,0:T(2,128)(2,1)} %copy.92.bias_ref, bf16[2,768,3072]{2,1,0:T(8,128)(2,1)} %refs_5_.5, ...), custom_call_target="tpu_custom_call" | custom-call | flops 9663676416 | bytes 27262976 | tf_op jit(solution)/shard_map/ffn_forward/pallas_call | solution.py:687
  136.1 1.9 convert_multiply_fusion
  138.0 45.3 %ffn_backward.2 = (f32[1024,768]{1,0:T(8,128)}, f32[1,768]{1,0:T(1,128)}, f32[1,768]{1,0:T(1,128)}, bf16[4,384,1536]{2,1,0:T(8,128)(2,1)}, bf16[2,384,768]{2,1,0:T(8,128)(2,1)}) custom-call(f32[1024,768]{1,0:T(8,128)} %bitcast.124, f32[1024,768]{1,0:T(8,128)} %get-tuple-element.65.hidden_ref.refs_1_, bf16[2,1,768]{2,1,0:T(2,128)(2,1)} %copy.91.gain_ref.refs_2_, ...), custom_call_target="tpu_custom_call" | custom-call | flops 19327352832 | bytes 41943040 | tf_op jit(solution)/shard_map/ffn_backward/pallas_call | solution.py:861
  183.3 52.4 %mixer_backward.2 = (f32[1024,768]{1,0:T(8,128)}, bf16[4,384,768]{2,1,0:T(8,128)(2,1)}, bf16[2,4,96,768]{3,2,1,0:T(8,128)(2,1)}, f32[1024,768]{1,0:T(8,128)}, f3...) custom-call(f32[1024,768]{1,0:T(8,128)} %get-tuple-element.69.refs_0_, ...), custom_call_target="tpu_custom_call" | custom-call | flops 19327352832 | bytes 52428800 | tf_op jit(solution)/shard_map/mixer_backward/pallas_call | solution.py:1079
  235.7 47.6 %ffn_backward.3 = (f32[1024,768]{1,0:T(8,128)}, f32[1,768]{1,0:T(1,128)}, f32[1,768]{1,0:T(1,128)}, bf16[4,384,1536]{2,1,0:T(8,128)(2,1)}, bf16[2,384,768]{2,1,0...) custom-call(f32[1024,768]{1,0:T(8,128)} %get-tuple-element.76.refs_0_, ...), custom_call_target="tpu_custom_call" | custom-call | flops 19327352832 | bytes 41943040 | tf_op jit(solution)/shard_map/ffn_backward/pallas_call | solution.py:861
  283.3 63.4 %mixer_backward.3 = (f32[1024,768]{1,0:T(8,128)}, bf16[4,384,768]{2,1,0:T(8,128)(2,1)}, bf16[2,4,96,768]{3,2,1,0:T(8,128)(2,1)}, f32[1024,768]{1,0:T(8,128)}, f3...) custom-call(f32[1024,768]{1,0:T(8,128)} %get-tuple-element.81.refs_0_, ...), custom_call_target="tpu_custom_call" | custom-call | flops 19327352832 | bytes 52428800 | tf_op jit(solution)/shard_map/mixer_backward/pallas_call | solution.py:1079
  346.8 5.4 multiply_reduce_fusion.3
  352.2 1.9 convolution_bitcast_fusion.1
  354.1 2.5 multiply_reduce_fusion.2
  356.5 3.6 multiply_reduce_fusion.1
  360.1 1.9 convolution_bitcast_fusion
  362.0 2.5 multiply_reduce_fusion
  364.5 1.4 multiply_convert_fusion.2
  365.9 4.3 all-to-all-start.1
  370.5 3.4 convert_element_type.119
  375.4 0.7 pad_maximum_fusion.8
  376.7 0.6 pad_maximum_fusion.9
  379.4 4.1 fusion.33
  383.5 5.6 fusion.30
  389.1 0.8 pad_maximum_fusion.3
  389.9 39.5 %last_sums.1 = (f32[2,96,768]{2,1,0:T(8,128)S(1)}, f32[2,96,384]{2,1,0:T(8,128)S(1)}) custom-call(bf16[2,4,96,768]{3,2,1,0:T(8,128)(2,1)S(1)} %copy-done.3, bf16[4,384,768]{2,1,0:T(8,128)(2,1)S(1)} %copy-done.2), custom_call_target="tpu_custom_call" | custom-call | tf_op jit(solution)/shard_map/last_sums/pallas_call | solution.py:1195
  429.4 0.8 copy-done.4
  430.4 3.7 all-to-all-start.3
  434.1 0.8 pad_maximum_fusion.2
  435.0 0.9 pad_maximum_fusion.1
  436.0 0.7 pad_maximum_fusion.6
  436.7 0.9 pad_maximum_fusion
  437.6 88.5 %all-reduce.10.cloned.1.call-done = (f32[2,768]{1,0:T(2,128)}, f32[2,768]{1,0:T(2,128)}, f32[2,3,2304]{2,1,0:T(4,128)}, f32[2,33,64]{2,1,0:T(8,128)}, f32[2,2,64...) async-done(((f32[2,768]{1,0:T(2,128)}, f32[2,768]{1,0:T(2,128)}, f32[2,3,2304]{2,1,0:T(4,128)}, ...) | async-done | bytes 136720 | tf_op jit(solution)/shard_map/psum | solution.py:1294
  526.1 1.4 copy.116
  527.5 1.5 copy.115
  529.0 3.3 convert.4
  532.4 1.9 convert.5
  534.3 126.8 %all-reduce.8.cloned.1.call-done = f32[2,64,768]{2,1,0:T(8,128)} async-done(((f32[2,64,768]{2,1,0:T(8,128)}), f32[2,64,768]{2,1,0:T(8,128)}) %all-reduce.8.cloned.1.call-update) | async-done | bytes 393232 | tf_op jit(solution)/shard_map/psum | solution.py:1294
  663.6 1.8 copy.139
  (176 shorter events, 14.2 us)
Async XLA Ops:
  7.2 7.4 %copy-start.52 = (bf16[2,768]{1,0:T(2,128)(2,1)S(1)}, bf16[2,768]{1,0:T(2,128)(2,1)}, u32[]{:S(2)}) copy-start(bf16[2,768]{1,0:T(2,128)(2,1)} %param.29) | copy-start | bytes 9220
  7.2 8.0 %copy-start.53 = (bf16[2,768]{1,0:T(2,128)(2,1)S(1)}, bf16[2,768]{1,0:T(2,128)(2,1)}, u32[]{:S(2)}) copy-start(bf16[2,768]{1,0:T(2,128)(2,1)} %param.31) | copy-start | bytes 9220
  7.2 8.6 %copy-start.54 = (bf16[2,768]{1,0:T(2,128)(2,1)S(1)}, bf16[2,768]{1,0:T(2,128)(2,1)}, u32[]{:S(2)}) copy-start(bf16[2,768]{1,0:T(2,128)(2,1)} %param.22) | copy-start | bytes 9220
  7.3 9.2 %copy-start.55 = (bf16[2,768]{1,0:T(2,128)(2,1)S(1)}, bf16[2,768]{1,0:T(2,128)(2,1)}, u32[]{:S(2)}) copy-start(bf16[2,768]{1,0:T(2,128)(2,1)} %param.32) | copy-start | bytes 9220
  7.3 9.8 %copy-start.26 = (bf16[2,33,64]{2,0,1:T(2,128)(2,1)S(1)}, bf16[2,33,64]{2,0,1:T(2,128)(2,1)}, u32[]{:S(2)}) copy-start(bf16[2,33,64]{2,0,1:T(2,128)(2,1)} %param.25) | copy-start | bytes 25348
  7.3 9.8 %copy-start.30 = (bf16[2,3,2304]{2,0,1:T(2,128)(2,1)S(1)}, bf16[2,3,2304]{2,0,1:T(2,128)(2,1)}, u32[]{:S(2)}) copy-start(bf16[2,3,2304]{2,0,1:T(2,128)(2,1)} %param.24) | copy-start | bytes 82948
  7.3 11.5 %copy-start.22 = (bf16[2,64,64]{2,1,0:T(8,128)(2,1)S(1)}, bf16[2,64,64]{2,1,0:T(8,128)(2,1)}, u32[]{:S(2)}) copy-start(bf16[2,64,64]{2,1,0:T(8,128)(2,1)} %param.27) | copy-start | bytes 49156
  7.3 13.4 %copy-start.20 = (bf16[2,64,768]{2,1,0:T(8,128)(2,1)S(1)}, bf16[2,64,768]{2,1,0:T(8,128)(2,1)}, u32[]{:S(2)}) copy-start(bf16[2,64,768]{2,1,0:T(8,128)(2,1)} %param.28) | copy-start | bytes 589828
  7.3 30.7 %all-to-all-start = ((bf16[4,256,768]{2,1,0:T(8,128)(2,1)}), bf16[4,256,768]{2,1,0:T(8,128)(2,1)S(1)}, u32[]{:S(2)}, u32[]{:S(2)}) async-start(bf16[4,256,768]{2,1,0:T(8,128)(2,1)} %bitcast.125), calls=%async_computation | async-start | bytes 3145728 | tf_op jit(solution)/shard_map/all_to_all | solution.py:1226
  13.9 9.6 %copy-start.64 = (bf16[2048,1024]{1,0:T(8,128)(2,1)S(1)}, bf16[2048,1024]{1,0:T(8,128)(2,1)}, u32[]{:S(2)}) copy-start(bf16[2048,1024]{1,0:T(8,128)(2,1)} %constant.63.clone.table_ref.refs_12_) | copy-start | bytes 12582916
  14.0 14.4 %copy-start.34 = (f32[64]{0:T(128)}, f32[64]{0:T(128)S(1)}, u32[]{:S(2)}) copy-start(f32[64]{0:T(128)S(1)} %get-tuple-element.179) | copy-start | bytes 772
  14.0 14.4 %copy-start.31 = (f32[64]{0:T(128)}, f32[64]{0:T(128)S(1)}, u32[]{:S(2)}) copy-start(f32[64]{0:T(128)S(1)} %get-tuple-element.184) | copy-start | bytes 772
  14.0 15.6 %copy-start.36 = (f32[64]{0:T(128)}, f32[64]{0:T(128)S(1)}, u32[]{:S(2)}) copy-start(f32[64]{0:T(128)S(1)} %get-tuple-element.183) | copy-start | bytes 772
  18.7 9.7 %copy-start.8 = (f32[1024,64]{0,1:T(8,128)}, f32[1024,64]{0,1:T(8,128)S(1)}, u32[]{:S(2)}) copy-start(f32[1024,64]{0,1:T(8,128)S(1)} %fusion.70) | copy-start | bytes 786436
  38.0 98.1 %all-to-all-start.2 = ((bf16[4,256,768]{2,1,0:T(8,128)(2,1)}), bf16[4,256,768]{2,1,0:T(8,128)(2,1)S(1)}, u32[]{:S(2)}, u32[]{:S(2)}) async-start(bf16[4,256,768]{2,1,0:T(8,128)(2,1)} %bitcast.126), calls=%async_computation.2 | async-start | bytes 3145728 | tf_op jit(solution)/shard_map/all_to_all | solution.py:1226
  283.2 63.5 %copy-start.14 = (f32[1024,64]{0,1:T(8,128)S(1)}, f32[1024,64]{0,1:T(8,128)}, u32[]{:S(2)}) copy-start(f32[1024,64]{0,1:T(8,128)} %copy-done.13) | copy-start | bytes 786436
  283.3 63.5 %copy-start.21 = (bf16[2,64,768]{2,1,0:T(8,128)(2,1)S(1)}, bf16[2,64,768]{2,1,0:T(8,128)(2,1)}, u32[]{:S(2)}) copy-start(bf16[2,64,768]{2,1,0:T(8,128)(2,1)} %param.28) | copy-start | bytes 589828
  283.3 63.5 %copy-start.37 = (f32[64]{0:T(128)S(1)}, f32[64]{0:T(128)}, u32[]{:S(2)}) copy-start(f32[64]{0:T(128)} %copy-done.36) | copy-start | bytes 772
  346.7 7.4 %copy-start.23 = (bf16[2,64,64]{2,1,0:T(8,128)(2,1)S(1)}, bf16[2,64,64]{2,1,0:T(8,128)(2,1)}, u32[]{:S(2)}) copy-start(bf16[2,64,64]{2,1,0:T(8,128)(2,1)} %param.27) | copy-start | bytes 49156
  346.7 9.8 %copy-start.6 = (f32[1024,768]{1,0:T(8,128)S(1)}, f32[1024,768]{1,0:T(8,128)}, u32[]{:S(2)}) copy-start(f32[1024,768]{1,0:T(8,128)} %get-tuple-element.101) | copy-start | bytes 9437188
  346.7 9.8 %copy-start.12 = (f32[1024,64]{0,1:T(8,128)S(1)}, f32[1024,64]{0,1:T(8,128)}, u32[]{:S(2)}) copy-start(f32[1024,64]{0,1:T(8,128)} %copy-done.11) | copy-start | bytes 786436
  346.7 9.8 %copy-start.35 = (f32[64]{0:T(128)S(1)}, f32[64]{0:T(128)}, u32[]{:S(2)}) copy-start(f32[64]{0:T(128)} %copy-done.34) | copy-start | bytes 772
  352.1 12.3 %copy-start.10 = (f32[1024,768]{1,0:T(8,128)S(1)}, f32[1024,768]{1,0:T(8,128)}, u32[]{:S(2)}) copy-start(f32[1024,768]{1,0:T(8,128)} %get-tuple-element.66) | copy-start | bytes 9437188
  365.9 64.5 %all-to-all-start.1 = ((bf16[4,256,768]{2,1,0:T(8,128)(2,1)}), bf16[4,256,768]{2,1,0:T(8,128)(2,1)}, u32[]{:S(2)}, u32[]{:S(2)}) async-start(bf16[4,256,768]{2,1,0:T(8,128)(2,1)} %bitcast.20), calls=%async_computation.1 | async-start | bytes 3145728 | tf_op jit(solution)/shard_map/all_to_all | solution.py:1230
  370.2 9.2 %copy-start.7 = (f32[1024,768]{1,0:T(8,128)S(1)}, f32[1024,768]{1,0:T(8,128)}, u32[]{:S(2)}) copy-start(f32[1024,768]{1,0:T(8,128)} %get-tuple-element.100) | copy-start | bytes 9437188
  370.2 9.2 %copy-start.15 = (f32[1024,64]{0,1:T(8,128)S(1)}, f32[1024,64]{0,1:T(8,128)}, u32[]{:S(2)}) copy-start(f32[1024,64]{0,1:T(8,128)} %copy-done.13) | copy-start | bytes 786436
  370.2 155.8 %all-reduce.10.cloned.1.call-start = ((), (), s32[]{:S(2)}) async-start(), calls=%async_computation.5 | async-start | bytes 425984 | tf_op jit(solution)/shard_map/psum | solution.py:1294
  370.4 6.9 %copy-start.58 = (f32[64]{0:T(128)S(1)}, f32[64]{0:T(128)}, u32[]{:S(2)}) copy-start(f32[64]{0:T(128)} %get-tuple-element.191) | copy-start | bytes 772
  370.4 6.9 %copy-start.59 = (f32[64]{0:T(128)S(1)}, f32[64]{0:T(128)}, u32[]{:S(2)}) copy-start(f32[64]{0:T(128)} %get-tuple-element.187) | copy-start | bytes 772
  370.4 7.5 %copy-start.45 = (f32[1,768]{1,0:T(1,128)S(1)}, f32[1,768]{1,0:T(1,128)}, u32[]{:S(2)}) copy-start(f32[1,768]{1,0:T(1,128)} %get-tuple-element.91) | copy-start | bytes 9220
  370.4 7.5 %copy-start.46 = (f32[1,768]{1,0:T(1,128)S(1)}, f32[1,768]{1,0:T(1,128)}, u32[]{:S(2)}) copy-start(f32[1,768]{1,0:T(1,128)} %get-tuple-element.93) | copy-start | bytes 9220
  370.4 7.5 %copy-start.49 = (f32[1,768]{1,0:T(1,128)S(1)}, f32[1,768]{1,0:T(1,128)}, u32[]{:S(2)}) copy-start(f32[1,768]{1,0:T(1,128)} %get-tuple-element.90) | copy-start | bytes 9220
  370.5 7.5 %copy-start.50 = (f32[1,768]{1,0:T(1,128)S(1)}, f32[1,768]{1,0:T(1,128)}, u32[]{:S(2)}) copy-start(f32[1,768]{1,0:T(1,128)} %get-tuple-element.92) | copy-start | bytes 9220
  370.5 8.1 %copy-start.43 = (f32[1,768]{1,0:T(1,128)S(1)}, f32[1,768]{1,0:T(1,128)}, u32[]{:S(2)}) copy-start(f32[1,768]{1,0:T(1,128)} %get-tuple-element.105) | copy-start | bytes 9220
  370.5 8.1 %copy-start.44 = (f32[1,768]{1,0:T(1,128)S(1)}, f32[1,768]{1,0:T(1,128)}, u32[]{:S(2)}) copy-start(f32[1,768]{1,0:T(1,128)} %get-tuple-element.107) | copy-start | bytes 9220
  370.5 8.1 %copy-start.47 = (f32[1,768]{1,0:T(1,128)S(1)}, f32[1,768]{1,0:T(1,128)}, u32[]{:S(2)}) copy-start(f32[1,768]{1,0:T(1,128)} %get-tuple-element.104) | copy-start | bytes 9220
  370.5 8.1 %copy-start.48 = (f32[1,768]{1,0:T(1,128)S(1)}, f32[1,768]{1,0:T(1,128)}, u32[]{:S(2)}) copy-start(f32[1,768]{1,0:T(1,128)} %get-tuple-element.106) | copy-start | bytes 9220
  379.2 282.0 %all-reduce.8.cloned.1.call-start = ((), (), s32[]{:S(2)}) async-start(), calls=%async_computation.4 | async-start | bytes 786432 | tf_op jit(solution)/shard_map/psum | solution.py:1294
  389.9 40.4 %copy-start.19 = (f32[2,96,384]{2,1,0:T(8,128)S(1)}, f32[2,96,384]{2,1,0:T(8,128)}, u32[]{:S(2)}) copy-start(f32[2,96,384]{2,1,0:T(8,128)} %get-tuple-element.97) | copy-start | bytes 884740
  430.4 102.0 %all-to-all-start.3 = ((bf16[4,256,768]{2,1,0:T(8,128)(2,1)}), bf16[4,256,768]{2,1,0:T(8,128)(2,1)S(1)}, u32[]{:S(2)}, u32[]{:S(2)}) async-start(bf16[4,256,768]{2,1,0:T(8,128)(2,1)} %bitcast.122), calls=%async_computation.3 | async-start | bytes 3145728 | tf_op jit(solution)/shard_map/all_to_all | solution.py:1230
  529.0 138.1 %copy-start.1 = (s32[2,1]{0,1:T(1,128)S(1)}, s32[2,1]{0,1:T(1,128)}, u32[]{:S(2)}) copy-start(s32[2,1]{0,1:T(1,128)} %param.20) | copy-start | bytes 28
  532.4 128.8 %copy-start.42 = (f32[2,768]{1,0:T(2,128)S(1)}, f32[2,768]{1,0:T(2,128)}, u32[]{:S(2)}) copy-start(f32[2,768]{1,0:T(2,128)} %get-tuple-element.205) | copy-start | bytes 18436
  532.4 129.4 %copy-start.41 = (f32[2,768]{1,0:T(2,128)S(1)}, f32[2,768]{1,0:T(2,128)}, u32[]{:S(2)}) copy-start(f32[2,768]{1,0:T(2,128)} %get-tuple-element.206) | copy-start | bytes 18436
  532.4 130.0 %copy-start.60 = (f32[2,2,64]{2,1,0:T(2,128)S(1)}, f32[2,2,64]{2,1,0:T(2,128)}, u32[]{:S(2)}) copy-start(f32[2,2,64]{2,1,0:T(2,128)} %get-tuple-element.210) | copy-start | bytes 3076
  532.4 130.6 %copy-start.27 = (f32[2,64,64]{2,1,0:T(8,128)S(1)}, f32[2,64,64]{2,1,0:T(8,128)}, u32[]{:S(2)}) copy-start(f32[2,64,64]{2,1,0:T(8,128)} %get-tuple-element.211) | copy-start | bytes 98308
  532.4 133.0 %copy-start.40 = (f32[2,768]{1,0:T(2,128)S(1)}, f32[2,768]{1,0:T(2,128)}, u32[]{:S(2)}) copy-start(f32[2,768]{1,0:T(2,128)} %get-tuple-element.213) | copy-start | bytes 18436
  532.4 133.6 %copy-start.39 = (f32[2,768]{1,0:T(2,128)S(1)}, f32[2,768]{1,0:T(2,128)}, u32[]{:S(2)}) copy-start(f32[2,768]{1,0:T(2,128)} %get-tuple-element.215) | copy-start | bytes 18436
  532.4 134.2 %copy-start.38 = (f32[2,768]{1,0:T(2,128)S(1)}, f32[2,768]{1,0:T(2,128)}, u32[]{:S(2)}) copy-start(f32[2,768]{1,0:T(2,128)} %get-tuple-element.216) | copy-start | bytes 18436
  (23 other events, 111.1 us)
Sparse Core Ops, SparseCore 0:
  379.3 146.6 all-reduce.9
  532.8 128.3 all-reduce.7
